TPU v7x, 256 devices: a whole 4x4x8 slice. The times are simulated.
256 devices in a mesh: dp: 4 (over x), tm: 64 (over y, z, core).
Axes of the slice: x: 4, y: 4, z: 8, core: 2. Of those that a mesh axis runs over, the one named last changes fastest.
Arguments:
- frames: bfloat16 [4, 8192, 1536], P('dp', 'tm'), may hold values from -48 to 48
- taps: float32 [31, 1536], replicated, may hold values from -1 to 1
- batchnorm_gain_scale: float32 [1536], replicated, may hold values from 0.25 to 1.75
- batchnorm_shift_bias: float32 [1536], replicated, may hold values from -3 to 3
- w_router: bfloat16 [1536, 8], replicated, may hold values from -0.3125 to 0.3125
- w_in: bfloat16 [1536, 24576], P(None, 'tm'), may hold values from -0.15625 to 0.15625
- w_out: bfloat16 [24576, 1536], P('tm'), may hold values from -0.109375 to 0.109375
- choices: int32 [4, 8192, 2], P('dp', 'tm'), may hold values from 0 to 7, all different within a row; in each aligned block of 128 rows (0 to 127, 128 to 255, ..., all dimensions but the last counted through in order) at most 32 rows name the same one
- cotangent: bfloat16 [4, 8192, 1536], P('dp', 'tm'), may hold values from -48 to 48
Outputs:
- mixed: bfloat16 [4, 8192, 1536], P('dp', 'tm')
- grad_frames: bfloat16 [4, 8192, 1536], P('dp', 'tm')
- grad_taps: float32 [31, 1536], replicated
- grad_w_in: float32 [1536, 24576], P('dp', 'tm')
- grad_w_out: float32 [24576, 1536], P('tm', 'dp')
Inputs may be any that keep to these rules, and one draw needn't show every extreme that they name: `choices`: within the 128 frames of one device the two experts of a frame differ, and every expert is named exactly 32 times.
All inputs are finite; a program needn't handle non-finite values.
Results may differ from a plain program's by a relative error of at most 0.0063.
Values may be sent and summed in bfloat16 or wider, within the bound.
A program may use at most 192 MiB of HBM per device.

v0:
```python
import jax
import jax.numpy as jnp
from jax import lax
from jax.sharding import PartitionSpec as P

D = 1536
EXPERTS = 8
TOP = 2
TAPS = 31


EPS = 1e-05
CONTRACT_ROWS = (((0,), (0,)), ((), ()))
CONTRACT_COLS = (((1,), (1,)), ((), ()))


def extended(block, sides, width):
    for axis, dim in sides:
        count = lax.axis_size(axis)
        forward = [(i, i + 1) for i in range(count - 1)]
        backward = [(target, source) for source, target in forward]
        low = lax.ppermute(
            lax.slice_in_dim(block, block.shape[dim] - width, None, axis=dim), axis, forward
        )
        high = lax.ppermute(lax.slice_in_dim(block, 0, width, axis=dim), axis, backward)
        block = jnp.concatenate([low, block, high], axis=dim)
    return block


def swish_slope(pre):
    sigma = jax.nn.sigmoid(pre)
    return sigma * (1.0 + pre * (1.0 - sigma))


def conv_lags(rimmed, taps, length, reverse):
    total = jnp.zeros((length, rimmed.shape[1]), jnp.float32)
    last = taps.shape[0] - 1
    for lag in range(taps.shape[0]):
        start = last - lag if reverse else lag
        total = total + taps[lag] * rimmed[start : start + length]
    return total


def to_experts(buffer):
    tm_size = lax.axis_size("tm")
    group = tm_size // EXPERTS
    capacity = buffer.shape[1]
    width = buffer.shape[2]
    copies = jnp.repeat(buffer, group, axis=0)
    received = lax.all_to_all(copies, "tm", split_axis=0, concat_axis=0, tiled=True)
    return received.reshape(tm_size * capacity, width)


def return_sums(partial_value, capacity):
    tm_size = lax.axis_size("tm")
    group = tm_size // EXPERTS
    width = partial_value.shape[1]
    returned = lax.all_to_all(
        partial_value.reshape(tm_size, capacity, width),
        "tm",
        split_axis=0,
        concat_axis=0,
        tiled=True,
    )
    return jnp.sum(returned.reshape(EXPERTS, group, capacity, width).astype(jnp.float32), axis=1)


def body(
    frames,
    taps,
    batchnorm_gain_scale,
    batchnorm_shift_bias,
    w_router,
    w_in,
    w_out,
    choices,
    cotangent,
):
    length = frames.shape[1]
    half = TAPS // 2
    element_count = lax.axis_size("dp") * lax.axis_size("tm") * length
    capacity = length * TOP // EXPERTS
    signal = frames[0].astype(jnp.float32)
    rimmed = extended(frames, (("tm", 1),), half)[0].astype(jnp.float32)
    conv = conv_lags(rimmed, taps, length, False)
    mean = lax.psum(jnp.sum(conv, axis=0), ("dp", "tm")) / element_count
    centered_values = conv - mean
    variance = (
        lax.psum(jnp.sum(centered_values * centered_values, axis=0), ("dp", "tm")) / element_count
    )
    inverse_deviation = lax.rsqrt(variance + EPS)
    normalized_input = centered_values * inverse_deviation
    before_activation = normalized_input * batchnorm_gain_scale + batchnorm_shift_bias
    resid = signal + jax.nn.silu(before_activation)
    lcent = resid - jnp.mean(resid, axis=-1, keepdims=True)
    lrstd = lax.rsqrt(jnp.mean(lcent * lcent, axis=-1, keepdims=True) + EPS)
    vhat = lcent * lrstd
    normed = vhat.astype(jnp.bfloat16)
    logits = jnp.dot(normed, w_router, preferred_element_type=jnp.float32)
    ids = choices[0]
    onehot = (ids[:, :, None] == jnp.arange(EXPERTS, dtype=jnp.int32)[None, None, :]).astype(
        jnp.float32
    )
    picked = jnp.sum(onehot * logits[:, None, :], axis=-1)
    first = jax.nn.sigmoid(picked[:, 0] - picked[:, 1])
    gates = jnp.stack([first, 1.0 - first], axis=1)
    flat_ids = ids.reshape(-1)
    expert_hot = (flat_ids[:, None] == jnp.arange(EXPERTS, dtype=jnp.int32)[None, :]).astype(
        jnp.int32
    )
    slots = jnp.sum((jnp.cumsum(expert_hot, axis=0) - 1) * expert_hot, axis=1)
    frame_index = jnp.arange(length * TOP, dtype=jnp.int32) // TOP
    buffer = (
        jnp.zeros((EXPERTS, capacity, D), jnp.bfloat16).at[flat_ids, slots].set(normed[frame_index])
    )
    rows = to_experts(buffer)
    pre = jnp.dot(rows, w_in, preferred_element_type=jnp.float32)
    hidden = jax.nn.silu(pre).astype(jnp.bfloat16)
    partial_value = jnp.dot(hidden, w_out, preferred_element_type=jnp.float32).astype(jnp.bfloat16)
    combined = return_sums(partial_value, capacity)
    expert_out = combined[flat_ids, slots].reshape(length, TOP, D)
    mixed = (resid + jnp.sum(gates[:, :, None] * expert_out, axis=1)).astype(jnp.bfloat16)
    upstream = cotangent[0].astype(jnp.float32)
    dgate = jnp.sum(upstream[:, None, :] * expert_out, axis=-1)
    dpick = (dgate[:, 0] - dgate[:, 1]) * first * (1.0 - first)
    dlogits = (onehot[:, 0] - onehot[:, 1]) * dpick[:, None]
    dnormed = jnp.dot(dlogits, w_router.astype(jnp.float32).T, precision=lax.Precision.HIGHEST)
    sent = (gates[:, :, None] * upstream[:, None, :]).astype(jnp.bfloat16).reshape(length * TOP, D)
    sent_buffer = jnp.zeros((EXPERTS, capacity, D), jnp.bfloat16).at[flat_ids, slots].set(sent)
    upstream_rows = to_experts(sent_buffer)
    dhidden = lax.dot_general(
        upstream_rows, w_out, CONTRACT_COLS, preferred_element_type=jnp.float32
    )
    dpre = (dhidden * swish_slope(pre)).astype(jnp.bfloat16)
    grad_in_local = lax.dot_general(rows, dpre, CONTRACT_ROWS, preferred_element_type=jnp.float32)
    grad_out_local = lax.dot_general(
        hidden, upstream_rows, CONTRACT_ROWS, preferred_element_type=jnp.float32
    )
    back_rows = lax.dot_general(
        dpre, w_in, CONTRACT_COLS, preferred_element_type=jnp.float32
    ).astype(jnp.bfloat16)
    back = return_sums(back_rows, capacity)
    dnormed = dnormed + jnp.sum(back[flat_ids, slots].reshape(length, TOP, D), axis=1)
    dmean = jnp.mean(dnormed, axis=-1, keepdims=True)
    dproj = jnp.mean(dnormed * vhat, axis=-1, keepdims=True)
    dresid = upstream + lrstd * (dnormed - dmean - vhat * dproj)
    normalized_gradient = dresid * swish_slope(before_activation) * batchnorm_gain_scale
    first_moment_sum, second_moment_sum = lax.psum(
        (
            jnp.sum(normalized_gradient, axis=0),
            jnp.sum(normalized_gradient * normalized_input, axis=0),
        ),
        ("dp", "tm"),
    )
    convolution_gradient = (
        inverse_deviation
        * (
            normalized_gradient
            - first_moment_sum / element_count
            - normalized_input * second_moment_sum / element_count
        )
    ).astype(jnp.bfloat16)
    grad_rimmed = extended(convolution_gradient[None], (("tm", 1),), half)[0].astype(jnp.float32)
    grad_frames = (dresid + conv_lags(grad_rimmed, taps, length, True)).astype(jnp.bfloat16)
    dconv_f = convolution_gradient.astype(jnp.float32)
    local_taps = jnp.stack(
        [jnp.sum(dconv_f * rimmed[lag : lag + length], axis=0) for lag in range(TAPS)]
    )
    grad_taps = lax.psum(local_taps, ("dp", "tm"))
    grad_w_in, grad_w_out = (
        lax.psum_scatter(grad_in_local, "dp", scatter_dimension=0, tiled=True),
        lax.psum_scatter(grad_out_local, "dp", scatter_dimension=1, tiled=True),
    )
    return (mixed[None], grad_frames[None], grad_taps, grad_w_in, grad_w_out)


def solution(mesh):
    return jax.shard_map(
        body,
        mesh=mesh,
        in_specs=(
            P("dp", "tm", None),
            P(),
            P(),
            P(),
            P(),
            P(None, "tm"),
            P("tm", None),
            P("dp", "tm", None),
            P("dp", "tm", None),
        ),
        out_specs=(P("dp", "tm", None), P("dp", "tm", None), P(), P("dp", "tm"), P("tm", "dp")),
        check_vma=False,
    )
```

profile of v0, /device:TPU:1, one launch (start us, length us, event | category | flops | bytes accessed | tf_op | source)
XLA Modules:
  0.0 1171.1 jit_solution(16331875610728970326)
XLA Ops:
  9.0 4.9 collective-permute-start
  26.0 79.8 %psum.35 = f32[1536]{0:T(1024)S(1)} all-reduce(f32[1536]{0:T(1024)S(1)} %get-tuple-element.83), channel_id=1, replica_groups=mesh['dp'=4,'tm'=64] {'dp','tm'}, use_global_device_ids=true, to_apply=%region_1.0 | all-reduce | flops 1536 | bytes 12288 | tf_op jit(solution)/shard_map/psum | solution.py:86
  105.9 73.0 %psum.36 = f32[1536]{0:T(1024)S(1)} all-reduce(f32[1536]{0:T(1024)S(1)} %multiply_reduce_fusion.5), channel_id=1, replica_groups=mesh['dp'=4,'tm'=64] {'dp','tm'}, use_global_device_ids=true, to_apply=%region_3.0 | all-reduce | flops 1536 | bytes 12288 | tf_op jit(solution)/shard_map/psum | solution.py:89
  183.2 29.3 %scatter_fusion = bf16[8,32,1536]{2,1,0:T(8,128)(2,1)S(1)} fusion(bf16[8,32,1536]{2,1,0:T(8,128)(2,1)S(1)} %broadcast.196.clone, s32[256]{0:T(256)S(1)} %bitcast.595, bf16[256,1536]{1,0:T(8,128)(2,1)} %gather_fusion), kind=kCustom, calls=%fused_computation.3 | custom fusion | bytes 2361344 | tf_op jit(solution)/shard_map/scatter | solution.py:114
  216.0 8.6 all-to-all-start
  234.0 29.3 %scatter_fusion.1 = bf16[8,32,1536]{2,1,0:T(8,128)(2,1)S(1)} fusion(bf16[8,32,1536]{2,1,0:T(8,128)(2,1)S(1)} %broadcast.196.clone.1, s32[256]{0:T(256)S(1)} %bitcast.596, bf16[256,1536]{1,0:T(8,128)(2,1)} %multiply_convert_fusion.2), kind=kCustom, calls=%fused_computation.4 | custom fusion | bytes 2361344 | tf_op jit(solution)/shard_map/scatter | solution.py:129
  263.3 101.9 %all-to-all-done = bf16[64,32,1536]{2,1,0:T(8,128)(2,1)} async-done(((bf16[64,32,1536]{2,1,0:T(8,128)(2,1)}), bf16[64,32,1536]{2,1,0:T(8,128)(2,1)}, u32[]{:S(2)}, u32[]{:S(2)}) %all-to-all-start) | async-done | bytes 6291488 | tf_op jit(solution)/shard_map/all_to_all | solution.py:50
  368.7 5.9 all-to-all-start.2
  374.6 5.8 fusion.116
  382.1 5.3 convolution_convert_fusion.1
  387.3 128.1 %all-to-all-done.2 = bf16[64,32,1536]{2,1,0:T(8,128)(2,1)} async-done(((bf16[64,32,1536]{2,1,0:T(8,128)(2,1)}), bf16[64,32,1536]{2,1,0:T(8,128)(2,1)}, u32[]{:S(2)}, u32[]{:S(2)}) %all-to-all-start.2) | async-done | bytes 6291488 | tf_op jit(solution)/shard_map/all_to_all | solution.py:50
  515.5 6.3 all-to-all-start.1
  521.8 7.8 multiply_convert_fusion
  530.9 5.5 convolution_convert_fusion
  536.4 126.1 %all-to-all-done.1 = bf16[64,32,1536]{2,1,0:T(8,128)(2,1)} async-done(((bf16[64,32,1536]{2,1,0:T(8,128)(2,1)}), bf16[64,32,1536]{2,1,0:T(8,128)(2,1)}, u32[]{:S(2)}, u32[]{:S(2)}) %all-to-all-start.1) | async-done | bytes 6291488 | tf_op jit(solution)/shard_map/all_to_all | solution.py:58
  662.5 6.0 all-to-all-start.3
  668.5 8.1 fusion.117
  676.6 7.8 fusion.106
  685.0 5.6 convert_reduce_fusion.1
  703.5 105.8 %all-to-all-done.3 = bf16[64,32,1536]{2,1,0:T(8,128)(2,1)} async-done(((bf16[64,32,1536]{2,1,0:T(8,128)(2,1)}), bf16[64,32,1536]{2,1,0:T(8,128)(2,1)}, u32[]{:S(2)}, u32[]{:S(2)}) %all-to-all-start.3) | async-done | bytes 6291488 | tf_op jit(solution)/shard_map/all_to_all | solution.py:58
  809.3 5.2 convert_reduce_fusion
  832.5 74.2 %all-reduce = (f32[1536]{0:T(1024)S(1)}, f32[1536]{0:T(1024)S(1)}) all-reduce(f32[1536]{0:T(1024)S(1)} %get-tuple-element.39, f32[1536]{0:T(1024)S(1)} %get-tuple-element.38), channel_id=1, replica_groups=mesh['dp'=4,'tm'=64] {'dp','tm'}, use_global_device_ids=true, to_apply=%region_22.23 | all-reduce | flops 3072 | bytes 24576 | tf_op jit(solution)/shard_map/psum | solution.py:148
  921.1 5.2 fusion.96
  926.3 235.6 %all-reduce.3.cloned.1.call-done = f32[31,1536]{1,0:T(8,128)} async-done(((f32[31,1536]{1,0:T(8,128)}), f32[31,1536]{1,0:T(8,128)}) %all-reduce.3.cloned.1.call-update) | async-done | bytes 190480 | tf_op jit(solution)/shard_map/psum | solution.py:169
  (230 shorter events, 83.0 us)
Async XLA Ops:
  8.0 374.1 %copy-start = (bf16[384,1536]{1,0:T(8,128)(2,1)S(1)}, bf16[384,1536]{1,0:T(8,128)(2,1)}, u32[]{:S(2)}) copy-start(bf16[384,1536]{1,0:T(8,128)(2,1)} %param.15) | copy-start | bytes 3538948
  9.0 12.6 %collective-permute-start = (bf16[1,15,1536]{2,1,0:T(8,128)(2,1)S(1)}, bf16[1,15,1536]{2,1,0:T(8,128)(2,1)S(1)}, u32[]{:S(2)}, u32[]{:S(2)}) collective-permute-start(bf16[1,15,1536]{2,1,0:T(8,128)(2,1)S(1)} %get-tuple-element.88), channel_id=1, source_target_pairs={{0,1},{1,2},{2,3},{3,4},{4,5},{5,6},{6,7},{7,8},{8,9},{9,10},{10,1... | collective-permute-start | bytes 138248 | tf_op jit(solution)/shard_map/ppermute | solution.py:22
  13.9 7.7 collective-permute-start.1
  18.6 7.3 copy-start.25
  22.7 156.2 %copy-start.44 = (f32[1536]{0:T(1024)S(1)}, f32[1536]{0:T(1024)}, u32[]{:S(2)}) copy-start(f32[1536]{0:T(1024)} %param.12) | copy-start | bytes 18436
  22.7 156.2 %copy-start.46 = (f32[1536]{0:T(1024)S(1)}, f32[1536]{0:T(1024)}, u32[]{:S(2)}) copy-start(f32[1536]{0:T(1024)} %param.11) | copy-start | bytes 18436
  26.0 152.8 %copy-start.4 = (f32[128,1536]{1,0:T(8,128)}, f32[128,1536]{1,0:T(8,128)S(1)}, u32[]{:S(2)}) copy-start(f32[128,1536]{1,0:T(8,128)S(1)} %get-tuple-element.84) | copy-start | bytes 2359300
  216.0 8.6 copy-start.9
  216.0 149.2 %all-to-all-start = ((bf16[64,32,1536]{2,1,0:T(8,128)(2,1)}), bf16[64,32,1536]{2,1,0:T(8,128)(2,1)}, u32[]{:S(2)}, u32[]{:S(2)}) async-start(bf16[64,32,1536]{2,1,0:T(8,128)(2,1)} %bitcast.597), calls=%async_computation | async-start | bytes 12582912 | tf_op jit(solution)/shard_map/all_to_all | solution.py:50
  368.7 146.8 %all-to-all-start.2 = ((bf16[64,32,1536]{2,1,0:T(8,128)(2,1)}), bf16[64,32,1536]{2,1,0:T(8,128)(2,1)}, u32[]{:S(2)}, u32[]{:S(2)}) async-start(bf16[64,32,1536]{2,1,0:T(8,128)(2,1)} %bitcast.598), calls=%async_computation.2 | async-start | bytes 12582912 | tf_op jit(solution)/shard_map/all_to_all | solution.py:50
  515.5 147.0 %all-to-all-start.1 = ((bf16[64,32,1536]{2,1,0:T(8,128)(2,1)}), bf16[64,32,1536]{2,1,0:T(8,128)(2,1)}, u32[]{:S(2)}, u32[]{:S(2)}) async-start(bf16[64,32,1536]{2,1,0:T(8,128)(2,1)} %bitcast.600), calls=%async_computation.1 | async-start | bytes 12582912 | tf_op jit(solution)/shard_map/all_to_all | solution.py:58
  521.8 9.1 copy-start.58
  662.5 146.8 %all-to-all-start.3 = ((bf16[64,32,1536]{2,1,0:T(8,128)(2,1)}), bf16[64,32,1536]{2,1,0:T(8,128)(2,1)}, u32[]{:S(2)}, u32[]{:S(2)}) async-start(bf16[64,32,1536]{2,1,0:T(8,128)(2,1)} %bitcast.599), calls=%async_computation.3 | async-start | bytes 12582912 | tf_op jit(solution)/shard_map/all_to_all | solution.py:58
  668.4 257.9 %reduce-scatter.3.cloned.1.call-start = ((), (), s32[]{:S(2)}) async-start(), calls=%async_computation.7 | async-start | bytes 2949120 | tf_op jit(solution)/shard_map/reduce_scatter | solution.py:171
  676.6 8.4 copy-start.51
  676.6 249.7 %reduce-scatter.5.cloned.1.call-start = ((), (), s32[]{:S(2)}) async-start(), calls=%async_computation.8 | async-start | bytes 2949120 | tf_op jit(solution)/shard_map/reduce_scatter | solution.py:172
  684.5 477.4 %all-reduce.3.cloned.1.call-start = ((), (), s32[]{:S(2)}) async-start(), calls=%async_computation.6 | async-start | bytes 393216 | tf_op jit(solution)/shard_map/psum | solution.py:169
  819.1 7.4 copy-start.57
  819.1 7.4 copy-start.3
  819.1 7.4 copy-start.49
  819.1 7.4 copy-start.53
  909.9 10.9 collective-permute-start.2
  914.3 6.5 collective-permute-start.3
  921.1 242.4 %copy-start.1 = (bf16[384,1536]{1,0:T(8,128)(2,1)S(1)}, bf16[384,1536]{1,0:T(8,128)(2,1)}, u32[]{:S(2)}) copy-start(bf16[384,1536]{1,0:T(8,128)(2,1)} %param.15) | copy-start | bytes 3538948
  (48 other events, 268.8 us)
Sparse Core Ops, SparseCore 0:
  676.7 33.2 reduce-scatter.2
  713.1 34.1 reduce-scatter.4
Sparse Core Ops, SparseCore 1:
  920.9 241.0 all-reduce.2
where the time goes:
time: 1180 us; the launch traced here: 1170 us
  waiting for transfers between devices  698 us (59%)
  blocking collectives  227 us (19%)
  local copies, waits for them, and re-layouts  104 us (9%)
  matrix products  42.4 us (4%)
  other arithmetic  42.3 us (4%)
  starting transfers between devices  40.5 us (3%)
  between operations  17 us (1%)
    psum x1, waiting for transfers between devices, body(): grad_taps = lax.psum(local_taps, ('dp', 'tm'))  236 us
    all_to_all x2, waiting for transfers between devices, return_sums(): lax.all_to_all(partial_value.reshape(tm_size, capacity, width), 'tm', spl...  232 us
    all_to_all x2, waiting for transfers between devices, to_experts(): lax.all_to_all(copies, 'tm', split_axis=0, concat_axis=0, tiled=True)  230 us
    psum x1, blocking collectives, body(): mean = lax.psum(jnp.sum(conv, axis=0), ('dp', 'tm')) / element_count  79.8 us
    psum x1, blocking collectives, body(): lax.psum((jnp.sum(normalized_gradient, axis=0), jnp.sum(normalized_gradie...  74.2 us
    psum x1, blocking collectives, body(): lax.psum(jnp.sum(centered_values * centered_values, axis=0), ('dp', 'tm'))  73 us
    scatter x2, local copies, waits for them, and re-layouts, body(): jnp.zeros((EXPERTS, capacity, D), jnp.bfloat16).at[flat_ids, slots]  58.7 us
  transfers between devices with their start and end apart: 11, of which 5 were waited for; matrix products, arithmetic and copies ran while one was open for 12% of the time, Pallas kernels for 0%

commit v1 on v0

--- a/solution.py
+++ b/solution.py
@@ -1,17 +1,22 @@
+import functools
+
 import jax
 import jax.numpy as jnp
 from jax import lax
+from jax.experimental import pallas as pl
+from jax.experimental.pallas import tpu as pltpu
 from jax.sharding import PartitionSpec as P
 
 D = 1536
 EXPERTS = 8
 TOP = 2
 TAPS = 31
-
-
 EPS = 1e-05
+NEAR = 16
+MESH = pl.DeviceIdType.MESH
 CONTRACT_ROWS = (((0,), (0,)), ((), ()))
 CONTRACT_COLS = (((1,), (1,)), ((), ()))
+EXACT = lax.Precision.HIGHEST
 
 
 def extended(block, sides, width):
@@ -39,6 +44,159 @@
         start = last - lag if reverse else lag
         total = total + taps[lag] * rimmed[start : start + length]
     return total
+
+
+class Groups:
+    def __init__(self):
+        dp_size, tm_size = lax.axis_size("dp"), lax.axis_size("tm")
+        self.dp, self.tm = lax.axis_index("dp"), lax.axis_index("tm")
+        self.lines = tm_size // NEAR
+        self.near_size, self.far_size = NEAR, dp_size * self.lines
+        self.near_rank = self.tm % NEAR
+        self.far_rank = self.dp * self.lines + self.tm // NEAR
+
+    def near(self, rank):
+        return (self.dp, (self.tm // NEAR) * NEAR + rank)
+
+    def far(self, rank):
+        return (rank // self.lines, (rank % self.lines) * NEAR + self.near_rank)
+
+    def enter(self):
+        barrier = pltpu.get_barrier_semaphore()
+
+        def greet(size, rank, place):
+            def step(k, carry):
+                pl.semaphore_signal(
+                    barrier, inc=1, device_id=place((rank + k) % size), device_id_type=MESH
+                )
+                return carry
+
+            lax.fori_loop(1, size, step, 0)
+
+        greet(self.near_size, self.near_rank, self.near)
+        greet(self.far_size, self.far_rank, self.far)
+        pl.semaphore_wait(barrier, self.near_size + self.far_size - 2)
+
+
+def trade(size, rank, place, source, held, send_sem, recv_sem):
+    def copy(k):
+        peer = (rank + k) % size
+        return pltpu.make_async_remote_copy(
+            src_ref=source(peer),
+            dst_ref=held.at[rank],
+            send_sem=send_sem.at[k],
+            recv_sem=recv_sem.at[rank],
+            device_id=place(peer),
+            device_id_type=MESH,
+        )
+
+    def start(k, carry):
+        copy(k).start()
+        return carry
+
+    def finish(k, carry):
+        origin = (rank + k) % size
+        pltpu.make_async_remote_copy(
+            src_ref=held.at[origin],
+            dst_ref=held.at[origin],
+            send_sem=send_sem.at[k],
+            recv_sem=recv_sem.at[origin],
+            device_id=place(origin),
+            device_id_type=MESH,
+        ).wait_recv()
+        return carry
+
+    def sent(k, carry):
+        copy(k).wait_send()
+        return carry
+
+    lax.fori_loop(1, size, start, 0)
+    lax.fori_loop(1, size, finish, 0)
+    lax.fori_loop(1, size, sent, 0)
+
+
+def moments_merge(held, count):
+    means = held[:, 0, :]
+    mean = jnp.sum(means, axis=0) / means.shape[0]
+    spread = means - mean[None]
+    squares = jnp.sum(held[:, 1, :], axis=0) + count * jnp.sum(spread * spread, axis=0)
+    return mean, squares
+
+
+def sums_kernel(count, x_ref, o_ref, near_held, far_held, near_send, near_recv, far_send, far_recv):
+    groups = Groups()
+    near_held[groups.near_rank] = x_ref[...]
+    groups.enter()
+
+    def merge(held, parts):
+        if count is None:
+            return jnp.sum(held[...], axis=0)
+        return jnp.stack(moments_merge(held[...], float(parts)))
+
+    mine = near_held.at[groups.near_rank]
+    trade(groups.near_size, groups.near_rank, groups.near, lambda p: mine, near_held, near_send, near_recv)
+    far_held[groups.far_rank] = merge(near_held, count)
+    mine = far_held.at[groups.far_rank]
+    trade(groups.far_size, groups.far_rank, groups.far, lambda p: mine, far_held, far_send, far_recv)
+    o_ref[...] = merge(far_held, None if count is None else count * groups.near_size)
+
+
+def all_sums(x, count, collective_id):
+    far_size = lax.axis_size("dp") * (lax.axis_size("tm") // NEAR)
+    return pl.pallas_call(
+        functools.partial(sums_kernel, count),
+        out_shape=jax.ShapeDtypeStruct(x.shape, x.dtype),
+        in_specs=[pl.BlockSpec(memory_space=pltpu.VMEM)],
+        out_specs=pl.BlockSpec(memory_space=pltpu.VMEM),
+        scratch_shapes=[
+            pltpu.VMEM((NEAR,) + x.shape, x.dtype),
+            pltpu.VMEM((far_size,) + x.shape, x.dtype),
+            pltpu.SemaphoreType.DMA((NEAR,)),
+            pltpu.SemaphoreType.DMA((NEAR,)),
+            pltpu.SemaphoreType.DMA((far_size,)),
+            pltpu.SemaphoreType.DMA((far_size,)),
+        ],
+        compiler_params=pltpu.CompilerParams(collective_id=collective_id, has_side_effects=True),
+    )(x)
+
+
+def taps_kernel(
+    x_ref, o_ref, near_held, far_held, near_send, near_recv, far_send, far_recv, out_send, out_recv
+):
+    groups = Groups()
+    rank = groups.near_rank
+    near_held[rank] = x_ref[rank]
+    groups.enter()
+    trade(groups.near_size, rank, groups.near, lambda p: x_ref.at[p], near_held, near_send, near_recv)
+    far_held[groups.far_rank] = jnp.sum(near_held[...], axis=0)
+    mine = far_held.at[groups.far_rank]
+    trade(groups.far_size, groups.far_rank, groups.far, lambda p: mine, far_held, far_send, far_recv)
+    o_ref[rank] = jnp.sum(far_held[...], axis=0)
+    done = o_ref.at[rank]
+    trade(groups.near_size, rank, groups.near, lambda p: done, o_ref, out_send, out_recv)
+
+
+def taps_sum(x, collective_id):
+    far_size = lax.axis_size("dp") * (lax.axis_size("tm") // NEAR)
+    padded = jnp.pad(x, ((0, 2 * NEAR - x.shape[0]), (0, 0))).reshape(NEAR, 2, x.shape[1])
+    total = pl.pallas_call(
+        taps_kernel,
+        out_shape=jax.ShapeDtypeStruct(padded.shape, padded.dtype),
+        in_specs=[pl.BlockSpec(memory_space=pltpu.VMEM)],
+        out_specs=pl.BlockSpec(memory_space=pltpu.VMEM),
+        scratch_shapes=[
+            pltpu.VMEM(padded.shape, padded.dtype),
+            pltpu.VMEM((far_size,) + padded.shape[1:], padded.dtype),
+            pltpu.SemaphoreType.DMA((NEAR,)),
+            pltpu.SemaphoreType.DMA((NEAR,)),
+            pltpu.SemaphoreType.DMA((far_size,)),
+            pltpu.SemaphoreType.DMA((far_size,)),
+            pltpu.SemaphoreType.DMA((NEAR,)),
+            pltpu.SemaphoreType.DMA((NEAR,)),
+        ],
+        compiler_params=pltpu.CompilerParams(collective_id=collective_id, has_side_effects=True),
+    )(padded)
+    return total.reshape(2 * NEAR, x.shape[1])[: x.shape[0]]
 
 
 def to_experts(buffer):
@@ -83,11 +241,13 @@
     signal = frames[0].astype(jnp.float32)
     rimmed = extended(frames, (("tm", 1),), half)[0].astype(jnp.float32)
     conv = conv_lags(rimmed, taps, length, False)
-    mean = lax.psum(jnp.sum(conv, axis=0), ("dp", "tm")) / element_count
+    local_mean = jnp.sum(conv, axis=0) / length
+    local_spread = conv - local_mean
+    moments = all_sums(
+        jnp.stack([local_mean, jnp.sum(local_spread * local_spread, axis=0)]), length, 0
+    )
+    mean, variance = moments[0], moments[1] / element_count
     centered_values = conv - mean
-    variance = (
-        lax.psum(jnp.sum(centered_values * centered_values, axis=0), ("dp", "tm")) / element_count
-    )
     inverse_deviation = lax.rsqrt(variance + EPS)
     normalized_input = centered_values * inverse_deviation
     before_activation = normalized_input * batchnorm_gain_scale + batchnorm_shift_bias
@@ -109,25 +269,32 @@
         jnp.int32
     )
     slots = jnp.sum((jnp.cumsum(expert_hot, axis=0) - 1) * expert_hot, axis=1)
-    frame_index = jnp.arange(length * TOP, dtype=jnp.int32) // TOP
-    buffer = (
-        jnp.zeros((EXPERTS, capacity, D), jnp.bfloat16).at[flat_ids, slots].set(normed[frame_index])
-    )
+    places = (flat_ids * capacity + slots).reshape(length, TOP)
+    place_hot = places[:, :, None] == jnp.arange(EXPERTS * capacity, dtype=jnp.int32)[None, None, :]
+    place_any = jnp.any(place_hot, axis=1).astype(jnp.bfloat16)
+    place_hot = place_hot.astype(jnp.float32)
+    gate_rows = jnp.sum(place_hot * gates[:, :, None], axis=(0, 1))
+
+    def bucketed(rows):
+        return lax.dot_general(place_any, rows, CONTRACT_ROWS, preferred_element_type=jnp.float32)
+
+    buffer = bucketed(normed).astype(jnp.bfloat16).reshape(EXPERTS, capacity, D)
+    sent_buffer = (gate_rows[:, None] * bucketed(cotangent[0])).astype(jnp.bfloat16)
     rows = to_experts(buffer)
+    upstream_rows = to_experts(sent_buffer.reshape(EXPERTS, capacity, D))
     pre = jnp.dot(rows, w_in, preferred_element_type=jnp.float32)
     hidden = jax.nn.silu(pre).astype(jnp.bfloat16)
     partial_value = jnp.dot(hidden, w_out, preferred_element_type=jnp.float32).astype(jnp.bfloat16)
-    combined = return_sums(partial_value, capacity)
-    expert_out = combined[flat_ids, slots].reshape(length, TOP, D)
-    mixed = (resid + jnp.sum(gates[:, :, None] * expert_out, axis=1)).astype(jnp.bfloat16)
+    combined = return_sums(partial_value, capacity).reshape(EXPERTS * capacity, D)
+    expert_out = [
+        jnp.dot(place_hot[:, k], combined, precision=EXACT) for k in range(TOP)
+    ]
+    mixed = (resid + sum(gates[:, k, None] * expert_out[k] for k in range(TOP))).astype(jnp.bfloat16)
     upstream = cotangent[0].astype(jnp.float32)
-    dgate = jnp.sum(upstream[:, None, :] * expert_out, axis=-1)
-    dpick = (dgate[:, 0] - dgate[:, 1]) * first * (1.0 - first)
+    dgate = [jnp.sum(upstream * expert_out[k], axis=-1) for k in range(TOP)]
+    dpick = (dgate[0] - dgate[1]) * first * (1.0 - first)
     dlogits = (onehot[:, 0] - onehot[:, 1]) * dpick[:, None]
-    dnormed = jnp.dot(dlogits, w_router.astype(jnp.float32).T, precision=lax.Precision.HIGHEST)
-    sent = (gates[:, :, None] * upstream[:, None, :]).astype(jnp.bfloat16).reshape(length * TOP, D)
-    sent_buffer = jnp.zeros((EXPERTS, capacity, D), jnp.bfloat16).at[flat_ids, slots].set(sent)
-    upstream_rows = to_experts(sent_buffer)
+    dnormed = jnp.dot(dlogits, w_router.astype(jnp.float32).T, precision=EXACT)
     dhidden = lax.dot_general(
         upstream_rows, w_out, CONTRACT_COLS, preferred_element_type=jnp.float32
     )
@@ -139,25 +306,28 @@
     back_rows = lax.dot_general(
         dpre, w_in, CONTRACT_COLS, preferred_element_type=jnp.float32
     ).astype(jnp.bfloat16)
-    back = return_sums(back_rows, capacity)
-    dnormed = dnormed + jnp.sum(back[flat_ids, slots].reshape(length, TOP, D), axis=1)
+    back = return_sums(back_rows, capacity).reshape(EXPERTS * capacity, D)
+    dnormed = dnormed + jnp.dot(jnp.sum(place_hot, axis=1), back, precision=EXACT)
     dmean = jnp.mean(dnormed, axis=-1, keepdims=True)
     dproj = jnp.mean(dnormed * vhat, axis=-1, keepdims=True)
     dresid = upstream + lrstd * (dnormed - dmean - vhat * dproj)
     normalized_gradient = dresid * swish_slope(before_activation) * batchnorm_gain_scale
-    first_moment_sum, second_moment_sum = lax.psum(
-        (
-            jnp.sum(normalized_gradient, axis=0),
-            jnp.sum(normalized_gradient * normalized_input, axis=0),
+    moment_sums = all_sums(
+        jnp.stack(
+            [
+                jnp.sum(normalized_gradient, axis=0),
+                jnp.sum(normalized_gradient * normalized_input, axis=0),
+            ]
         ),
-        ("dp", "tm"),
+        None,
+        1,
     )
     convolution_gradient = (
         inverse_deviation
         * (
             normalized_gradient
-            - first_moment_sum / element_count
-            - normalized_input * second_moment_sum / element_count
+            - moment_sums[0] / element_count
+            - normalized_input * moment_sums[1] / element_count
         )
     ).astype(jnp.bfloat16)
     grad_rimmed = extended(convolution_gradient[None], (("tm", 1),), half)[0].astype(jnp.float32)
@@ -166,7 +336,7 @@
     local_taps = jnp.stack(
         [jnp.sum(dconv_f * rimmed[lag : lag + length], axis=0) for lag in range(TAPS)]
     )
-    grad_taps = lax.psum(local_taps, ("dp", "tm"))
+    grad_taps = taps_sum(local_taps, 2)
     grad_w_in, grad_w_out = (
         lax.psum_scatter(grad_in_local, "dp", scatter_dimension=0, tiled=True),
         lax.psum_scatter(grad_out_local, "dp", scatter_dimension=1, tiled=True),

time: 1180 us -> 746 us (0.63)
  blocking collectives: 227 us -> 0 us
  waiting for transfers between devices: 698 us -> 508 us
  local copies, waits for them, and re-layouts: 104 us -> 22.2 us
  Pallas kernels: 0 us -> 72.1 us
    psum x1 -> x0, waiting for transfers between devices: 236 us -> none  [body(): grad_taps = lax.psum(local_taps, ('dp', 'tm'))]
    psum x3 -> x0, blocking collectives: 227 us -> none  [the longest x1 79.8 us: body(): mean = lax.psum(jnp.sum(conv, axis=0), ('dp', 'tm')) / element_count]
    pallas_call x0 -> x3, Pallas kernels: none -> 72.1 us  [the longest x2 43.2 us: all_sums(): pl.pallas_call(functools.partial(sums_kernel, count), out_shape=jax.Shape...]
    scatter x2 -> x0, local copies, waits for them, and re-layouts: 58.7 us -> none  [body(): jnp.zeros((EXPERTS, capacity, D), jnp.bfloat16).at[flat_ids, slots]]
    all_to_all x2, waiting for transfers between devices: 230 us -> 265 us  [to_experts(): lax.all_to_all(copies, 'tm', split_axis=0, concat_axis=0, tiled=True)]
  transfers between devices with their start and end apart: 11 -> 10, of which waited for: 5 -> 4; matrix products, arithmetic and copies ran while one was open for 12% -> 11% of each run, Pallas kernels for 0% -> 6%
where the time goes in v1:
time: 746 us; the launch traced here: 736 us
  waiting for transfers between devices  508 us (68%)
  Pallas kernels  72.1 us (10%)
  matrix products  48.4 us (6%)
  starting transfers between devices  38.5 us (5%)
  other arithmetic  31.5 us (4%)
  local copies, waits for them, and re-layouts  22.2 us (3%)
  between operations  16 us (2%)
    all_to_all x2, waiting for transfers between devices, to_experts(): lax.all_to_all(copies, 'tm', split_axis=0, concat_axis=0, tiled=True)  265 us
    all_to_all x2, waiting for transfers between devices, return_sums(): lax.all_to_all(partial_value.reshape(tm_size, capacity, width), 'tm', spl...  243 us
    pallas_call x2, Pallas kernels, all_sums(): pl.pallas_call(functools.partial(sums_kernel, count), out_shape=jax.Shape...  43.2 us
    pallas_call x1, Pallas kernels, taps_sum(): pl.pallas_call(taps_kernel, out_shape=jax.ShapeDtypeStruct(padded.shape,...  28.9 us
  transfers between devices with their start and end apart: 10, of which 4 were waited for; matrix products, arithmetic and copies ran while one was open for 11% of the time, Pallas kernels for 6%

profile of v1, /device:TPU:1, one launch (start us, length us, event | category | flops | bytes accessed | tf_op | source)
XLA Modules:
  0.0 736.5 jit_solution(16744221608546703146)
XLA Ops:
  8.1 4.9 collective-permute-start
  27.2 24.8 %shard_map.128 = f32[2,1536]{1,0:T(2,128)} custom-call(f32[2,1536]{1,0:T(2,128)} %pad_maximum_fusion.x_ref), custom_call_target="tpu_custom_call" | custom-call | tf_op jit(solution)/shard_map/pallas_call | solution.py:146
  56.0 3.4 broadcast_in_dim.10
  59.4 8.5 %all-to-all-start = ((bf16[64,32,1536]{2,1,0:T(8,128)(2,1)}), bf16[64,32,1536]{2,1,0:T(8,128)(2,1)}, u32[]{:S(2)}, u32[]{:S(2)}) async-start(bf16[64,32,1536]{2,1,0:T(8,128)(2,1)} %bitcast.616), calls=%async_computation | async-start | bytes 12582912 | tf_op jit(solution)/shard_map/all_to_all | solution.py:208
  72.0 136.8 %all-to-all-done = bf16[64,32,1536]{2,1,0:T(8,128)(2,1)} async-done(((bf16[64,32,1536]{2,1,0:T(8,128)(2,1)}), bf16[64,32,1536]{2,1,0:T(8,128)(2,1)}, u32[]{:S(2)}, u32[]{:S(2)}) %all-to-all-start) | async-done | bytes 6291488 | tf_op jit(solution)/shard_map/all_to_all | solution.py:208
  208.8 4.5 broadcast_in_dim.12
  213.3 6.0 all-to-all-start.2
  219.3 5.8 fusion.124
  226.7 5.4 convolution_convert_fusion.1
  232.1 128.0 %all-to-all-done.2 = bf16[64,32,1536]{2,1,0:T(8,128)(2,1)} async-done(((bf16[64,32,1536]{2,1,0:T(8,128)(2,1)}), bf16[64,32,1536]{2,1,0:T(8,128)(2,1)}, u32[]{:S(2)}, u32[]{:S(2)}) %all-to-all-start.2) | async-done | bytes 6291488 | tf_op jit(solution)/shard_map/all_to_all | solution.py:208
  360.1 6.0 all-to-all-start.1
  366.1 7.8 %multiply_convert_fusion = bf16[2048,384]{1,0:T(8,128)(2,1)S(1)} fusion(f32[2048,384]{1,0:T(8,128)} %copy-done.81, bf16[2048,1536]{1,0:T(8,128)(2,1)} %bitcast.52, bf16[384,1536]{1,0:T(8,128)(2,1)S(1)} %copy-done), kind=kOutput, calls=%fused_computation.35 | convolution fusion | flops 2422996992 | bytes 12189696 | tf_op jit(solution)/shard_map/dot_general | solution.py:298
  375.1 5.5 convolution_convert_fusion
  380.6 126.3 %all-to-all-done.1 = bf16[64,32,1536]{2,1,0:T(8,128)(2,1)} async-done(((bf16[64,32,1536]{2,1,0:T(8,128)(2,1)}), bf16[64,32,1536]{2,1,0:T(8,128)(2,1)}, u32[]{:S(2)}, u32[]{:S(2)}) %all-to-all-start.1) | async-done | bytes 6291488 | tf_op jit(solution)/shard_map/all_to_all | solution.py:216
  506.9 6.0 all-to-all-start.3
  513.0 8.1 %fusion.125 = f32[1536,384]{1,0:T(8,128)} fusion(bf16[2048,1536]{1,0:T(8,128)(2,1)} %bitcast.39, bf16[2048,384]{1,0:T(8,128)(2,1)} %copy-done.80), kind=kOutput, calls=%fused_computation.304 | convolution fusion | flops 2415919104 | bytes 10223616 | tf_op jit(solution)/shard_map/dot_general | solution.py:302
  521.3 7.8 %fusion.116 = f32[384,1536]{1,0:T(8,128)} fusion(bf16[2048,1536]{1,0:T(8,128)(2,1)} %bitcast.52, f32[2048,384]{1,0:T(8,128)} %copy-done.81), kind=kOutput, calls=%fused_computation.295 | convolution fusion | flops 2419851264 | bytes 11796480 | tf_op jit(solution)/shard_map/dot_general | solution.py:303
  529.2 4.1 convert_reduce_fusion.1
  537.3 116.5 %all-to-all-done.3 = bf16[64,32,1536]{2,1,0:T(8,128)(2,1)} async-done(((bf16[64,32,1536]{2,1,0:T(8,128)(2,1)}), bf16[64,32,1536]{2,1,0:T(8,128)(2,1)}, u32[]{:S(2)}, u32[]{:S(2)}) %all-to-all-start.3) | async-done | bytes 6291488 | tf_op jit(solution)/shard_map/all_to_all | solution.py:216
  653.8 4.1 convert_reduce_fusion
  662.6 18.3 %shard_map.129 = f32[2,1536]{1,0:T(2,128)} custom-call(f32[2,1536]{1,0:T(2,128)} %pad_maximum_fusion.1.x_ref), custom_call_target="tpu_custom_call" | custom-call | tf_op jit(solution)/shard_map/pallas_call | solution.py:146
  681.8 3.2 fusion.33
  693.1 28.9 %shard_map.130 = f32[16,2,1536]{2,1,0:T(2,128)} custom-call(f32[16,2,1536]{2,1,0:T(2,128)} %reshape.206.x_ref), custom_call_target="tpu_custom_call" | custom-call | tf_op jit(solution)/shard_map/pallas_call | solution.py:182
  724.1 5.2 fusion.100
  (265 shorter events, 44.4 us)
Async XLA Ops:
  7.2 219.6 %copy-start = (bf16[384,1536]{1,0:T(8,128)(2,1)S(1)}, bf16[384,1536]{1,0:T(8,128)(2,1)}, u32[]{:S(2)}) copy-start(bf16[384,1536]{1,0:T(8,128)(2,1)} %param.15) | copy-start | bytes 3538948
  8.1 13.6 %collective-permute-start = (bf16[1,15,1536]{2,1,0:T(8,128)(2,1)S(1)}, bf16[1,15,1536]{2,1,0:T(8,128)(2,1)S(1)}, u32[]{:S(2)}, u32[]{:S(2)}) collective-permute-start(bf16[1,15,1536]{2,1,0:T(8,128)(2,1)S(1)} %get-tuple-element.90), channel_id=1, source_target_pairs={{0,1},{1,2},{2,3},{3,4},{4,5},{5,6},{6,7},{7,8},{8,9},{9,10},{10,1... | collective-permute-start | bytes 138248 | tf_op jit(solution)/shard_map/ppermute | solution.py:27
  13.1 8.7 %collective-permute-start.1 = (bf16[1,15,1536]{2,1,0:T(8,128)(2,1)S(1)}, bf16[1,15,1536]{2,1,0:T(8,128)(2,1)S(1)}, u32[]{:S(2)}, u32[]{:S(2)}) collective-permute-start(bf16[1,15,1536]{2,1,0:T(8,128)(2,1)S(1)} %get-tuple-element.91), channel_id=1, source_target_pairs={{1,0},{2,1},{3,2},{4,3},{5,4},{6,5},{7,6},{8,7},{9,8},{10,9},{11,1... | collective-permute-start | bytes 138248 | tf_op jit(solution)/shard_map/ppermute | solution.py:30
  59.4 149.4 %all-to-all-start = ((bf16[64,32,1536]{2,1,0:T(8,128)(2,1)}), bf16[64,32,1536]{2,1,0:T(8,128)(2,1)}, u32[]{:S(2)}, u32[]{:S(2)}) async-start(bf16[64,32,1536]{2,1,0:T(8,128)(2,1)} %bitcast.616), calls=%async_computation | async-start | bytes 12582912 | tf_op jit(solution)/shard_map/all_to_all | solution.py:208
  213.3 146.8 %all-to-all-start.2 = ((bf16[64,32,1536]{2,1,0:T(8,128)(2,1)}), bf16[64,32,1536]{2,1,0:T(8,128)(2,1)}, u32[]{:S(2)}, u32[]{:S(2)}) async-start(bf16[64,32,1536]{2,1,0:T(8,128)(2,1)} %bitcast.617), calls=%async_computation.2 | async-start | bytes 12582912 | tf_op jit(solution)/shard_map/all_to_all | solution.py:208
  360.1 146.8 %all-to-all-start.1 = ((bf16[64,32,1536]{2,1,0:T(8,128)(2,1)}), bf16[64,32,1536]{2,1,0:T(8,128)(2,1)}, u32[]{:S(2)}, u32[]{:S(2)}) async-start(bf16[64,32,1536]{2,1,0:T(8,128)(2,1)} %bitcast.621), calls=%async_computation.1 | async-start | bytes 12582912 | tf_op jit(solution)/shard_map/all_to_all | solution.py:216
  506.9 146.8 %all-to-all-start.3 = ((bf16[64,32,1536]{2,1,0:T(8,128)(2,1)}), bf16[64,32,1536]{2,1,0:T(8,128)(2,1)}, u32[]{:S(2)}, u32[]{:S(2)}) async-start(bf16[64,32,1536]{2,1,0:T(8,128)(2,1)} %bitcast.620), calls=%async_computation.3 | async-start | bytes 12582912 | tf_op jit(solution)/shard_map/all_to_all | solution.py:216
  512.9 216.4 %reduce-scatter.3.cloned.1.call-start = ((), (), s32[]{:S(2)}) async-start(), calls=%async_computation.6 | async-start | bytes 2949120 | tf_op jit(solution)/shard_map/reduce_scatter | solution.py:341
  521.1 208.3 %reduce-scatter.5.cloned.1.call-start = ((), (), s32[]{:S(2)}) async-start(), calls=%async_computation.7 | async-start | bytes 2949120 | tf_op jit(solution)/shard_map/reduce_scatter | solution.py:342
  537.3 120.7 %copy-start.69 = (f32[128]{0:T(128)S(1)}, f32[128]{0:T(128)}, u32[]{:S(2)}) copy-start(f32[128]{0:T(128)} %copy-done.68) | copy-start | bytes 1540
  537.3 120.7 %copy-start.74 = (f32[128]{0:T(128)S(1)}, f32[128]{0:T(128)}, u32[]{:S(2)}) copy-start(f32[128]{0:T(128)} %copy-done.73) | copy-start | bytes 1540
  685.0 38.7 %collective-permute-start.2 = (bf16[1,15,1536]{2,1,0:T(8,128)(2,1)S(1)}, bf16[1,15,1536]{2,1,0:T(8,128)(2,1)S(1)}, u32[]{:S(2)}, u32[]{:S(2)}) collective-permute-start(bf16[1,15,1536]{2,1,0:T(8,128)(2,1)S(1)} %get-tuple-element.88), channel_id=1, source_target_pairs={{0,1},{1,2},{2,3},{3,4},{4,5},{5,6},{6,7},{7,8},{8,9},{9,10},{10,1... | collective-permute-start | bytes 138248 | tf_op jit(solution)/shard_map/ppermute | solution.py:27
  687.1 36.6 %collective-permute-start.3 = (bf16[1,15,1536]{2,1,0:T(8,128)(2,1)S(1)}, bf16[1,15,1536]{2,1,0:T(8,128)(2,1)S(1)}, u32[]{:S(2)}, u32[]{:S(2)}) collective-permute-start(bf16[1,15,1536]{2,1,0:T(8,128)(2,1)S(1)} %get-tuple-element.89), channel_id=1, source_target_pairs={{1,0},{2,1},{3,2},{4,3},{5,4},{6,5},{7,6},{8,7},{9,8},{10,9},{11,1... | collective-permute-start | bytes 138248 | tf_op jit(solution)/shard_map/ppermute | solution.py:30
  691.3 32.6 %copy-start.12 = (f32[1536]{0:T(1024)S(1)}, f32[1536]{0:T(1024)}, u32[]{:S(2)}) copy-start(f32[1536]{0:T(1024)} %copy-done.11) | copy-start | bytes 18436
  691.3 32.6 %copy-start.14 = (f32[1536]{0:T(1024)S(1)}, f32[1536]{0:T(1024)}, u32[]{:S(2)}) copy-start(f32[1536]{0:T(1024)} %copy-done.13) | copy-start | bytes 18436
  691.3 32.6 %copy-start.16 = (f32[1536]{0:T(1024)S(1)}, f32[1536]{0:T(1024)}, u32[]{:S(2)}) copy-start(f32[1536]{0:T(1024)} %copy-done.15) | copy-start | bytes 18436
  691.3 32.6 %copy-start.18 = (f32[1536]{0:T(1024)S(1)}, f32[1536]{0:T(1024)}, u32[]{:S(2)}) copy-start(f32[1536]{0:T(1024)} %copy-done.17) | copy-start | bytes 18436
  691.3 32.6 %copy-start.20 = (f32[1536]{0:T(1024)S(1)}, f32[1536]{0:T(1024)}, u32[]{:S(2)}) copy-start(f32[1536]{0:T(1024)} %copy-done.19) | copy-start | bytes 18436
  691.3 32.6 %copy-start.22 = (f32[1536]{0:T(1024)S(1)}, f32[1536]{0:T(1024)}, u32[]{:S(2)}) copy-start(f32[1536]{0:T(1024)} %copy-done.21) | copy-start | bytes 18436
  691.3 32.6 %copy-start.24 = (f32[1536]{0:T(1024)S(1)}, f32[1536]{0:T(1024)}, u32[]{:S(2)}) copy-start(f32[1536]{0:T(1024)} %copy-done.23) | copy-start | bytes 18436
  691.3 32.6 %copy-start.26 = (f32[1536]{0:T(1024)S(1)}, f32[1536]{0:T(1024)}, u32[]{:S(2)}) copy-start(f32[1536]{0:T(1024)} %copy-done.25) | copy-start | bytes 18436
  691.3 32.6 %copy-start.28 = (f32[1536]{0:T(1024)S(1)}, f32[1536]{0:T(1024)}, u32[]{:S(2)}) copy-start(f32[1536]{0:T(1024)} %copy-done.27) | copy-start | bytes 18436
  691.3 32.6 %copy-start.30 = (f32[1536]{0:T(1024)S(1)}, f32[1536]{0:T(1024)}, u32[]{:S(2)}) copy-start(f32[1536]{0:T(1024)} %copy-done.29) | copy-start | bytes 18436
  691.4 32.6 %copy-start.32 = (f32[1536]{0:T(1024)S(1)}, f32[1536]{0:T(1024)}, u32[]{:S(2)}) copy-start(f32[1536]{0:T(1024)} %copy-done.31) | copy-start | bytes 18436
  (68 other events, 818.3 us)
Sparse Core Ops, SparseCore 0:
  521.2 33.6 reduce-scatter.2
  558.0 34.1 reduce-scatter.4

commit v2 on v1

--- a/solution.py
+++ b/solution.py
@@ -199,28 +199,313 @@
     return total.reshape(2 * NEAR, x.shape[1])[: x.shape[0]]
 
 
-def to_experts(buffer):
-    tm_size = lax.axis_size("tm")
-    group = tm_size // EXPERTS
-    capacity = buffer.shape[1]
-    width = buffer.shape[2]
-    copies = jnp.repeat(buffer, group, axis=0)
-    received = lax.all_to_all(copies, "tm", split_axis=0, concat_axis=0, tiled=True)
-    return received.reshape(tm_size * capacity, width)
-
-
-def return_sums(partial_value, capacity):
-    tm_size = lax.axis_size("tm")
-    group = tm_size // EXPERTS
-    width = partial_value.shape[1]
-    returned = lax.all_to_all(
-        partial_value.reshape(tm_size, capacity, width),
-        "tm",
-        split_axis=0,
-        concat_axis=0,
-        tiled=True,
-    )
-    return jnp.sum(returned.reshape(EXPERTS, group, capacity, width).astype(jnp.float32), axis=1)
+CORES = 2
+LINES = 4
+ZEDS = EXPERTS
+SPAN = ZEDS * CORES
+HALF = ZEDS // 2
+TURN = ((3, 1, 0, 2), (1, 3, 2, 0), (0, 2, 1, 3), (2, 0, 3, 1))
+SWEEP = (0, 1, 7, 2, 6, 3, 5, 4)
+
+
+def position(ids):
+    return HALF * (ids % 2) + ids // 2
+
+
+def home_to_work():
+    pairs = []
+    for y in range(LINES):
+        for z in range(ZEDS):
+            line, half = z % HALF, z // HALF
+            source_z = HALF * half + TURN[y][line]
+            for core in range(CORES):
+                pairs.append((line * SPAN + source_z * CORES + core, y * SPAN + z * CORES + core))
+    return pairs
+
+
+class Place:
+    def __init__(self):
+        self.dp, tm = lax.axis_index("dp"), lax.axis_index("tm")
+        self.core, self.z, self.y = tm % CORES, (tm // CORES) % ZEDS, tm // SPAN
+
+    def at(self, y, z, core):
+        return (self.dp, (y % LINES) * SPAN + z * CORES + core)
+
+    def sibling(self):
+        return self.at(self.y, self.z, 1 - self.core)
+
+    def line(self, step):
+        return self.at(self.y + step + LINES, self.z, self.core)
+
+    def zed(self, z):
+        return self.at(self.y, z, self.core)
+
+    def enter(self):
+        barrier = pltpu.get_barrier_semaphore()
+        peers = [self.sibling(), self.line(1), self.line(-1)]
+        peers += [self.zed((self.z + k) % ZEDS) for k in range(1, ZEDS)]
+        for peer in peers:
+            pl.semaphore_signal(barrier, inc=1, device_id=peer, device_id_type=MESH)
+        pl.semaphore_wait(barrier, len(peers))
+
+
+def remote(source, target, send_sem, recv_sem, device):
+    return pltpu.make_async_remote_copy(
+        src_ref=source,
+        dst_ref=target,
+        send_sem=send_sem,
+        recv_sem=recv_sem,
+        device_id=device,
+        device_id_type=MESH,
+    )
+
+
+def dispatch_kernel(
+    x_ref, u_ref, rx_ref, ru_ref, own_sem, z_send, z_recv, pair_send, pair_recv, y_send, y_recv
+):
+    place = Place()
+    y, z, core = place.y, place.z, place.core
+    arrays = ((x_ref, rx_ref), (u_ref, ru_ref))
+    place.enter()
+    waits = []
+
+    def z_copy(a, k):
+        source, rows = arrays[a]
+        target = (z + k) % ZEDS
+        return remote(
+            source.at[target], rows.at[core, y, z], z_send.at[a, k], z_recv.at[a, k], place.zed(target)
+        )
+
+    def own_copy(a):
+        source, rows = arrays[a]
+        return pltpu.make_async_copy(source.at[z], rows.at[core, y, z], own_sem.at[a])
+
+    def block(a, from_core, step, k):
+        return arrays[a][1].at[from_core, (y + step + LINES) % LINES, (z - k + ZEDS) % ZEDS]
+
+    def pass_on(a, step, k, send_sem, recv_sem, device):
+        ref = block(a, core, step, k)
+        copy = remote(ref, ref, send_sem, recv_sem, device)
+        copy.start()
+        waits.append(copy)
+
+    def arrived(a, from_core, step, k, send_sem, recv_sem):
+        ref = block(a, from_core, step, k)
+        remote(ref, ref, send_sem, recv_sem, place.sibling()).wait_recv()
+
+    def to_pair(a, step, k):
+        index = step % LINES * ZEDS + k
+        pass_on(a, step, k, pair_send.at[a, index], pair_recv.at[a, index], place.sibling())
+
+    for a in range(2):
+        own_copy(a).start()
+        for k in SWEEP[1:]:
+            z_copy(a, k).start()
+    items = [(a, i, k) for a in range(2) for i, k in enumerate(SWEEP)]
+    for m in range(len(items) + 4):
+        if m < len(items):
+            a, i, k = items[m]
+            if k == 0:
+                own_copy(a).wait()
+            else:
+                arrived(a, core, 0, k, z_send.at[a, k], z_recv.at[a, k])
+            for way, step in ((0, 1), (1, -1)):
+                pass_on(a, 0, k, y_send.at[a, way, k], y_recv.at[a, way, k], place.line(step))
+            to_pair(a, 0, k)
+        if 0 <= m - 2 < len(items):
+            a, i, k = items[m - 2]
+            for way, step in ((0, 1), (1, -1)):
+                arrived(a, core, -step, k, y_send.at[a, way, k], y_recv.at[a, way, k])
+                if i % 2 == way:
+                    pass_on(a, -step, k, y_send.at[a, 2, k], y_recv.at[a, 2, k], place.line(step))
+                to_pair(a, -step, k)
+        if m >= 4:
+            a, i, k = items[m - 4]
+            arrived(a, core, 2, k, y_send.at[a, 2, k], y_recv.at[a, 2, k])
+            to_pair(a, 2, k)
+    for a in range(2):
+        for step in range(LINES):
+            for k in range(ZEDS):
+                index = step * ZEDS + k
+                arrived(a, 1 - core, step, k, pair_send.at[a, index], pair_recv.at[a, index])
+    for a in range(2):
+        for k in SWEEP[1:]:
+            z_copy(a, k).wait_send()
+    for copy in waits:
+        copy.wait_send()
+
+
+def dispatch(x, u, collective_id):
+    rows = jax.ShapeDtypeStruct((CORES, LINES) + x.shape, x.dtype)
+    dma = pltpu.SemaphoreType.DMA
+    return pl.pallas_call(
+        dispatch_kernel,
+        out_shape=(rows, rows),
+        in_specs=[pl.BlockSpec(memory_space=pl.ANY)] * 2,
+        out_specs=[pl.BlockSpec(memory_space=pl.ANY)] * 2,
+        scratch_shapes=[
+            dma((2,)),
+            dma((2, ZEDS)),
+            dma((2, ZEDS)),
+            dma((2, LINES * ZEDS)),
+            dma((2, LINES * ZEDS)),
+            dma((2, 3, ZEDS)),
+            dma((2, 3, ZEDS)),
+        ],
+        compiler_params=pltpu.CompilerParams(collective_id=collective_id, has_side_effects=True),
+    )(x, u)
+
+
+PIECES = ((2, 0, 1, None), (2, 1, -1, None), (1, 1, 1, None), (-1, 0, -1, None), (1, 0, 1, 0), (-1, 1, -1, 1))
+PAIR_ORDER = ((2, 0), (2, 1), (1, 1), (3, 0), (1, 0), (3, 1), (0, 0), (0, 1))
+
+
+def return_kernel(
+    p0_ref,
+    p1_ref,
+    o0_ref,
+    o1_ref,
+    pair_held,
+    leaving,
+    line_held,
+    total,
+    pair_send,
+    pair_recv,
+    y_send,
+    y_recv,
+    z_send,
+    z_recv,
+):
+    place = Place()
+    y, z, core = place.y, place.z, place.core
+    arrays = ((p0_ref, o0_ref), (p1_ref, o1_ref))
+    place.enter()
+
+    def pair_copy(a, step, half):
+        source = arrays[a][0].at[1 - core, (y + step) % LINES, pl.ds(half * HALF, HALF)]
+        return remote(
+            source,
+            pair_held.at[a, step, half],
+            pair_send.at[a, step, half],
+            pair_recv.at[a, step, half],
+            place.sibling(),
+        )
+
+    def y_copy(a, piece):
+        return remote(
+            leaving.at[a, piece],
+            line_held.at[a, piece],
+            y_send.at[a, piece],
+            y_recv.at[a, piece],
+            place.line(PIECES[piece][2]),
+        )
+
+    def z_copy(a, target):
+        return remote(
+            total.at[a, target], arrays[a][1].at[z], z_send.at[a, target], z_recv.at[a, z], place.zed(target)
+        )
+
+    def add_up(a, step, half, pieces, store):
+        pair_copy(a, step, half).wait_recv()
+
+        def one(i, carry):
+            value = arrays[a][0][core, (y + step) % LINES, half * HALF + i].astype(jnp.float32)
+            value = value + pair_held[a, step, half, i].astype(jnp.float32)
+            for piece in pieces:
+                value = value + line_held[a, piece, i].astype(jnp.float32)
+            store(i, value.astype(jnp.bfloat16))
+            return carry
+
+        lax.fori_loop(0, HALF, one, 0)
+
+    def send_piece(a, piece):
+        step, half, _, extra = PIECES[piece]
+        if extra is not None:
+            y_copy(a, extra).wait_recv()
+
+        def store(i, value):
+            leaving[a, piece, i] = value
+
+        add_up(a, step % LINES, half, () if extra is None else (extra,), store)
+        y_copy(a, piece).start()
+
+    def finish(a, half):
+        pieces = (4, 3) if half == 0 else (2, 5)
+        for piece in pieces:
+            y_copy(a, piece).wait_recv()
+
+        def store(i, value):
+            total[a, half * HALF + i] = value
+
+        add_up(a, 0, half, pieces, store)
+        for i in range(HALF):
+            target = half * HALF + i
+
+            @pl.when(target != z)
+            def _():
+                z_copy(a, target).start()
+
+            @pl.when(target == z)
+            def _():
+                arrays[a][1][target] = total[a, target]
+
+    for a in range(2):
+        for step, half in PAIR_ORDER:
+            pair_copy(a, step, half).start()
+    for piece in range(4):
+        send_piece(0, piece)
+    for piece in range(2):
+        send_piece(1, piece)
+    for piece in range(4, 6):
+        send_piece(0, piece)
+    for piece in range(2, 4):
+        send_piece(1, piece)
+    for half in range(2):
+        finish(0, half)
+    for piece in range(4, 6):
+        send_piece(1, piece)
+    for half in range(2):
+        finish(1, half)
+    for a in range(2):
+        for k in range(1, ZEDS):
+            other = (z + k) % ZEDS
+            remote(
+                total.at[a, other], arrays[a][1].at[other], z_send.at[a, other], z_recv.at[a, other], place.zed(other)
+            ).wait_recv()
+    for a in range(2):
+        for step, half in PAIR_ORDER:
+            pair_copy(a, step, half).wait_send()
+        for piece in range(len(PIECES)):
+            y_copy(a, piece).wait_send()
+        for k in range(1, ZEDS):
+            z_copy(a, (z + k) % ZEDS).wait_send()
+
+
+def give_back(p0, p1, collective_id):
+    tile = p0.shape[3:]
+    out = jax.ShapeDtypeStruct((ZEDS,) + tile, p0.dtype)
+    dma = pltpu.SemaphoreType.DMA
+    return pl.pallas_call(
+        return_kernel,
+        out_shape=(out, out),
+        in_specs=[pl.BlockSpec(memory_space=pltpu.VMEM)] * 2,
+        out_specs=[pl.BlockSpec(memory_space=pltpu.VMEM)] * 2,
+        scratch_shapes=[
+            pltpu.VMEM((2, LINES, 2, HALF) + tile, p0.dtype),
+            pltpu.VMEM((2, len(PIECES), HALF) + tile, p0.dtype),
+            pltpu.VMEM((2, len(PIECES), HALF) + tile, p0.dtype),
+            pltpu.VMEM((2, ZEDS) + tile, p0.dtype),
+            dma((2, LINES, 2)),
+            dma((2, LINES, 2)),
+            dma((2, len(PIECES))),
+            dma((2, len(PIECES))),
+            dma((2, ZEDS)),
+            dma((2, ZEDS)),
+        ],
+        compiler_params=pltpu.CompilerParams(
+            collective_id=collective_id, has_side_effects=True, vmem_limit_bytes=48 << 20
+        ),
+    )(p0, p1)
 
 
 def body(
@@ -236,6 +521,9 @@
 ):
     length = frames.shape[1]
     half = TAPS // 2
+    moves = home_to_work()
+    w_in = lax.ppermute(w_in, "tm", moves)
+    w_out = lax.ppermute(w_out, "tm", moves)
     element_count = lax.axis_size("dp") * lax.axis_size("tm") * length
     capacity = length * TOP // EXPERTS
     signal = frames[0].astype(jnp.float32)
@@ -269,7 +557,7 @@
         jnp.int32
     )
     slots = jnp.sum((jnp.cumsum(expert_hot, axis=0) - 1) * expert_hot, axis=1)
-    places = (flat_ids * capacity + slots).reshape(length, TOP)
+    places = (position(flat_ids) * capacity + slots).reshape(length, TOP)
     place_hot = places[:, :, None] == jnp.arange(EXPERTS * capacity, dtype=jnp.int32)[None, None, :]
     place_any = jnp.any(place_hot, axis=1).astype(jnp.bfloat16)
     place_hot = place_hot.astype(jnp.float32)
@@ -280,12 +568,27 @@
 
     buffer = bucketed(normed).astype(jnp.bfloat16).reshape(EXPERTS, capacity, D)
     sent_buffer = (gate_rows[:, None] * bucketed(cotangent[0])).astype(jnp.bfloat16)
-    rows = to_experts(buffer)
-    upstream_rows = to_experts(sent_buffer.reshape(EXPERTS, capacity, D))
+    sent_buffer = sent_buffer.reshape(EXPERTS, capacity, D)
+    rows, upstream_rows = dispatch(buffer, sent_buffer, 3)
+    rows_shape = rows.shape
+    rows, upstream_rows = rows.reshape(-1, D), upstream_rows.reshape(-1, D)
     pre = jnp.dot(rows, w_in, preferred_element_type=jnp.float32)
     hidden = jax.nn.silu(pre).astype(jnp.bfloat16)
     partial_value = jnp.dot(hidden, w_out, preferred_element_type=jnp.float32).astype(jnp.bfloat16)
-    combined = return_sums(partial_value, capacity).reshape(EXPERTS * capacity, D)
+    dhidden = lax.dot_general(
+        upstream_rows, w_out, CONTRACT_COLS, preferred_element_type=jnp.float32
+    )
+    dpre = (dhidden * swish_slope(pre)).astype(jnp.bfloat16)
+    back_rows = lax.dot_general(
+        dpre, w_in, CONTRACT_COLS, preferred_element_type=jnp.float32
+    ).astype(jnp.bfloat16)
+    grad_in_local = lax.dot_general(rows, dpre, CONTRACT_ROWS, preferred_element_type=jnp.float32)
+    grad_out_local = lax.dot_general(
+        hidden, upstream_rows, CONTRACT_ROWS, preferred_element_type=jnp.float32
+    )
+    combined, back = give_back(partial_value.reshape(rows_shape), back_rows.reshape(rows_shape), 4)
+    combined = combined.reshape(EXPERTS * capacity, D).astype(jnp.float32)
+    back = back.reshape(EXPERTS * capacity, D).astype(jnp.float32)
     expert_out = [
         jnp.dot(place_hot[:, k], combined, precision=EXACT) for k in range(TOP)
     ]
@@ -295,18 +598,6 @@
     dpick = (dgate[0] - dgate[1]) * first * (1.0 - first)
     dlogits = (onehot[:, 0] - onehot[:, 1]) * dpick[:, None]
     dnormed = jnp.dot(dlogits, w_router.astype(jnp.float32).T, precision=EXACT)
-    dhidden = lax.dot_general(
-        upstream_rows, w_out, CONTRACT_COLS, preferred_element_type=jnp.float32
-    )
-    dpre = (dhidden * swish_slope(pre)).astype(jnp.bfloat16)
-    grad_in_local = lax.dot_general(rows, dpre, CONTRACT_ROWS, preferred_element_type=jnp.float32)
-    grad_out_local = lax.dot_general(
-        hidden, upstream_rows, CONTRACT_ROWS, preferred_element_type=jnp.float32
-    )
-    back_rows = lax.dot_general(
-        dpre, w_in, CONTRACT_COLS, preferred_element_type=jnp.float32
-    ).astype(jnp.bfloat16)
-    back = return_sums(back_rows, capacity).reshape(EXPERTS * capacity, D)
     dnormed = dnormed + jnp.dot(jnp.sum(place_hot, axis=1), back, precision=EXACT)
     dmean = jnp.mean(dnormed, axis=-1, keepdims=True)
     dproj = jnp.mean(dnormed * vhat, axis=-1, keepdims=True)
@@ -337,10 +628,13 @@
         [jnp.sum(dconv_f * rimmed[lag : lag + length], axis=0) for lag in range(TAPS)]
     )
     grad_taps = taps_sum(local_taps, 2)
+    returns = [(target, source) for source, target in moves]
     grad_w_in, grad_w_out = (
         lax.psum_scatter(grad_in_local, "dp", scatter_dimension=0, tiled=True),
         lax.psum_scatter(grad_out_local, "dp", scatter_dimension=1, tiled=True),
     )
+    grad_w_in = lax.ppermute(grad_w_in, "tm", returns)
+    grad_w_out = lax.ppermute(grad_w_out, "tm", returns)
     return (mixed[None], grad_frames[None], grad_taps, grad_w_in, grad_w_out)
 
 

time: 746 us -> 504 us (0.68)
  waiting for transfers between devices: 508 us -> 22 us
  Pallas kernels: 72.1 us -> 353 us
  starting transfers between devices: 38.5 us -> 19.6 us
  local copies, waits for them, and re-layouts: 22.2 us -> 13.8 us
  other arithmetic: 31.5 us -> 23.5 us
    all_to_all x4 -> x0, waiting for transfers between devices: 508 us -> none  [the longest x2 265 us: to_experts(): lax.all_to_all(copies, 'tm', split_axis=0, concat_axis=0, tiled=True)]
    pallas_call x0 -> x2, Pallas kernels: none -> 144 us  [the longest x1 76.8 us: give_back(): pl.pallas_call(return_kernel, out_shape=(out, out), in_specs=[pl.BlockSpe...]
    pallas_call x2, Pallas kernels: 43.2 us -> 180 us  [all_sums(): pl.pallas_call(functools.partial(sums_kernel, count), out_shape=jax.Shape...]
    all_to_all x4 -> x0, starting transfers between devices: 26.4 us -> none  [the longest x2 14.5 us: to_experts(): lax.all_to_all(copies, 'tm', split_axis=0, concat_axis=0, tiled=True)]
    ppermute x0 -> x4, waiting for transfers between devices: none -> 22 us  [the longest x1 12.5 us: body(): grad_w_out = lax.ppermute(grad_w_out, 'tm', returns)]
    reduce_sum x3 -> x1, other arithmetic: 9.1 us -> 0.15 us  [body(): jnp.sum(place_hot, axis=1)]
    broadcast_in_dim x2 -> x0, local copies, waits for them, and re-layouts: 7.92 us -> none  [to_experts(): copies = jnp.repeat(buffer, group, axis=0)]
    ppermute x0 -> x4, starting transfers between devices: none -> 7.62 us  [the longest x1 2.99 us: body(): w_in = lax.ppermute(w_in, 'tm', moves)]
  transfers between devices with their start and end apart: 10 -> 10, of which waited for: 4 -> 2; matrix products, arithmetic and copies ran while one was open for 11% -> 14% of each run, Pallas kernels for 6% -> 71%
where the time goes in v2:
time: 504 us; the launch traced here: 495 us
  Pallas kernels  353 us (70%)
  matrix products  46.3 us (9%)
  other arithmetic  23.5 us (5%)
  waiting for transfers between devices  22 us (4%)
  starting transfers between devices  19.6 us (4%)
  between operations  16.1 us (3%)
  local copies, waits for them, and re-layouts  13.8 us (3%)
    pallas_call x2, Pallas kernels, all_sums(): pl.pallas_call(functools.partial(sums_kernel, count), out_shape=jax.Shape...  180 us
    pallas_call x1, Pallas kernels, give_back(): pl.pallas_call(return_kernel, out_shape=(out, out), in_specs=[pl.BlockSpe...  76.8 us
    pallas_call x1, Pallas kernels, dispatch(): pl.pallas_call(dispatch_kernel, out_shape=(rows, rows), in_specs=[pl.Bloc...  67.2 us
    pallas_call x1, Pallas kernels, taps_sum(): pl.pallas_call(taps_kernel, out_shape=jax.ShapeDtypeStruct(padded.shape,...  29.7 us
    ppermute x1, waiting for transfers between devices, body(): grad_w_out = lax.ppermute(grad_w_out, 'tm', returns)  12.5 us
  transfers between devices with their start and end apart: 10, of which 2 were waited for; matrix products, arithmetic and copies ran while one was open for 14% of the time, Pallas kernels for 71%

profile of v2, /device:TPU:1, one launch (start us, length us, event | category | flops | bytes accessed | tf_op | source)
XLA Modules:
  0.0 494.8 jit_solution(10308455997955256031)
XLA Ops:
  8.1 4.9 collective-permute-start
  13.0 1.9 collective-permute-start.1
  14.9 3.0 collective-permute-start.2
  17.9 2.8 collective-permute-start.3
  29.2 3.1 fusion.122
  33.4 153.2 %shard_map.128 = f32[2,1536]{1,0:T(2,128)} custom-call(f32[2,1536]{1,0:T(2,128)} %pad_maximum_fusion.x_ref), custom_call_target="tpu_custom_call" | custom-call | tf_op jit(solution)/shard_map/pallas_call | solution.py:146
  192.2 67.2 %shard_map.129 = (bf16[2,4,8,32,1536]{4,3,2,1,0:T(8,128)(2,1)}, bf16[2,4,8,32,1536]{4,3,2,1,0:T(8,128)(2,1)}) custom-call(bf16[8,32,1536]{2,1,0:T(8,128)(2,1)} %bitcast.615, bf16[8,32,1536]{2,1,0:T(8,128)(2,1)} %bitcast.616), custom_call_target="tpu_custom_call" | custom-call | tf_op jit(solution)/shard_map/pallas_call | solution.py:341
  259.4 6.1 %fusion.126 = f32[2048,384]{1,0:T(8,128)S(1)} fusion(bf16[2048,1536]{1,0:T(8,128)(2,1)} %bitcast.623, bf16[1536,384]{1,0:T(8,128)(2,1)} %collective-permute-done.2), kind=kOutput, calls=%fused_computation.308 | convolution fusion | flops 2415919104 | bytes 10616832 | tf_op jit(solution)/shard_map/dot_general | solution.py:575
  265.6 6.6 %multiply_convert_fusion = bf16[2048,384]{1,0:T(8,128)(2,1)S(1)} fusion(f32[2048,384]{1,0:T(8,128)S(1)} %fusion.126, bf16[2048,1536]{1,0:T(8,128)(2,1)S(1)} %bitcast.622, bf16[384,1536]{1,0:T(8,128)(2,1)} %collective-permute-done.3), kind=kOutput, calls=%fused_computation.33 | convolution fusion | flops 2422996992 | bytes 12189696 | tf_op jit(solution)/shard_map/dot_general | solution.py:578
  273.4 4.9 fusion.127
  278.4 7.8 %fusion.118 = f32[384,1536]{1,0:T(8,128)} fusion(bf16[2048,1536]{1,0:T(8,128)(2,1)} %bitcast.621, f32[2048,384]{1,0:T(8,128)} %copy-done.74), kind=kOutput, calls=%fused_computation.300 | convolution fusion | flops 2419851264 | bytes 11796480 | tf_op jit(solution)/shard_map/dot_general | solution.py:586
  286.2 8.6 %convolution_convert_fusion.1 = bf16[2048,1536]{1,0:T(8,128)(2,1)} fusion(bf16[384,1536]{1,0:T(8,128)(2,1)} %collective-permute-done.3, f32[2048,384]{1,0:T(8,128)} %copy-done.74), kind=kOutput, calls=%fused_computation.1 | convolution fusion | flops 2422996992 | bytes 10616832 | tf_op jit(solution)/shard_map/dot_general | solution.py:577
  294.8 6.8 %convolution_convert_fusion = bf16[2048,1536]{1,0:T(8,128)(2,1)} fusion(bf16[2048,384]{1,0:T(8,128)(2,1)S(1)} %copy-done.73, bf16[1536,384]{1,0:T(8,128)(2,1)} %collective-permute-done.2), kind=kOutput, calls=%fused_computation | convolution fusion | flops 2419064832 | bytes 9043968 | tf_op jit(solution)/shard_map/dot_general | solution.py:582
  301.6 76.8 %shard_map.130 = (bf16[8,32,1536]{2,1,0:T(8,128)(2,1)S(1)}, bf16[8,32,1536]{2,1,0:T(8,128)(2,1)S(1)}) custom-call(bf16[2,4,8,32,1536]{4,3,2,1,0:T(8,128)(2,1)} %bitcast.611, bf16[2,4,8,32,1536]{4,3,2,1,0:T(8,128)(2,1)} %bitcast.612), custom_call_target="tpu_custom_call" | custom-call | tf_op jit(solution)/shard_map/pallas_call | solution.py:488
  381.4 1.9 fusion.119
  383.9 26.5 %shard_map.131 = f32[2,1536]{1,0:T(2,128)} custom-call(f32[2,1536]{1,0:T(2,128)} %pad_maximum_fusion.1.x_ref), custom_call_target="tpu_custom_call" | custom-call | tf_op jit(solution)/shard_map/pallas_call | solution.py:146
  411.2 3.2 fusion.33
  415.2 1.9 collective-permute-start.4
  417.1 3.2 collective-permute-start.5
  423.3 29.7 %shard_map.132 = f32[16,2,1536]{2,1,0:T(2,128)} custom-call(f32[16,2,1536]{2,1,0:T(2,128)} %reshape.238.x_ref), custom_call_target="tpu_custom_call" | custom-call | tf_op jit(solution)/shard_map/pallas_call | solution.py:182
  458.0 4.9 fusion.100
  462.9 9.4 %collective-permute-done.6 = f32[384,384]{1,0:T(8,128)} collective-permute-done((f32[384,384]{1,0:T(8,128)}, f32[384,384]{1,0:T(8,128)}, u32[]{:S(2)}, u32[]{:S(2)}) %collective-permute-start.6) | collective-permute-done | bytes 589856 | tf_op jit(solution)/shard_map/ppermute | solution.py:636
  472.3 12.5 %collective-permute-done.7 = f32[384,384]{1,0:T(8,128)S(1)} collective-permute-done((f32[384,384]{1,0:T(8,128)}, f32[384,384]{1,0:T(8,128)S(1)}, u32[]{:S(2)}, u32[]{:S(2)}) %collective-permute-start.7) | collective-permute-done | bytes 589856 | tf_op jit(solution)/shard_map/ppermute | solution.py:637
  484.8 1.9 copy.34
  (255 shorter events, 29.8 us)
Async XLA Ops:
  7.2 181.8 %copy-start = (bf16[1536,8]{0,1:T(8,128)(2,1)S(1)}, bf16[1536,8]{0,1:T(8,128)(2,1)}, u32[]{:S(2)}) copy-start(bf16[1536,8]{0,1:T(8,128)(2,1)} %param.13) | copy-start | bytes 73732
  7.2 448.7 %reduce-scatter.3.cloned.1.call-start = ((), (), s32[]{:S(2)}) async-start(), calls=%async_computation.2 | async-start | bytes 2949120 | tf_op jit(solution)/shard_map/reduce_scatter | solution.py:633
  8.1 20.0 %collective-permute-start = (bf16[1,15,1536]{2,1,0:T(8,128)(2,1)S(1)}, bf16[1,15,1536]{2,1,0:T(8,128)(2,1)S(1)}, u32[]{:S(2)}, u32[]{:S(2)}) collective-permute-start(bf16[1,15,1536]{2,1,0:T(8,128)(2,1)S(1)} %get-tuple-element.98), channel_id=1, source_target_pairs={{0,1},{1,2},{2,3},{3,4},{4,5},{5,6},{6,7},{7,8},{8,9},{9,10},{10,1... | collective-permute-start | bytes 138248 | tf_op jit(solution)/shard_map/ppermute | solution.py:27
  13.0 15.1 %collective-permute-start.1 = (bf16[1,15,1536]{2,1,0:T(8,128)(2,1)S(1)}, bf16[1,15,1536]{2,1,0:T(8,128)(2,1)S(1)}, u32[]{:S(2)}, u32[]{:S(2)}) collective-permute-start(bf16[1,15,1536]{2,1,0:T(8,128)(2,1)S(1)} %get-tuple-element.99), channel_id=1, source_target_pairs={{1,0},{2,1},{3,2},{4,3},{5,4},{6,5},{7,6},{8,7},{9,8},{10,9},{11,1... | collective-permute-start | bytes 138248 | tf_op jit(solution)/shard_map/ppermute | solution.py:30
  14.9 244.5 %collective-permute-start.2 = (bf16[1536,384]{1,0:T(8,128)(2,1)}, bf16[1536,384]{1,0:T(8,128)(2,1)}, u32[]{:S(2)}, u32[]{:S(2)}) collective-permute-start(bf16[1536,384]{1,0:T(8,128)(2,1)} %param.14), channel_id=1, source_target_pairs={{6,0},{7,1},{18,2},{19,3},{32,4},{33,5},{52,6},{53,7},{14,8},{15,9... | collective-permute-start | bytes 3538952 | tf_op jit(solution)/shard_map/ppermute | solution.py:525
  17.9 247.6 %collective-permute-start.3 = (bf16[384,1536]{1,0:T(8,128)(2,1)}, bf16[384,1536]{1,0:T(8,128)(2,1)}, u32[]{:S(2)}, u32[]{:S(2)}) collective-permute-start(bf16[384,1536]{1,0:T(8,128)(2,1)} %param.15), channel_id=1, source_target_pairs={{6,0},{7,1},{18,2},{19,3},{32,4},{33,5},{52,6},{53,7},{14,8},{15,9... | collective-permute-start | bytes 3538952 | tf_op jit(solution)/shard_map/ppermute | solution.py:526
  29.2 158.2 %copy-start.5 = (bf16[1,128,1536]{2,1,0:T(8,128)(2,1)S(1)}, bf16[1,128,1536]{2,1,0:T(8,128)(2,1)}, u32[]{:S(2)}) copy-start(bf16[1,128,1536]{2,1,0:T(8,128)(2,1)} %param.9) | copy-start | bytes 1179652
  32.6 156.6 %copy-start.61 = (s32[1,128,2]{1,2,0:T(2,128)S(1)}, s32[1,128,2]{1,2,0:T(2,128)}, u32[]{:S(2)}) copy-start(s32[1,128,2]{1,2,0:T(2,128)} %param.16) | copy-start | bytes 3076
  32.7 158.2 %copy-start.1 = (bf16[1,128,1536]{2,1,0:T(8,128)(2,1)S(1)}, bf16[1,128,1536]{2,1,0:T(8,128)(2,1)}, u32[]{:S(2)}) copy-start(bf16[1,128,1536]{2,1,0:T(8,128)(2,1)} %param.17) | copy-start | bytes 1179652
  278.3 177.7 %reduce-scatter.5.cloned.1.call-start = ((), (), s32[]{:S(2)}) async-start(), calls=%async_computation.3 | async-start | bytes 2949120 | tf_op jit(solution)/shard_map/reduce_scatter | solution.py:634
  301.6 76.9 %copy-start.6 = (pred[128,2,256]{2,0,1:T(32,128)(4,1)S(1)}, pred[128,2,256]{2,0,1:T(32,128)(4,1)}, u32[]{:S(2)}) copy-start(pred[128,2,256]{2,0,1:T(32,128)(4,1)} %get-tuple-element.100) | copy-start | bytes 196612
  415.2 39.5 %collective-permute-start.4 = (bf16[1,15,1536]{2,1,0:T(8,128)(2,1)}, bf16[1,15,1536]{2,1,0:T(8,128)(2,1)}, u32[]{:S(2)}, u32[]{:S(2)}) collective-permute-start(bf16[1,15,1536]{2,1,0:T(8,128)(2,1)} %get-tuple-element.96), channel_id=1, source_target_pairs={{0,1},{1,2},{2,3},{3,4},{4,5},{5,6},{6,7},{7,8},{8,9},{9,10},{10,1... | collective-permute-start | bytes 138248 | tf_op jit(solution)/shard_map/ppermute | solution.py:27
  417.1 37.6 %collective-permute-start.5 = (bf16[1,15,1536]{2,1,0:T(8,128)(2,1)}, bf16[1,15,1536]{2,1,0:T(8,128)(2,1)}, u32[]{:S(2)}, u32[]{:S(2)}) collective-permute-start(bf16[1,15,1536]{2,1,0:T(8,128)(2,1)} %get-tuple-element.97), channel_id=1, source_target_pairs={{1,0},{2,1},{3,2},{4,3},{5,4},{6,5},{7,6},{8,7},{9,8},{10,9},{11,1... | collective-permute-start | bytes 138248 | tf_op jit(solution)/shard_map/ppermute | solution.py:30
  421.5 36.3 %copy-start.3 = (bf16[1,128,1536]{2,1,0:T(8,128)(2,1)S(1)}, bf16[1,128,1536]{2,1,0:T(8,128)(2,1)}, u32[]{:S(2)}) copy-start(bf16[1,128,1536]{2,1,0:T(8,128)(2,1)} %param.17) | copy-start | bytes 1179652
  421.5 36.3 %copy-start.8 = (f32[1536]{0:T(1024)S(1)}, f32[1536]{0:T(1024)}, u32[]{:S(2)}) copy-start(f32[1536]{0:T(1024)} %copy-done.7) | copy-start | bytes 18436
  421.5 36.3 %copy-start.10 = (f32[1536]{0:T(1024)S(1)}, f32[1536]{0:T(1024)}, u32[]{:S(2)}) copy-start(f32[1536]{0:T(1024)} %copy-done.9) | copy-start | bytes 18436
  421.5 36.3 %copy-start.12 = (f32[1536]{0:T(1024)S(1)}, f32[1536]{0:T(1024)}, u32[]{:S(2)}) copy-start(f32[1536]{0:T(1024)} %copy-done.11) | copy-start | bytes 18436
  421.5 36.3 %copy-start.14 = (f32[1536]{0:T(1024)S(1)}, f32[1536]{0:T(1024)}, u32[]{:S(2)}) copy-start(f32[1536]{0:T(1024)} %copy-done.13) | copy-start | bytes 18436
  421.5 36.3 %copy-start.16 = (f32[1536]{0:T(1024)S(1)}, f32[1536]{0:T(1024)}, u32[]{:S(2)}) copy-start(f32[1536]{0:T(1024)} %copy-done.15) | copy-start | bytes 18436
  421.5 36.3 %copy-start.18 = (f32[1536]{0:T(1024)S(1)}, f32[1536]{0:T(1024)}, u32[]{:S(2)}) copy-start(f32[1536]{0:T(1024)} %copy-done.17) | copy-start | bytes 18436
  421.5 36.3 %copy-start.20 = (f32[1536]{0:T(1024)S(1)}, f32[1536]{0:T(1024)}, u32[]{:S(2)}) copy-start(f32[1536]{0:T(1024)} %copy-done.19) | copy-start | bytes 18436
  421.6 36.3 %copy-start.22 = (f32[1536]{0:T(1024)S(1)}, f32[1536]{0:T(1024)}, u32[]{:S(2)}) copy-start(f32[1536]{0:T(1024)} %copy-done.21) | copy-start | bytes 18436
  455.9 16.4 %collective-permute-start.6 = (f32[384,384]{1,0:T(8,128)}, f32[384,384]{1,0:T(8,128)}, u32[]{:S(2)}, u32[]{:S(2)}) collective-permute-start(f32[384,384]{1,0:T(8,128)} %reduce-scatter.3.cloned.1.call-done), channel_id=1, source_target_pairs={{0,6},{1,7},{2,18},{3,19},{4,32},{5,33},{6,52},{7,53},{8,14},{9,15... | collective-permute-start | bytes 1769480 | tf_op jit(solution)/shard_map/ppermute | solution.py:636
  456.0 28.8 %collective-permute-start.7 = (f32[384,384]{1,0:T(8,128)}, f32[384,384]{1,0:T(8,128)S(1)}, u32[]{:S(2)}, u32[]{:S(2)}) collective-permute-start(f32[384,384]{1,0:T(8,128)} %reduce-scatter.5.cloned.1.call-done), channel_id=1, source_target_pairs={{0,6},{1,7},{2,18},{3,19},{4,32},{5,33},{6,52},{7,53},{8,14},{9,15... | collective-permute-start | bytes 1769480 | tf_op jit(solution)/shard_map/ppermute | solution.py:637
  (63 other events, 802.9 us)
Sparse Core Ops, SparseCore 0:
  278.4 30.9 reduce-scatter.2
  312.0 34.0 reduce-scatter.4

commit v3 on v1

v3 whole, which is shorter than its diff:
```python
import functools

import jax
import jax.numpy as jnp
from jax import lax
from jax.experimental import pallas as pl
from jax.experimental.pallas import tpu as pltpu
from jax.sharding import PartitionSpec as P

D = 1536
EXPERTS = 8
TOP = 2
TAPS = 31
EPS = 1e-05
NEAR = 16
MESH = pl.DeviceIdType.MESH
CONTRACT_ROWS = (((0,), (0,)), ((), ()))
CONTRACT_COLS = (((1,), (1,)), ((), ()))
EXACT = lax.Precision.HIGHEST


def extended(block, sides, width):
    for axis, dim in sides:
        count = lax.axis_size(axis)
        forward = [(i, i + 1) for i in range(count - 1)]
        backward = [(target, source) for source, target in forward]
        low = lax.ppermute(
            lax.slice_in_dim(block, block.shape[dim] - width, None, axis=dim), axis, forward
        )
        high = lax.ppermute(lax.slice_in_dim(block, 0, width, axis=dim), axis, backward)
        block = jnp.concatenate([low, block, high], axis=dim)
    return block


def swish_slope(pre):
    sigma = jax.nn.sigmoid(pre)
    return sigma * (1.0 + pre * (1.0 - sigma))


def conv_lags(rimmed, taps, length, reverse):
    total = jnp.zeros((length, rimmed.shape[1]), jnp.float32)
    last = taps.shape[0] - 1
    for lag in range(taps.shape[0]):
        start = last - lag if reverse else lag
        total = total + taps[lag] * rimmed[start : start + length]
    return total


def lag_sums(value, rimmed):
    length = value.shape[0]
    return [jnp.sum(value * rimmed[lag : lag + length], axis=0) for lag in range(TAPS)]


class Groups:
    def __init__(self):
        dp_size, tm_size = lax.axis_size("dp"), lax.axis_size("tm")
        self.dp, self.tm = lax.axis_index("dp"), lax.axis_index("tm")
        self.lines = tm_size // NEAR
        self.near_size, self.far_size = NEAR, dp_size * self.lines
        self.near_rank = self.tm % NEAR
        self.far_rank = self.dp * self.lines + self.tm // NEAR

    def near(self, rank):
        return (self.dp, (self.tm // NEAR) * NEAR + rank)

    def far(self, rank):
        return (rank // self.lines, (rank % self.lines) * NEAR + self.near_rank)

    def enter(self):
        barrier = pltpu.get_barrier_semaphore()

        def greet(size, rank, place):
            def step(k, carry):
                pl.semaphore_signal(
                    barrier, inc=1, device_id=place((rank + k) % size), device_id_type=MESH
                )
                return carry

            lax.fori_loop(1, size, step, 0)

        greet(self.near_size, self.near_rank, self.near)
        greet(self.far_size, self.far_rank, self.far)
        pl.semaphore_wait(barrier, self.near_size + self.far_size - 2)


CORES = 2
LINES = 4
ZEDS = EXPERTS
SPAN = ZEDS * CORES
HALF = ZEDS // 2
TURN = ((3, 1, 0, 2), (1, 3, 2, 0), (0, 2, 1, 3), (2, 0, 3, 1))
SWEEP = (0, 1, 7, 2, 6, 3, 5, 4)


def position(ids):
    return HALF * (ids % 2) + ids // 2


class Place:
    def __init__(self):
        self.dp, tm = lax.axis_index("dp"), lax.axis_index("tm")
        self.core, self.z, self.y = tm % CORES, (tm // CORES) % ZEDS, tm // SPAN

    def at(self, y, z, core):
        return (self.dp, (y % LINES) * SPAN + z * CORES + core)

    def sibling(self):
        return self.at(self.y, self.z, 1 - self.core)

    def line(self, step):
        return self.at(self.y + step + LINES, self.z, self.core)

    def zed(self, z):
        return self.at(self.y, z, self.core)

    def other_dp(self, step):
        dp_size = lax.axis_size("dp")
        return (self.dp + step + dp_size) % dp_size

    def on_dp(self, dp):
        return (dp, self.at(self.y, self.z, self.core)[1])

    def enter(self):
        barrier = pltpu.get_barrier_semaphore()
        peers = [self.sibling(), self.line(1), self.line(-1)]
        peers += [self.on_dp(self.other_dp(step)) for step in range(1, lax.axis_size("dp"))]
        peers += [self.zed((self.z + k) % ZEDS) for k in range(1, ZEDS)]
        for peer in peers:
            pl.semaphore_signal(barrier, inc=1, device_id=peer, device_id_type=MESH)
        pl.semaphore_wait(barrier, len(peers))


def remote(source, target, send_sem, recv_sem, device):
    return pltpu.make_async_remote_copy(
        src_ref=source,
        dst_ref=target,
        send_sem=send_sem,
        recv_sem=recv_sem,
        device_id=device,
        device_id_type=MESH,
    )


class Trade:
    def __init__(self, size, rank, place, source, held, send_sem, recv_sem):
        self.size, self.rank, self.place, self.source = size, rank, place, source
        self.held, self.send_sem, self.recv_sem = held, send_sem, recv_sem

    def copy(self, k):
        peer = (self.rank + k) % self.size
        return remote(
            self.source(peer),
            self.held.at[self.rank],
            self.send_sem.at[k],
            self.recv_sem.at[self.rank],
            self.place(peer),
        )

    def each(self, act):
        def step(k, carry):
            act(k)
            return carry

        lax.fori_loop(1, self.size, step, 0)

    def start(self):
        self.each(lambda k: self.copy(k).start())

    def finish(self):
        def arrival(k):
            origin = (self.rank + k) % self.size
            ref = self.held.at[origin]
            remote(
                ref, ref, self.send_sem.at[k], self.recv_sem.at[origin], self.place(origin)
            ).wait_recv()

        self.each(arrival)
        self.each(lambda k: self.copy(k).wait_send())


class Hop:
    def __init__(self, source, target, stays, device, sems):
        self.stays = stays
        self.local = pltpu.make_async_copy(source, target, sems.at[0])
        self.far = remote(source, target, sems.at[1], sems.at[2], device)

    def start(self):
        pl.when(self.stays)(self.local.start)
        pl.when(jnp.logical_not(self.stays))(self.far.start)

    def finish(self):
        pl.when(self.stays)(self.local.wait)

        @pl.when(jnp.logical_not(self.stays))
        def _():
            self.far.wait_recv()
            self.far.wait_send()


def look(table, index):
    value = table[0]
    for i, entry in enumerate(table):
        value = jnp.where(index == i, entry, value)
    return value


def work_line(place):
    table = [[row[line] for row in TURN].index(turn) for line in range(LINES) for turn in range(HALF)]
    return look(table, place.y * HALF + place.z % HALF)


def home_line(place):
    table = [row.index(turn) for row in TURN for turn in range(HALF)]
    return look(table, place.y * HALF + place.z % HALF)


def moments_merge(held, count):
    means = held[:, 0, :]
    mean = jnp.sum(means, axis=0) / means.shape[0]
    spread = means - mean[None]
    squares = jnp.sum(held[:, 1, :], axis=0) + count * jnp.sum(spread * spread, axis=0)
    return jnp.stack([mean, squares])


def moments_kernel(
    count,
    x_ref,
    w_in_ref,
    w_out_ref,
    o_ref,
    w_in_share,
    w_out_share,
    near_held,
    far_held,
    w_in_mid,
    w_out_mid,
    near_send,
    near_recv,
    far_send,
    far_recv,
    y_sems,
    z_sems,
):
    groups, place = Groups(), Place()
    near_held[groups.near_rank] = x_ref[...]
    line = work_line(place)
    zed = place.z // HALF * HALF + home_line(place)
    y_hops, z_hops = [], []
    cargo = ((w_in_ref, w_in_mid, w_in_share), (w_out_ref, w_out_mid, w_out_share))
    for i, (source, mid, share) in enumerate(cargo):
        depth = share.shape[0]
        mine = source.at[pl.ds(pl.multiple_of(place.dp * depth, depth), depth)]
        y_hops.append(Hop(mine, mid, line == place.y, place.at(line, place.z, place.core), y_sems.at[i]))
        z_hops.append(Hop(mid, share, zed == place.z, place.zed(zed), z_sems.at[i]))
    groups.enter()
    mine = near_held.at[groups.near_rank]
    near = Trade(
        groups.near_size, groups.near_rank, groups.near, lambda p: mine, near_held, near_send, near_recv
    )
    near.start()
    for hop in y_hops:
        hop.start()
    near.finish()
    far_held[groups.far_rank] = moments_merge(near_held[...], float(count))
    mine_far = far_held.at[groups.far_rank]
    far = Trade(
        groups.far_size, groups.far_rank, groups.far, lambda p: mine_far, far_held, far_send, far_recv
    )
    far.start()
    for y_hop, z_hop in zip(y_hops, z_hops):
        y_hop.finish()
        z_hop.start()
    far.finish()
    o_ref[...] = moments_merge(far_held[...], float(count * groups.near_size))
    for hop in z_hops:
        hop.finish()


def moments_and_weights(x, count, w_in, w_out, collective_id):
    dp_size = lax.axis_size("dp")
    far_size = dp_size * (lax.axis_size("tm") // NEAR)
    shares = [
        jax.ShapeDtypeStruct((w.shape[0] // dp_size, w.shape[1]), w.dtype) for w in (w_in, w_out)
    ]
    dma = pltpu.SemaphoreType.DMA
    return pl.pallas_call(
        functools.partial(moments_kernel, count),
        out_shape=(jax.ShapeDtypeStruct(x.shape, x.dtype), *shares),
        in_specs=[pl.BlockSpec(memory_space=pltpu.VMEM)] + [pl.BlockSpec(memory_space=pl.ANY)] * 2,
        out_specs=[pl.BlockSpec(memory_space=pltpu.VMEM)] + [pl.BlockSpec(memory_space=pl.ANY)] * 2,
        scratch_shapes=[
            pltpu.VMEM((NEAR,) + x.shape, x.dtype),
            pltpu.VMEM((far_size,) + x.shape, x.dtype),
            *[pltpu.VMEM(share.shape, share.dtype) for share in shares],
            dma((NEAR,)),
            dma((NEAR,)),
            dma((far_size,)),
            dma((far_size,)),
            dma((2, 3)),
            dma((2, 3)),
        ],
        compiler_params=pltpu.CompilerParams(
            collective_id=collective_id, has_side_effects=True, vmem_limit_bytes=16 << 20
        ),
    )(x, w_in, w_out)


def sums_kernel(
    x_ref,
    g0_ref,
    g1_ref,
    o_ref,
    h0_ref,
    h1_ref,
    near_held,
    far_held,
    mids,
    near_send,
    near_recv,
    far_send,
    far_recv,
    out_send,
    out_recv,
    y_sems,
    z_sems,
):
    groups, place = Groups(), Place()
    rank = groups.near_rank
    near_held[rank] = x_ref[rank]
    half, line = place.z // HALF * HALF, place.z % HALF
    turn = look([entry for row in TURN for entry in row], place.y * HALF + line)
    home = home_line(place)
    y_hops, z_hops = [], []
    for i, (source, target) in enumerate(((g0_ref, h0_ref), (g1_ref, h1_ref))):
        z_hops.append(
            Hop(source, mids.at[i], half + turn == place.z, place.zed(half + turn), z_sems.at[i])
        )
        y_hops.append(
            Hop(mids.at[i], target, home == place.y, place.at(home, place.z, place.core), y_sems.at[i])
        )
    groups.enter()
    near = Trade(
        groups.near_size, rank, groups.near, lambda p: x_ref.at[p], near_held, near_send, near_recv
    )
    near.start()
    for hop in z_hops:
        hop.start()
    near.finish()
    far_held[groups.far_rank] = jnp.sum(near_held[...], axis=0)
    mine = far_held.at[groups.far_rank]
    far = Trade(
        groups.far_size, groups.far_rank, groups.far, lambda p: mine, far_held, far_send, far_recv
    )
    far.start()
    for y_hop, z_hop in zip(y_hops, z_hops):
        z_hop.finish()
        y_hop.start()
    far.finish()
    o_ref[rank] = jnp.sum(far_held[...], axis=0)
    done = o_ref.at[rank]
    out = Trade(groups.near_size, rank, groups.near, lambda p: done, o_ref, out_send, out_recv)
    out.start()
    out.finish()
    for hop in y_hops:
        hop.finish()


def sums_and_gradients(x, g0, g1, collective_id):
    far_size = lax.axis_size("dp") * (lax.axis_size("tm") // NEAR)
    dma = pltpu.SemaphoreType.DMA
    gradient = jax.ShapeDtypeStruct(g0.shape, g0.dtype)
    return pl.pallas_call(
        sums_kernel,
        out_shape=(jax.ShapeDtypeStruct(x.shape, x.dtype), gradient, gradient),
        in_specs=[pl.BlockSpec(memory_space=pltpu.VMEM)] + [pl.BlockSpec(memory_space=pl.ANY)] * 2,
        out_specs=[pl.BlockSpec(memory_space=pltpu.VMEM)] + [pl.BlockSpec(memory_space=pl.ANY)] * 2,
        scratch_shapes=[
            pltpu.VMEM(x.shape, x.dtype),
            pltpu.VMEM((far_size,) + x.shape[1:], x.dtype),
            pltpu.VMEM((2,) + g0.shape, g0.dtype),
            dma((NEAR,)),
            dma((NEAR,)),
            dma((far_size,)),
            dma((far_size,)),
            dma((NEAR,)),
            dma((NEAR,)),
            dma((2, 3)),
            dma((2, 3)),
        ],
        compiler_params=pltpu.CompilerParams(
            collective_id=collective_id, has_side_effects=True, vmem_limit_bytes=16 << 20
        ),
    )(x, g0, g1)


CHUNKS = ((2, 0, 1, None), (2, 1, -1, None), (1, 1, 1, None), (3, 0, -1, None), (1, 0, 1, 0), (3, 1, -1, 1), (0, 0, 0, None), (0, 1, 0, None))
LEAVING = 6
LAG = 4
WIDE = 512


def experts_kernel(shares, x_ref, u_ref, in_share, out_share, *refs):
    o_refs, g_refs, refs = refs[:2], refs[2:4], refs[4:]
    (
        rows_x,
        rows_u,
        w_in,
        w_out,
        pre_held,
        hid_held,
        dpre_held,
        results,
        pair_held,
        line_held,
        gradient,
        parting,
        parts,
        weight_own,
        weight_send,
        weight_recv,
        part_send,
        part_recv,
        own_sem,
        zin_send,
        zin_recv,
        share_send,
        share_recv,
        yin_send,
        yin_recv,
        pair_send,
        pair_recv,
        y_send,
        y_recv,
        z_send,
        z_recv,
    ) = refs
    place = Place()
    y, z, core = place.y, place.z, place.core
    arrays = ((x_ref, rows_x), (u_ref, rows_u))
    waits = []

    weights = ((in_share, w_in), (out_share, w_out))

    def weight_own_copy(i):
        share, held = weights[i]
        return pltpu.make_async_copy(share, held.at[place.dp], weight_own.at[i])

    def weight_copy(i, step):
        share, held = weights[i]
        return remote(
            share,
            held.at[place.dp],
            weight_send.at[i, step],
            weight_recv.at[i, step],
            place.on_dp(place.other_dp(step)),
        )

    def weights_arrive():
        for i, (_, held) in enumerate(weights):
            weight_own_copy(i).wait()
            for step in range(1, shares):
                ref = held.at[place.other_dp(-step)]
                remote(
                    ref, ref, weight_send.at[i, step], weight_recv.at[i, step], place.sibling()
                ).wait_recv()


    def zin_copy(a, k):
        source, rows = arrays[a]
        target = (z + k) % ZEDS
        return remote(
            source.at[target], rows.at[core, y, z], zin_send.at[a, k], zin_recv.at[a, k], place.zed(target)
        )

    def own_copy(a):
        source, rows = arrays[a]
        return pltpu.make_async_copy(source.at[z], rows.at[core, y, z], own_sem.at[a])

    def block(a, from_core, step, k):
        return arrays[a][1].at[from_core, (y + step + LINES) % LINES, (z - k + ZEDS) % ZEDS]

    def pass_on(a, step, k, send_sem, recv_sem, device):
        ref = block(a, core, step, k)
        copy = remote(ref, ref, send_sem, recv_sem, device)
        copy.start()
        waits.append(copy)

    def arrived(a, from_core, step, k, send_sem, recv_sem):
        ref = block(a, from_core, step, k)
        remote(ref, ref, send_sem, recv_sem, place.sibling()).wait_recv()

    def share(a, step, k):
        index = step % LINES * ZEDS + k
        pass_on(a, step, k, share_send.at[a, index], share_recv.at[a, index], place.sibling())

    def spread(a, m):
        if m < ZEDS:
            k = SWEEP[m]
            if k == 0:
                own_copy(a).wait()
            else:
                arrived(a, core, 0, k, zin_send.at[a, k], zin_recv.at[a, k])
            for way, step in ((0, 1), (1, -1)):
                pass_on(a, 0, k, yin_send.at[a, way, k], yin_recv.at[a, way, k], place.line(step))
            share(a, 0, k)
        if 0 <= m - LAG // 2 < ZEDS:
            i = m - LAG // 2
            k = SWEEP[i]
            for way, step in ((0, 1), (1, -1)):
                arrived(a, core, -step, k, yin_send.at[a, way, k], yin_recv.at[a, way, k])
                if i % 2 == way:
                    pass_on(a, -step, k, yin_send.at[a, 2, k], yin_recv.at[a, 2, k], place.line(step))
                share(a, -step, k)
        if 0 <= m - LAG < ZEDS:
            k = SWEEP[m - LAG]
            arrived(a, core, 2, k, yin_send.at[a, 2, k], yin_recv.at[a, 2, k])
            share(a, 2, k)

    def all_shared(a):
        for step in range(LINES):
            for k in range(ZEDS):
                index = step * ZEDS + k
                arrived(a, 1 - core, step, k, share_send.at[a, index], share_recv.at[a, index])


    def chunk_of(ref, i):
        step, half = CHUNKS[i][:2]
        return ref.at[:, (y + step) % LINES, pl.ds(half * HALF, HALF)]

    def flat(value):
        return value.reshape(-1, value.shape[-1])

    def keep(ref, i, value):
        target = chunk_of(ref, i)
        target[...] = value.astype(ref.dtype).reshape(target.shape)

    def put(a, i, columns, value):
        target = results.at[a, i, :, :, :, pl.ds(columns, WIDE)]
        target[...] = value.astype(results.dtype).reshape(target.shape)

    w_in_rows, w_out_rows = w_in.shape[1] * shares, w_out.shape[1] * shares

    def forward(i):
        pre = jnp.dot(
            flat(chunk_of(rows_x, i)[...]),
            w_in[...].reshape(w_in_rows, -1),
            preferred_element_type=jnp.float32,
        )
        keep(pre_held, i, pre)
        hidden = (pre * jax.nn.sigmoid(pre)).astype(jnp.bfloat16)
        keep(hid_held, i, hidden)
        for columns in range(0, D, WIDE):
            weights = w_out[:, :, pl.ds(columns, WIDE)].reshape(w_out_rows, WIDE)
            put(0, i, columns, jnp.dot(hidden, weights, preferred_element_type=jnp.float32))
        pair_copy(0, i).start()

    def backward(i):
        dhidden = lax.dot_general(
            flat(chunk_of(rows_u, i)[...]),
            w_out[...].reshape(w_out_rows, -1),
            CONTRACT_COLS,
            preferred_element_type=jnp.float32,
        )
        dpre = (dhidden * swish_slope(flat(chunk_of(pre_held, i)[...]))).astype(jnp.bfloat16)
        keep(dpre_held, i, dpre)
        weights_all = w_in[...].reshape(w_in_rows, -1)
        for columns in range(0, D, WIDE):
            weights = weights_all[columns : columns + WIDE]
            put(
                1,
                i,
                columns,
                lax.dot_general(dpre, weights, CONTRACT_COLS, preferred_element_type=jnp.float32),
            )
        pair_copy(1, i).start()

    def part_copy(i, step):
        target = place.other_dp(step)
        return remote(
            parting.at[i, target],
            parts.at[i, place.dp],
            part_send.at[i, step],
            part_recv.at[i, step],
            place.on_dp(target),
        )

    def weight_gradient(i, left, right):
        def line(step, carry):
            for columns in range(0, D, WIDE):
                value = lax.dot_general(
                    flat(left[:, step]),
                    flat(right[:, step, :, :, pl.ds(columns, WIDE)]),
                    CONTRACT_ROWS,
                    preferred_element_type=jnp.float32,
                )
                gradient[:, pl.ds(columns, WIDE)] += value
            return carry

        gradient[...] = jnp.zeros_like(gradient)
        lax.fori_loop(0, LINES, line, 0)
        width = D // shares
        for part in range(shares):
            parting[i, part] = gradient[:, part * width : (part + 1) * width].astype(parting.dtype)
        for step in range(1, shares):
            part_copy(i, step).start()

    def gather_gradient(i):
        total = parting[i, place.dp].astype(jnp.float32)
        for step in range(1, shares):
            origin = place.other_dp(-step)
            ref = parts.at[i, origin]
            remote(
                ref, ref, part_send.at[i, step], part_recv.at[i, step], place.sibling()
            ).wait_recv()
            total = total + parts[i, origin].astype(jnp.float32)
        g_refs[i][...] = total.astype(g_refs[i].dtype)


    def pair_copy(a, i):
        return remote(
            results.at[a, i, 1 - core],
            pair_held.at[a, i],
            pair_send.at[a, i],
            pair_recv.at[a, i],
            place.sibling(),
        )

    def y_copy(a, i):
        return remote(
            results.at[a, i, core],
            line_held.at[a, i],
            y_send.at[a, i],
            y_recv.at[a, i],
            place.line(CHUNKS[i][2]),
        )

    def z_copy(a, target):
        source = results.at[a, LEAVING + target // HALF, core, target % HALF]
        return remote(source, o_refs[a].at[z], z_send.at[a, target], z_recv.at[a, z], place.zed(target))

    def settle(a, i, extras):
        pair_copy(a, i).wait_recv()
        for extra in extras:
            y_copy(a, extra).wait_recv()

        def one(j, carry):
            value = results[a, i, core, j].astype(jnp.float32) + pair_held[a, i, j].astype(jnp.float32)
            for extra in extras:
                value = value + line_held[a, extra, j].astype(jnp.float32)
            results[a, i, core, j] = value.astype(results.dtype)
            return carry

        lax.fori_loop(0, HALF, one, 0)

    def leave(a, i):
        extra = CHUNKS[i][3]
        settle(a, i, () if extra is None else (extra,))
        y_copy(a, i).start()

    def finish(a, half):
        settle(a, LEAVING + half, (4, 3) if half == 0 else (2, 5))
        for j in range(HALF):
            target = half * HALF + j

            @pl.when(target != z)
            def _():
                z_copy(a, target).start()

            @pl.when(target == z)
            def _():
                o_refs[a][target] = results[a, LEAVING + half, core, j]

    place.enter()
    for a in range(2):
        own_copy(a).start()
        for k in SWEEP[1:]:
            zin_copy(a, k).start()
    for i in range(2):
        weight_own_copy(i).start()
        for step in range(1, shares):
            weight_copy(i, step).start()
    for m in range(ZEDS + LAG):
        spread(0, m)
    all_shared(0)
    weights_arrive()
    for m in range(ZEDS + LAG):
        spread(1, m)
        if m < len(CHUNKS):
            forward(m)
        if 1 <= m <= 4:
            leave(0, m - 1)
    for i in (4, 5):
        leave(0, i)
    all_shared(1)
    for i in range(len(CHUNKS)):
        backward(i)
        if 1 <= i <= 4:
            leave(1, i - 1)
        if i == 6:
            finish(0, 0)
        if i == 7:
            finish(0, 1)
    weight_gradient(1, hid_held, rows_u)
    for i in (4, 5):
        leave(1, i)
    weight_gradient(0, dpre_held, rows_x)
    for half in range(2):
        finish(1, half)
    for i in (1, 0):
        gather_gradient(i)
    for a in range(2):
        for k in range(1, ZEDS):
            other = (z + k) % ZEDS
            ref = o_refs[a].at[other]
            remote(ref, ref, z_send.at[a, other], z_recv.at[a, other], place.zed(other)).wait_recv()
    for a in range(2):
        for k in SWEEP[1:]:
            zin_copy(a, k).wait_send()
        for i in range(len(CHUNKS)):
            pair_copy(a, i).wait_send()
        for i in range(LEAVING):
            y_copy(a, i).wait_send()
        for k in range(1, ZEDS):
            z_copy(a, (z + k) % ZEDS).wait_send()
    for copy in waits:
        copy.wait_send()
    for i in range(2):
        for step in range(1, shares):
            weight_copy(i, step).wait_send()
            part_copy(i, step).wait_send()


def experts(x, u, in_share, out_share, collective_id):
    shares = lax.axis_size("dp")
    hidden = in_share.shape[1]
    tile = x.shape[1:]
    lines = (CORES, LINES, ZEDS)
    chunk = (HALF,) + tile
    bf16, f32, dma = jnp.bfloat16, jnp.float32, pltpu.SemaphoreType.DMA
    out = jax.ShapeDtypeStruct(x.shape, bf16)
    gradient = jax.ShapeDtypeStruct((hidden, D // shares), bf16)
    held = lines + (tile[0], hidden)
    sems = [
        (2,),
        (2, shares),
        (2, shares),
        (2, shares),
        (2, shares),
        (2,),
        (2, ZEDS),
        (2, ZEDS),
        (2, LINES * ZEDS),
        (2, LINES * ZEDS),
        (2, 3, ZEDS),
        (2, 3, ZEDS),
        (2, len(CHUNKS)),
        (2, len(CHUNKS)),
        (2, LEAVING),
        (2, LEAVING),
        (2, ZEDS),
        (2, ZEDS),
    ]
    return pl.pallas_call(
        functools.partial(experts_kernel, shares),
        out_shape=(out, out, gradient, gradient),
        in_specs=[pl.BlockSpec(memory_space=pl.ANY)] * 4,
        out_specs=[pl.BlockSpec(memory_space=pltpu.VMEM)] * 4,
        scratch_shapes=[
            pltpu.VMEM(lines + tile, bf16),
            pltpu.VMEM(lines + tile, bf16),
            pltpu.VMEM((shares,) + in_share.shape, bf16),
            pltpu.VMEM((shares,) + out_share.shape, bf16),
            pltpu.VMEM(held, f32),
            pltpu.VMEM(held, bf16),
            pltpu.VMEM(held, bf16),
            pltpu.VMEM((2, len(CHUNKS), CORES) + chunk, bf16),
            pltpu.VMEM((2, len(CHUNKS)) + chunk, bf16),
            pltpu.VMEM((2, LEAVING) + chunk, bf16),
            pltpu.VMEM((hidden, D), f32),
            pltpu.VMEM((2, shares) + gradient.shape, bf16),
            pltpu.VMEM((2, shares) + gradient.shape, bf16),
        ]
        + [dma(shape) for shape in sems],
        compiler_params=pltpu.CompilerParams(
            collective_id=collective_id, has_side_effects=True, vmem_limit_bytes=58 << 20
        ),
    )(x, u, in_share, out_share)


def body(
    frames,
    taps,
    batchnorm_gain_scale,
    batchnorm_shift_bias,
    w_router,
    w_in,
    w_out,
    choices,
    cotangent,
):
    length = frames.shape[1]
    half = TAPS // 2
    element_count = lax.axis_size("dp") * lax.axis_size("tm") * length
    capacity = length * TOP // EXPERTS
    signal = frames[0].astype(jnp.float32)
    rimmed = extended(frames, (("tm", 1),), half)[0].astype(jnp.float32)
    conv = conv_lags(rimmed, taps, length, False)
    local_mean = jnp.sum(conv, axis=0) / length
    local_spread = conv - local_mean
    moments, w_in_share, w_out_share = moments_and_weights(
        jnp.stack([local_mean, jnp.sum(local_spread * local_spread, axis=0)]), length, w_in, w_out, 0
    )
    mean, variance = moments[0], moments[1] / element_count
    centered_values = conv - mean
    inverse_deviation = lax.rsqrt(variance + EPS)
    normalized_input = centered_values * inverse_deviation
    before_activation = normalized_input * batchnorm_gain_scale + batchnorm_shift_bias
    resid = signal + jax.nn.silu(before_activation)
    lcent = resid - jnp.mean(resid, axis=-1, keepdims=True)
    lrstd = lax.rsqrt(jnp.mean(lcent * lcent, axis=-1, keepdims=True) + EPS)
    vhat = lcent * lrstd
    normed = vhat.astype(jnp.bfloat16)
    logits = jnp.dot(normed, w_router, preferred_element_type=jnp.float32)
    ids = choices[0]
    onehot = (ids[:, :, None] == jnp.arange(EXPERTS, dtype=jnp.int32)[None, None, :]).astype(
        jnp.float32
    )
    picked = jnp.sum(onehot * logits[:, None, :], axis=-1)
    first = jax.nn.sigmoid(picked[:, 0] - picked[:, 1])
    gates = jnp.stack([first, 1.0 - first], axis=1)
    flat_ids = ids.reshape(-1)
    expert_hot = (flat_ids[:, None] == jnp.arange(EXPERTS, dtype=jnp.int32)[None, :]).astype(
        jnp.int32
    )
    slots = jnp.sum((jnp.cumsum(expert_hot, axis=0) - 1) * expert_hot, axis=1)
    places = (position(flat_ids) * capacity + slots).reshape(length, TOP)
    place_hot = places[:, :, None] == jnp.arange(EXPERTS * capacity, dtype=jnp.int32)[None, None, :]
    place_any = jnp.any(place_hot, axis=1).astype(jnp.bfloat16)
    place_hot = place_hot.astype(jnp.float32)
    gate_rows = jnp.sum(place_hot * gates[:, :, None], axis=(0, 1))

    def bucketed(rows):
        return lax.dot_general(place_any, rows, CONTRACT_ROWS, preferred_element_type=jnp.float32)

    buffer = bucketed(normed).astype(jnp.bfloat16).reshape(EXPERTS, capacity, D)
    sent_buffer = (gate_rows[:, None] * bucketed(cotangent[0])).astype(jnp.bfloat16)
    sent_buffer = sent_buffer.reshape(EXPERTS, capacity, D)
    combined, back, grad_in_local, grad_out_local = experts(
        buffer, sent_buffer, w_in_share, w_out_share, 1
    )
    combined = combined.reshape(EXPERTS * capacity, D).astype(jnp.float32)
    back = back.reshape(EXPERTS * capacity, D).astype(jnp.float32)
    expert_out = [
        jnp.dot(place_hot[:, k], combined, precision=EXACT) for k in range(TOP)
    ]
    mixed = (resid + sum(gates[:, k, None] * expert_out[k] for k in range(TOP))).astype(jnp.bfloat16)
    upstream = cotangent[0].astype(jnp.float32)
    dgate = [jnp.sum(upstream * expert_out[k], axis=-1) for k in range(TOP)]
    dpick = (dgate[0] - dgate[1]) * first * (1.0 - first)
    dlogits = (onehot[:, 0] - onehot[:, 1]) * dpick[:, None]
    dnormed = jnp.dot(dlogits, w_router.astype(jnp.float32).T, precision=EXACT)
    dnormed = dnormed + jnp.dot(jnp.sum(place_hot, axis=1), back, precision=EXACT)
    dmean = jnp.mean(dnormed, axis=-1, keepdims=True)
    dproj = jnp.mean(dnormed * vhat, axis=-1, keepdims=True)
    dresid = upstream + lrstd * (dnormed - dmean - vhat * dproj)
    normalized_gradient = dresid * swish_slope(before_activation) * batchnorm_gain_scale
    signal_lags = [jnp.sum(rimmed[lag : lag + length], axis=0) for lag in range(TAPS)]
    normalized_lags = lag_sums(normalized_input, rimmed)
    gradient_lags = lag_sums(normalized_gradient, rimmed)
    moment_rows = [
        jnp.sum(normalized_gradient, axis=0),
        jnp.sum(normalized_gradient * normalized_input, axis=0),
    ]
    lag_rows = jnp.stack(gradient_lags + signal_lags + normalized_lags)
    per_rank = -(-lag_rows.shape[0] // NEAR)
    lag_rows = jnp.pad(lag_rows, ((0, NEAR * per_rank - lag_rows.shape[0]), (0, 0)))
    to_sum = jnp.concatenate(
        [
            lag_rows.reshape(NEAR, per_rank, D),
            jnp.broadcast_to(jnp.stack(moment_rows)[None], (NEAR, 2, D)),
        ],
        axis=1,
    )
    rims = extended(jnp.stack([normalized_gradient, normalized_input]), (("tm", 1),), half)
    summed, grad_w_in, grad_w_out = sums_and_gradients(to_sum, grad_in_local, grad_out_local, 2)
    first_mean, second_mean = (summed[0, per_rank + i] / element_count for i in range(2))
    lag_rows = summed[:, :per_rank].reshape(NEAR * per_rank, D)
    grad_taps = inverse_deviation * (
        lag_rows[:TAPS]
        - first_mean * lag_rows[TAPS : 2 * TAPS]
        - second_mean * lag_rows[2 * TAPS : 3 * TAPS]
    )
    convolution_gradient = (
        inverse_deviation * (rims[0] - first_mean - rims[1] * second_mean)
    ).astype(jnp.bfloat16)
    at = lax.axis_index("tm") * length - half + jnp.arange(length + 2 * half)
    inside = (at >= 0) & (at < lax.axis_size("tm") * length)
    grad_rimmed = jnp.where(inside[:, None], convolution_gradient, 0).astype(jnp.float32)
    grad_frames = (dresid + conv_lags(grad_rimmed, taps, length, True)).astype(jnp.bfloat16)
    grad_w_in, grad_w_out = grad_w_in.T.astype(jnp.float32), grad_w_out.astype(jnp.float32)
    return (mixed[None], grad_frames[None], grad_taps, grad_w_in, grad_w_out)


def solution(mesh):
    return jax.shard_map(
        body,
        mesh=mesh,
        in_specs=(
            P("dp", "tm", None),
            P(),
            P(),
            P(),
            P(),
            P(None, "tm"),
            P("tm", None),
            P("dp", "tm", None),
            P("dp", "tm", None),
        ),
        out_specs=(P("dp", "tm", None), P("dp", "tm", None), P(), P("dp", "tm"), P("tm", "dp")),
        check_vma=False,
    )
```

time: 746 us -> 316 us (0.42)
  the two profiles are of different devices: /device:TPU:1 before, /device:TPU:57 now
where the time goes in v3:
time: 316 us; the launch traced here: 311 us
  Pallas kernels  245 us (78%)
  other arithmetic  29.3 us (9%)
  local copies, waits for them, and re-layouts  13.7 us (4%)
  starting transfers between devices  12.8 us (4%)
  matrix products  6.76 us (2%)
    pallas_call x1, Pallas kernels, experts(): pl.pallas_call(functools.partial(experts_kernel, shares), out_shape=(out,...  142 us
    pallas_call x1, Pallas kernels, sums_and_gradients(): pl.pallas_call(sums_kernel, out_shape=(jax.ShapeDtypeStruct(x.shape, x.dt...  72.7 us
    pallas_call x1, Pallas kernels, moments_and_weights(): pl.pallas_call(functools.partial(moments_kernel, count), out_shape=(jax.S...  31.2 us
    ppermute x2, starting transfers between devices, extended(): lax.ppermute(lax.slice_in_dim(block, block.shape[dim] - width, None, axis...  8.96 us
    reduce_sum x4, other arithmetic, lag_sums(): jnp.sum(value * rimmed[lag:lag + length], axis=0)  8.68 us
  transfers between devices with their start and end apart: 4, of which 1 were waited for; matrix products, arithmetic and copies ran while one was open for 4% of the time, Pallas kernels for 0%

profile of v3, /device:TPU:57, one launch (start us, length us, event | category | flops | bytes accessed | tf_op | source)
XLA Modules:
  0.0 311.5 jit_solution(7093321619096090743)
XLA Ops:
  1.5 4.1 %collective-permute-start = (bf16[1,15,1536]{2,1,0:T(8,128)(2,1)S(1)}, bf16[1,15,1536]{2,1,0:T(8,128)(2,1)S(1)}, u32[]{:S(2)}, u32[]{:S(2)}) collective-permute-start(bf16[1,15,1536]{2,1,0:T(8,128)(2,1)S(1)} %get-tuple-element.192), channel_id=1, source_target_pairs={{0,1},{1,2},{2,3},{3,4},{4,5},{5,6},{6,7},{7,8},{8,9},{9,10},{10,1... | collective-permute-start | bytes 138248 | tf_op jit(solution)/shard_map/ppermute | solution.py:27
  5.6 1.9 collective-permute-start.1
  7.5 2.1 slice_reduce_fusion.63
  9.7 1.5 slice_reduce_fusion.62
  16.8 3.1 fusion.161
  20.2 31.2 %shard_map.128 = (f32[2,1536]{1,0:T(2,128)S(1)}, bf16[384,384]{1,0:T(8,128)(2,1)S(1)}, bf16[96,1536]{1,0:T(8,128)(2,1)S(1)}) custom-call(f32[2,1536]{1,0:T(2,128)S(1)} %pad_maximum_fusion.4.x_ref, bf16[1536,384]{1,0:T(8,128)(2,1)S(1)} %copy-done.1, bf16[384,1536]{1,0:T(8,128)(2,1)S(1)} %copy-done.2), custom_call_target="tpu_custom_call" | custom-call | tf_op jit(solution)/shard_map/pallas_call | solution.py:286
  52.8 1.3 convolution_convert_fusion
  54.1 1.3 fusion
  55.4 141.7 %shard_map.129 = (bf16[8,32,1536]{2,1,0:T(8,128)(2,1)}, bf16[8,32,1536]{2,1,0:T(8,128)(2,1)}, bf16[384,384]{1,0:T(8,128)(2,1)}, bf16[384,384]{1,0:T(8,128)(2,1)}) custom-call(bf16[8,32,1536]{2,1,0:T(8,128)(2,1)} %bitcast.497, bf16[8,32,1536]{2,1,0:T(8,128)(2,1)} %bitcast.498, bf16[384,384]{1,0:T(8,128)(2,1)} %copy-done.5, bf16[96,1536]{1,0:T(8,128)(2,1)} %copy-done.6), custom_call_target="tpu_custom_call" | custom-call | tf_op jit(solution)/shard_map/pallas_call | solution.py:763
  197.1 1.5 fusion.142
  198.6 1.3 fusion.7
  201.2 3.2 %fusion.41 = (f32[1536]{0:T(1024)S(1)}, f32[1536]{0:T(1024)S(1)}, f32[1536]{0:T(1024)S(1)}, f32[1536]{0:T(1024)S(1)}, f32[1536]{0:T(1024)S(1)}, /*index=5*/f32[1...) fusion(f32[1,158,1536]{2,1,0:T(8,128)S(1)} %maximum_convert_fus, ...), kind=kLoop, calls=%fused_computation.86 | loop fusion | flops 11179008 | bytes 17831936 | tf_op jit(solution)/shard_map/reduce_sum | solution.py:51
  204.4 1.8 fusion.45
  206.2 1.2 fusion.95
  207.4 2.5 fusion.42
  209.9 1.6 slice_reduce_fusion
  215.5 1.2 reshape.212
  217.0 72.7 %shard_map.130 = (f32[16,8,1536]{2,1,0:T(8,128)S(1)}, bf16[384,384]{1,0:T(8,128)(2,1)S(1)}, bf16[384,384]{1,0:T(8,128)(2,1)S(1)}) custom-call(f32[16,8,1536]{2,1,0:T(8,128)S(1)} %pad_maximum_fusion.1.x_ref, bf16[384,384]{1,0:T(8,128)(2,1)S(1)} %copy-done.3, bf16[384,384]{1,0:T(8,128)(2,1)S(1)} %copy-done.4), custom_call_target="tpu_custom_call" | custom-call | tf_op jit(solution)/shard_map/pallas_call | solution.py:372
  290.6 1.9 pad_maximum_fusion.3
  292.5 4.8 %collective-permute-start.2 = (f32[2,15,1536]{2,1,0:T(8,128)}, f32[2,15,1536]{2,1,0:T(8,128)}, u32[]{:S(2)}, u32[]{:S(2)}) collective-permute-start(f32[2,15,1536]{2,1,0:T(8,128)} %get-tuple-element.188), channel_id=1, source_target_pairs={{0,1},{1,2},{2,3},{3,4},{4,5},{5,6},{6,7},{7,8},{8,9},{9,10},{10,1... | collective-permute-start | bytes 552968 | tf_op jit(solution)/shard_map/ppermute | solution.py:27
  297.3 1.9 collective-permute-start.3
  300.9 2.1 copy.34
  304.6 1.3 pad_maximum_fusion
  307.2 4.0 %fusion.137 = bf16[1,128,1536]{2,1,0:T(8,128)(2,1)} fusion(f32[158,1536]{1,0:T(8,128)S(1)} %fusion.134, f32[1536]{0:T(1024)S(1)} %copy-done.36, f32[1536]{0:T(1024)S(1)} %copy-done.38, f32[1536]{0:T(1024)S(1)} %get-tuple-element.147, f32[1536]{0:T(1024)S(1)} %get-tuple-element.148, f32[1536]{0:T(1024)S(1)} %get-tuple-element.149, ...), kind=kLoop, calls=%fused_computation.315 | loop fusion | flops 13959168 | bytes 26931200 | tf_op jit(solution)/shard_map/broadcast_in_dim | solution.py:901
  (251 shorter events, 17.7 us)
Async XLA Ops:
  0.6 51.7 %copy-start = (bf16[1536,8]{0,1:T(8,128)(2,1)S(1)}, bf16[1536,8]{0,1:T(8,128)(2,1)}, u32[]{:S(2)}) copy-start(bf16[1536,8]{0,1:T(8,128)(2,1)} %param.13) | copy-start | bytes 73732
  1.5 14.1 %collective-permute-start = (bf16[1,15,1536]{2,1,0:T(8,128)(2,1)S(1)}, bf16[1,15,1536]{2,1,0:T(8,128)(2,1)S(1)}, u32[]{:S(2)}, u32[]{:S(2)}) collective-permute-start(bf16[1,15,1536]{2,1,0:T(8,128)(2,1)S(1)} %get-tuple-element.192), channel_id=1, source_target_pairs={{0,1},{1,2},{2,3},{3,4},{4,5},{5,6},{6,7},{7,8},{8,9},{9,10},{10,1... | collective-permute-start | bytes 138248 | tf_op jit(solution)/shard_map/ppermute | solution.py:27
  5.6 10.0 %collective-permute-start.1 = (bf16[1,15,1536]{2,1,0:T(8,128)(2,1)S(1)}, bf16[1,15,1536]{2,1,0:T(8,128)(2,1)S(1)}, u32[]{:S(2)}, u32[]{:S(2)}) collective-permute-start(bf16[1,15,1536]{2,1,0:T(8,128)(2,1)S(1)} %get-tuple-element.193), channel_id=1, source_target_pairs={{1,0},{2,1},{3,2},{4,3},{5,4},{6,5},{7,6},{8,7},{9,8},{10,9},{11,1... | collective-permute-start | bytes 138248 | tf_op jit(solution)/shard_map/ppermute | solution.py:30
  11.2 8.7 %copy-start.17 = (f32[1536]{0:T(1024)}, f32[1536]{0:T(1024)S(1)}, u32[]{:S(2)}) copy-start(f32[1536]{0:T(1024)S(1)} %get-tuple-element.166) | copy-start | bytes 18436
  11.2 8.7 %copy-start.19 = (f32[1536]{0:T(1024)}, f32[1536]{0:T(1024)S(1)}, u32[]{:S(2)}) copy-start(f32[1536]{0:T(1024)S(1)} %get-tuple-element.167) | copy-start | bytes 18436
  11.2 8.7 %copy-start.21 = (f32[1536]{0:T(1024)}, f32[1536]{0:T(1024)S(1)}, u32[]{:S(2)}) copy-start(f32[1536]{0:T(1024)S(1)} %get-tuple-element.168) | copy-start | bytes 18436
  11.2 8.7 %copy-start.23 = (f32[1536]{0:T(1024)}, f32[1536]{0:T(1024)S(1)}, u32[]{:S(2)}) copy-start(f32[1536]{0:T(1024)S(1)} %get-tuple-element.169) | copy-start | bytes 18436
  11.2 8.7 %copy-start.25 = (f32[1536]{0:T(1024)}, f32[1536]{0:T(1024)S(1)}, u32[]{:S(2)}) copy-start(f32[1536]{0:T(1024)S(1)} %get-tuple-element.170) | copy-start | bytes 18436
  11.3 8.7 %copy-start.27 = (f32[1536]{0:T(1024)}, f32[1536]{0:T(1024)S(1)}, u32[]{:S(2)}) copy-start(f32[1536]{0:T(1024)S(1)} %get-tuple-element.171) | copy-start | bytes 18436
  11.3 8.7 %copy-start.29 = (f32[1536]{0:T(1024)}, f32[1536]{0:T(1024)S(1)}, u32[]{:S(2)}) copy-start(f32[1536]{0:T(1024)S(1)} %get-tuple-element.172) | copy-start | bytes 18436
  11.3 8.7 %copy-start.31 = (f32[1536]{0:T(1024)}, f32[1536]{0:T(1024)S(1)}, u32[]{:S(2)}) copy-start(f32[1536]{0:T(1024)S(1)} %get-tuple-element.173) | copy-start | bytes 18436
  11.3 8.7 %copy-start.33 = (f32[1536]{0:T(1024)}, f32[1536]{0:T(1024)S(1)}, u32[]{:S(2)}) copy-start(f32[1536]{0:T(1024)S(1)} %get-tuple-element.174) | copy-start | bytes 18436
  11.3 8.7 %copy-start.35 = (f32[1536]{0:T(1024)}, f32[1536]{0:T(1024)S(1)}, u32[]{:S(2)}) copy-start(f32[1536]{0:T(1024)S(1)} %get-tuple-element.175) | copy-start | bytes 18436
  11.3 8.7 %copy-start.37 = (f32[1536]{0:T(1024)}, f32[1536]{0:T(1024)S(1)}, u32[]{:S(2)}) copy-start(f32[1536]{0:T(1024)S(1)} %get-tuple-element.176) | copy-start | bytes 18436
  20.0 31.5 %copy-start.15 = (bf16[1,128,1536]{2,1,0:T(8,128)(2,1)S(1)}, bf16[1,128,1536]{2,1,0:T(8,128)(2,1)}, u32[]{:S(2)}) copy-start(bf16[1,128,1536]{2,1,0:T(8,128)(2,1)} %param.9) | copy-start | bytes 1179652
  20.0 31.5 %copy-start.39 = (f32[1536]{0:T(1024)S(1)}, f32[1536]{0:T(1024)}, u32[]{:S(2)}) copy-start(f32[1536]{0:T(1024)} %param.12) | copy-start | bytes 18436
  20.0 31.5 %copy-start.40 = (f32[1536]{0:T(1024)S(1)}, f32[1536]{0:T(1024)}, u32[]{:S(2)}) copy-start(f32[1536]{0:T(1024)} %param.11) | copy-start | bytes 18436
  51.9 149.2 %copy-start.42 = (f32[128]{0:T(128)}, f32[128]{0:T(128)S(1)}, u32[]{:S(2)}) copy-start(f32[128]{0:T(128)S(1)} %broadcast_multiply_fusion.3) | copy-start | bytes 1540
  52.2 149.0 %copy-start.44 = (f32[128]{0:T(128)}, f32[128]{0:T(128)S(1)}, u32[]{:S(2)}) copy-start(f32[128]{0:T(128)S(1)} %add_rsqrt_fusion) | copy-start | bytes 1540
  290.6 8.7 %copy-start.14 = (f32[96,1536]{1,0:T(8,128)S(1)}, f32[96,1536]{1,0:T(8,128)}, u32[]{:S(2)}) copy-start(f32[96,1536]{1,0:T(8,128)} %reshape.213) | copy-start | bytes 1769476
  292.5 12.2 %copy-start.8 = (f32[128,1536]{1,0:T(8,128)S(1)}, f32[128,1536]{1,0:T(8,128)}, u32[]{:S(2)}) copy-start(f32[128,1536]{1,0:T(8,128)} %copy-done.7) | copy-start | bytes 2359300
  292.5 12.2 %copy-start.11 = (f32[1,128,1536]{2,1,0:T(8,128)S(1)}, f32[1,128,1536]{2,1,0:T(8,128)}, u32[]{:S(2)}) copy-start(f32[1,128,1536]{2,1,0:T(8,128)} %get-tuple-element.191) | copy-start | bytes 2359300
  292.5 11.4 %collective-permute-start.2 = (f32[2,15,1536]{2,1,0:T(8,128)}, f32[2,15,1536]{2,1,0:T(8,128)}, u32[]{:S(2)}, u32[]{:S(2)}) collective-permute-start(f32[2,15,1536]{2,1,0:T(8,128)} %get-tuple-element.188), channel_id=1, source_target_pairs={{0,1},{1,2},{2,3},{3,4},{4,5},{5,6},{6,7},{7,8},{8,9},{9,10},{10,1... | collective-permute-start | bytes 552968 | tf_op jit(solution)/shard_map/ppermute | solution.py:27
  297.3 7.3 %collective-permute-start.3 = (f32[2,15,1536]{2,1,0:T(8,128)}, f32[2,15,1536]{2,1,0:T(8,128)}, u32[]{:S(2)}, u32[]{:S(2)}) collective-permute-start(f32[2,15,1536]{2,1,0:T(8,128)} %get-tuple-element.189), channel_id=1, source_target_pairs={{1,0},{2,1},{3,2},{4,3},{5,4},{6,5},{7,6},{8,7},{9,8},{10,9},{11,1... | collective-permute-start | bytes 552968 | tf_op jit(solution)/shard_map/ppermute | solution.py:30
  (31 other events, 49.7 us)

commit v4 on v3

--- a/solution.py
+++ b/solution.py
@@ -51,6 +51,11 @@
     return [jnp.sum(value * rimmed[lag : lag + length], axis=0) for lag in range(TAPS)]
 
 
+def by_rank(rows):
+    short = -len(rows) % NEAR
+    return jnp.pad(jnp.stack(rows), ((0, short), (0, 0))).reshape(NEAR, -1, D)
+
+
 class Groups:
     def __init__(self):
         dp_size, tm_size = lax.axis_size("dp"), lax.axis_size("tm")
@@ -66,8 +71,10 @@
     def far(self, rank):
         return (rank // self.lines, (rank % self.lines) * NEAR + self.near_rank)
 
-    def enter(self):
+    def enter(self, others=()):
         barrier = pltpu.get_barrier_semaphore()
+        for other in others:
+            pl.semaphore_signal(barrier, inc=1, device_id=other, device_id_type=MESH)
 
         def greet(size, rank, place):
             def step(k, carry):
@@ -80,7 +87,7 @@
 
         greet(self.near_size, self.near_rank, self.near)
         greet(self.far_size, self.far_rank, self.far)
-        pl.semaphore_wait(barrier, self.near_size + self.far_size - 2)
+        pl.semaphore_wait(barrier, self.near_size + self.far_size - 2 + len(others))
 
 
 CORES = 2
@@ -119,15 +126,6 @@
 
     def on_dp(self, dp):
         return (dp, self.at(self.y, self.z, self.core)[1])
-
-    def enter(self):
-        barrier = pltpu.get_barrier_semaphore()
-        peers = [self.sibling(), self.line(1), self.line(-1)]
-        peers += [self.on_dp(self.other_dp(step)) for step in range(1, lax.axis_size("dp"))]
-        peers += [self.zed((self.z + k) % ZEDS) for k in range(1, ZEDS)]
-        for peer in peers:
-            pl.semaphore_signal(barrier, inc=1, device_id=peer, device_id_type=MESH)
-        pl.semaphore_wait(barrier, len(peers))
 
 
 def remote(source, target, send_sem, recv_sem, device):
@@ -305,16 +303,28 @@
     )(x, w_in, w_out)
 
 
-def sums_kernel(
+SIDE = 16
+
+
+def last_kernel(
+    count,
     x_ref,
+    grad_ref,
+    norm_ref,
+    resid_ref,
+    scale_ref,
+    taps_ref,
     g0_ref,
     g1_ref,
     o_ref,
+    frames_ref,
     h0_ref,
     h1_ref,
     near_held,
     far_held,
     mids,
+    rims,
+    wide,
     near_send,
     near_recv,
     far_send,
@@ -323,9 +333,14 @@
     out_recv,
     y_sems,
     z_sems,
+    rim_send,
+    rim_recv,
 ):
     groups, place = Groups(), Place()
     rank = groups.near_rank
+    length = grad_ref.shape[0]
+    tm, tm_size = groups.tm, lax.axis_size("tm")
+    after, before = (groups.dp, (tm + 1) % tm_size), (groups.dp, (tm + tm_size - 1) % tm_size)
     near_held[rank] = x_ref[rank]
     half, line = place.z // HALF * HALF, place.z % HALF
     turn = look([entry for row in TURN for entry in row], place.y * HALF + line)
@@ -338,11 +353,25 @@
         y_hops.append(
             Hop(mids.at[i], target, home == place.y, place.at(home, place.z, place.core), y_sems.at[i])
         )
-    groups.enter()
+    rim_copies = []
+    for i, ref in enumerate((grad_ref, norm_ref)):
+        for side, rows, device in ((0, length - SIDE, after), (1, 0, before)):
+            rim_copies.append(
+                remote(
+                    ref.at[pl.ds(rows, SIDE)],
+                    rims.at[i, side],
+                    rim_send.at[i, side],
+                    rim_recv.at[i, side],
+                    device,
+                )
+            )
+    groups.enter((after, before))
     near = Trade(
         groups.near_size, rank, groups.near, lambda p: x_ref.at[p], near_held, near_send, near_recv
     )
     near.start()
+    for copy in rim_copies:
+        copy.start()
     for hop in z_hops:
         hop.start()
     near.finish()
@@ -355,29 +384,63 @@
     for y_hop, z_hop in zip(y_hops, z_hops):
         z_hop.finish()
         y_hop.start()
+    for copy in rim_copies:
+        copy.wait_recv()
     far.finish()
-    o_ref[rank] = jnp.sum(far_held[...], axis=0)
+    total = jnp.sum(far_held[...], axis=0)
+    o_ref[rank] = total
     done = o_ref.at[rank]
     out = Trade(groups.near_size, rank, groups.near, lambda p: done, o_ref, out_send, out_recv)
     out.start()
+    first, second = total[-2:-1] / count, total[-1:] / count
+
+    def conv_gradient(grad, norm):
+        value = scale_ref[...] * (grad - first - norm * second)
+        return value.astype(jnp.bfloat16).astype(jnp.float32)
+
+    for side, rows, edge in ((0, 0, tm == 0), (1, SIDE + length, tm == tm_size - 1)):
+        value = conv_gradient(rims[0, side], rims[1, side])
+        wide[pl.ds(rows, SIDE)] = jnp.where(edge, 0.0, value)
+    wide[pl.ds(SIDE, length)] = conv_gradient(grad_ref[...], norm_ref[...])
+
+    def columns_of(j, carry):
+        columns = pl.ds(pl.multiple_of(j * 128, 128), 128)
+        value = resid_ref[:, columns]
+        for lag in range(TAPS):
+            start = SIDE + TAPS // 2 - lag
+            value = value + taps_ref[pl.ds(lag, 1), columns] * wide[pl.ds(start, length), columns]
+        frames_ref[:, columns] = value.astype(frames_ref.dtype)
+        return carry
+
+    lax.fori_loop(0, resid_ref.shape[1] // 128, columns_of, 0)
     out.finish()
     for hop in y_hops:
         hop.finish()
-
-
-def sums_and_gradients(x, g0, g1, collective_id):
+    for copy in rim_copies:
+        copy.wait_send()
+
+
+def last_step(x, grad, norm, resid, scale, taps, g0, g1, count, collective_id):
     far_size = lax.axis_size("dp") * (lax.axis_size("tm") // NEAR)
-    dma = pltpu.SemaphoreType.DMA
+    length, f32, dma = grad.shape[0], jnp.float32, pltpu.SemaphoreType.DMA
     gradient = jax.ShapeDtypeStruct(g0.shape, g0.dtype)
+    vmem, anywhere = pl.BlockSpec(memory_space=pltpu.VMEM), pl.BlockSpec(memory_space=pl.ANY)
     return pl.pallas_call(
-        sums_kernel,
-        out_shape=(jax.ShapeDtypeStruct(x.shape, x.dtype), gradient, gradient),
-        in_specs=[pl.BlockSpec(memory_space=pltpu.VMEM)] + [pl.BlockSpec(memory_space=pl.ANY)] * 2,
-        out_specs=[pl.BlockSpec(memory_space=pltpu.VMEM)] + [pl.BlockSpec(memory_space=pl.ANY)] * 2,
+        functools.partial(last_kernel, count),
+        out_shape=(
+            jax.ShapeDtypeStruct(x.shape, x.dtype),
+            jax.ShapeDtypeStruct(grad.shape, jnp.bfloat16),
+            gradient,
+            gradient,
+        ),
+        in_specs=[vmem] * 6 + [anywhere] * 2,
+        out_specs=[vmem] * 2 + [anywhere] * 2,
         scratch_shapes=[
             pltpu.VMEM(x.shape, x.dtype),
             pltpu.VMEM((far_size,) + x.shape[1:], x.dtype),
             pltpu.VMEM((2,) + g0.shape, g0.dtype),
+            pltpu.VMEM((2, 2, SIDE, D), f32),
+            pltpu.VMEM((length + 2 * SIDE, D), f32),
             dma((NEAR,)),
             dma((NEAR,)),
             dma((far_size,)),
@@ -386,11 +449,13 @@
             dma((NEAR,)),
             dma((2, 3)),
             dma((2, 3)),
+            dma((2, 2)),
+            dma((2, 2)),
         ],
         compiler_params=pltpu.CompilerParams(
-            collective_id=collective_id, has_side_effects=True, vmem_limit_bytes=16 << 20
+            collective_id=collective_id, has_side_effects=True, vmem_limit_bytes=24 << 20
         ),
-    )(x, g0, g1)
+    )(x, grad, norm, resid, scale, taps, g0, g1)
 
 
 CHUNKS = ((2, 0, 1, None), (2, 1, -1, None), (1, 1, 1, None), (3, 0, -1, None), (1, 0, 1, 0), (3, 1, -1, 1), (0, 0, 0, None), (0, 1, 0, None))
@@ -399,8 +464,8 @@
 WIDE = 512
 
 
-def experts_kernel(shares, x_ref, u_ref, in_share, out_share, *refs):
-    o_refs, g_refs, refs = refs[:2], refs[2:4], refs[4:]
+def experts_kernel(shares, x_ref, u_ref, in_share, out_share, lags_ref, *refs):
+    o_refs, g_refs, sums_ref, refs = refs[:2], refs[2:4], refs[4], refs[5:]
     (
         rows_x,
         rows_u,
@@ -415,6 +480,14 @@
         gradient,
         parting,
         parts,
+        near_held,
+        far_held,
+        near_send,
+        near_recv,
+        far_send,
+        far_recv,
+        out_send,
+        out_recv,
         weight_own,
         weight_send,
         weight_recv,
@@ -434,9 +507,20 @@
         z_send,
         z_recv,
     ) = refs
-    place = Place()
+    place, groups = Place(), Groups()
     y, z, core = place.y, place.z, place.core
     arrays = ((x_ref, rows_x), (u_ref, rows_u))
+    rank = groups.near_rank
+    near_held[rank] = lags_ref[rank]
+    near = Trade(
+        groups.near_size, rank, groups.near, lambda p: lags_ref.at[p], near_held, near_send, near_recv
+    )
+    mine = far_held.at[groups.far_rank]
+    far = Trade(
+        groups.far_size, groups.far_rank, groups.far, lambda p: mine, far_held, far_send, far_recv
+    )
+    done = sums_ref.at[rank]
+    out = Trade(groups.near_size, rank, groups.near, lambda p: done, sums_ref, out_send, out_recv)
     waits = []
 
     weights = ((in_share, w_in), (out_share, w_out))
@@ -670,7 +754,7 @@
             def _():
                 o_refs[a][target] = results[a, LEAVING + half, core, j]
 
-    place.enter()
+    groups.enter()
     for a in range(2):
         own_copy(a).start()
         for k in SWEEP[1:]:
@@ -683,6 +767,7 @@
         spread(0, m)
     all_shared(0)
     weights_arrive()
+    near.start()
     for m in range(ZEDS + LAG):
         spread(1, m)
         if m < len(CHUNKS):
@@ -692,6 +777,9 @@
     for i in (4, 5):
         leave(0, i)
     all_shared(1)
+    near.finish()
+    far_held[groups.far_rank] = jnp.sum(near_held[...], axis=0)
+    far.start()
     for i in range(len(CHUNKS)):
         backward(i)
         if 1 <= i <= 4:
@@ -700,6 +788,9 @@
             finish(0, 0)
         if i == 7:
             finish(0, 1)
+    far.finish()
+    sums_ref[rank] = jnp.sum(far_held[...], axis=0)
+    out.start()
     weight_gradient(1, hid_held, rows_u)
     for i in (4, 5):
         leave(1, i)
@@ -708,6 +799,7 @@
         finish(1, half)
     for i in (1, 0):
         gather_gradient(i)
+    out.finish()
     for a in range(2):
         for k in range(1, ZEDS):
             other = (z + k) % ZEDS
@@ -730,7 +822,7 @@
             part_copy(i, step).wait_send()
 
 
-def experts(x, u, in_share, out_share, collective_id):
+def experts(x, u, in_share, out_share, lags, collective_id):
     shares = lax.axis_size("dp")
     hidden = in_share.shape[1]
     tile = x.shape[1:]
@@ -740,7 +832,14 @@
     out = jax.ShapeDtypeStruct(x.shape, bf16)
     gradient = jax.ShapeDtypeStruct((hidden, D // shares), bf16)
     held = lines + (tile[0], hidden)
+    far_size = shares * (lax.axis_size("tm") // NEAR)
     sems = [
+        (NEAR,),
+        (NEAR,),
+        (far_size,),
+        (far_size,),
+        (NEAR,),
+        (NEAR,),
         (2,),
         (2, shares),
         (2, shares),
@@ -762,9 +861,9 @@
     ]
     return pl.pallas_call(
         functools.partial(experts_kernel, shares),
-        out_shape=(out, out, gradient, gradient),
-        in_specs=[pl.BlockSpec(memory_space=pl.ANY)] * 4,
-        out_specs=[pl.BlockSpec(memory_space=pltpu.VMEM)] * 4,
+        out_shape=(out, out, gradient, gradient, jax.ShapeDtypeStruct(lags.shape, lags.dtype)),
+        in_specs=[pl.BlockSpec(memory_space=pl.ANY)] * 4 + [pl.BlockSpec(memory_space=pltpu.VMEM)],
+        out_specs=[pl.BlockSpec(memory_space=pltpu.VMEM)] * 5,
         scratch_shapes=[
             pltpu.VMEM(lines + tile, bf16),
             pltpu.VMEM(lines + tile, bf16),
@@ -779,12 +878,14 @@
             pltpu.VMEM((hidden, D), f32),
             pltpu.VMEM((2, shares) + gradient.shape, bf16),
             pltpu.VMEM((2, shares) + gradient.shape, bf16),
+            pltpu.VMEM(lags.shape, lags.dtype),
+            pltpu.VMEM((far_size,) + lags.shape[1:], lags.dtype),
         ]
         + [dma(shape) for shape in sems],
         compiler_params=pltpu.CompilerParams(
             collective_id=collective_id, has_side_effects=True, vmem_limit_bytes=58 << 20
         ),
-    )(x, u, in_share, out_share)
+    )(x, u, in_share, out_share, lags)
 
 
 def body(
@@ -845,8 +946,10 @@
     buffer = bucketed(normed).astype(jnp.bfloat16).reshape(EXPERTS, capacity, D)
     sent_buffer = (gate_rows[:, None] * bucketed(cotangent[0])).astype(jnp.bfloat16)
     sent_buffer = sent_buffer.reshape(EXPERTS, capacity, D)
-    combined, back, grad_in_local, grad_out_local = experts(
-        buffer, sent_buffer, w_in_share, w_out_share, 1
+    signal_lags = [jnp.sum(rimmed[lag : lag + length], axis=0) for lag in range(TAPS)]
+    lags = by_rank(signal_lags + lag_sums(normalized_input, rimmed))
+    combined, back, grad_in_local, grad_out_local, lags = experts(
+        buffer, sent_buffer, w_in_share, w_out_share, lags, 1
     )
     combined = combined.reshape(EXPERTS * capacity, D).astype(jnp.float32)
     back = back.reshape(EXPERTS * capacity, D).astype(jnp.float32)
@@ -864,39 +967,37 @@
     dproj = jnp.mean(dnormed * vhat, axis=-1, keepdims=True)
     dresid = upstream + lrstd * (dnormed - dmean - vhat * dproj)
     normalized_gradient = dresid * swish_slope(before_activation) * batchnorm_gain_scale
-    signal_lags = [jnp.sum(rimmed[lag : lag + length], axis=0) for lag in range(TAPS)]
-    normalized_lags = lag_sums(normalized_input, rimmed)
-    gradient_lags = lag_sums(normalized_gradient, rimmed)
-    moment_rows = [
-        jnp.sum(normalized_gradient, axis=0),
-        jnp.sum(normalized_gradient * normalized_input, axis=0),
-    ]
-    lag_rows = jnp.stack(gradient_lags + signal_lags + normalized_lags)
-    per_rank = -(-lag_rows.shape[0] // NEAR)
-    lag_rows = jnp.pad(lag_rows, ((0, NEAR * per_rank - lag_rows.shape[0]), (0, 0)))
+    moment_rows = jnp.stack(
+        [
+            jnp.sum(normalized_gradient, axis=0),
+            jnp.sum(normalized_gradient * normalized_input, axis=0),
+        ]
+    )
     to_sum = jnp.concatenate(
         [
-            lag_rows.reshape(NEAR, per_rank, D),
-            jnp.broadcast_to(jnp.stack(moment_rows)[None], (NEAR, 2, D)),
+            by_rank(lag_sums(normalized_gradient, rimmed)),
+            jnp.broadcast_to(moment_rows[None], (NEAR,) + moment_rows.shape),
         ],
         axis=1,
     )
-    rims = extended(jnp.stack([normalized_gradient, normalized_input]), (("tm", 1),), half)
-    summed, grad_w_in, grad_w_out = sums_and_gradients(to_sum, grad_in_local, grad_out_local, 2)
-    first_mean, second_mean = (summed[0, per_rank + i] / element_count for i in range(2))
-    lag_rows = summed[:, :per_rank].reshape(NEAR * per_rank, D)
+    summed, grad_frames, grad_w_in, grad_w_out = last_step(
+        to_sum,
+        normalized_gradient,
+        normalized_input,
+        dresid,
+        inverse_deviation[None],
+        taps,
+        grad_in_local,
+        grad_out_local,
+        element_count,
+        2,
+    )
+    lag_rows = lags.reshape(-1, D)
     grad_taps = inverse_deviation * (
-        lag_rows[:TAPS]
-        - first_mean * lag_rows[TAPS : 2 * TAPS]
-        - second_mean * lag_rows[2 * TAPS : 3 * TAPS]
-    )
-    convolution_gradient = (
-        inverse_deviation * (rims[0] - first_mean - rims[1] * second_mean)
-    ).astype(jnp.bfloat16)
-    at = lax.axis_index("tm") * length - half + jnp.arange(length + 2 * half)
-    inside = (at >= 0) & (at < lax.axis_size("tm") * length)
-    grad_rimmed = jnp.where(inside[:, None], convolution_gradient, 0).astype(jnp.float32)
-    grad_frames = (dresid + conv_lags(grad_rimmed, taps, length, True)).astype(jnp.bfloat16)
+        summed[:, :-2].reshape(-1, D)[:TAPS]
+        - summed[0, -2] / element_count * lag_rows[:TAPS]
+        - summed[0, -1] / element_count * lag_rows[TAPS : 2 * TAPS]
+    )
     grad_w_in, grad_w_out = grad_w_in.T.astype(jnp.float32), grad_w_out.astype(jnp.float32)
     return (mixed[None], grad_frames[None], grad_taps, grad_w_in, grad_w_out)
 

time: 316 us -> 286 us (0.905)
  the two profiles are of different devices: /device:TPU:57 before, /device:TPU:1 now
where the time goes in v4:
time: 286 us; the launch traced here: 281 us
  Pallas kernels  229 us (80%)
  other arithmetic  18.7 us (7%)
  local copies, waits for them, and re-layouts  17.1 us (6%)
  starting transfers between devices  6.86 us (2%)
  matrix products  6.76 us (2%)
    pallas_call x1, Pallas kernels, experts(): pl.pallas_call(functools.partial(experts_kernel, shares), out_shape=(out,...  148 us
    pallas_call x1, Pallas kernels, last_step(): pl.pallas_call(functools.partial(last_kernel, count), out_shape=(jax.Shap...  48.4 us
    pallas_call x1, Pallas kernels, moments_and_weights(): pl.pallas_call(functools.partial(moments_kernel, count), out_shape=(jax.S...  33.1 us
    reduce_sum x4, other arithmetic, lag_sums(): jnp.sum(value * rimmed[lag:lag + length], axis=0)  8.17 us
    unnamed x43, local copies, waits for them, and re-layouts  7.91 us
  transfers between devices with their start and end apart: 2, of which 0 were waited for; matrix products, arithmetic and copies ran while one was open for 3% of the time, Pallas kernels for 0%

profile of v4, /device:TPU:1, one launch (start us, length us, event | category | flops | bytes accessed | tf_op | source)
XLA Modules:
  0.0 280.7 jit_solution(519313298834861535)
XLA Ops:
  0.7 0.9 fusion.123
  1.5 4.9 %collective-permute-start = (bf16[1,15,1536]{2,1,0:T(8,128)(2,1)S(1)}, bf16[1,15,1536]{2,1,0:T(8,128)(2,1)S(1)}, u32[]{:S(2)}, u32[]{:S(2)}) collective-permute-start(bf16[1,15,1536]{2,1,0:T(8,128)(2,1)S(1)} %get-tuple-element.197), channel_id=1, source_target_pairs={{0,1},{1,2},{2,3},{3,4},{4,5},{5,6},{6,7},{7,8},{8,9},{9,10},{10,1... | collective-permute-start | bytes 138248 | tf_op jit(solution)/shard_map/ppermute | solution.py:27
  6.5 1.9 collective-permute-start.1
  9.5 2.1 slice_reduce_fusion.63
  14.3 1.5 slice_reduce_fusion.62
  16.0 1.6 slice_reduce_fusion
  18.4 3.1 %fusion.121 = (f32[1536]{0:T(1024)S(1)}, f32[128,1536]{1,0:T(8,128)S(1)}) fusion(f32[1,158,1536]{2,1,0:T(8,128)S(1)} %maximum_convert_fusion, f32[1536]{0:T(1024)S(1)} %get-tuple-element.180, f32[1536]{0:T(1024)S(1)} %get-tuple-element.151, f32[1536]{0:T(1024)S(1)} %get-tuple-element.152, f32[1536]{0:T(1024)S(1)} %get-tuple-element.153, ...), kind=kLoop, calls=%fused_computation.330 | loop fusion | flops 12188160 | bytes 25362432 | tf_op jit(solution)/shard_map/reduce_sum | solution.py:909
  21.7 33.1 %shard_map.128 = (f32[2,1536]{1,0:T(2,128)S(1)}, bf16[384,384]{1,0:T(8,128)(2,1)S(1)}, bf16[96,1536]{1,0:T(8,128)(2,1)S(1)}) custom-call(f32[2,1536]{1,0:T(2,128)S(1)} %pad_maximum_fusion.1.x_ref, bf16[1536,384]{1,0:T(8,128)(2,1)S(1)} %copy-done.1, bf16[384,1536]{1,0:T(8,128)(2,1)S(1)} %copy-done.2), custom_call_target="tpu_custom_call" | custom-call | tf_op jit(solution)/shard_map/pallas_call | solution.py:284
  56.3 2.1 fusion.4
  58.4 1.7 fusion.58
  61.7 0.9 reshape.209.lags_ref
  63.4 1.3 convolution_convert_fusion
  64.8 1.3 fusion
  66.0 147.7 %shard_map.129 = (bf16[8,32,1536]{2,1,0:T(8,128)(2,1)}, bf16[8,32,1536]{2,1,0:T(8,128)(2,1)}, bf16[384,384]{1,0:T(8,128)(2,1)}, bf16[384,384]{1,0:T(8,128)(2,1)}, f32[16,4,1536]{2,1,0:T(4,128)}) custom-call(bf16[8,32,1536]{2,1,0:T(8,128)(2,1)} %bitcast.464, bf16[8,32,1536]{2,1,0:T(8,128)(2,1)} %bitcast.465, bf16[384,384]{1,0:T(8,128)(2,1)} %copy-done.4, ...), custom_call_target="tpu_custom_call" | custom-call | tf_op jit(solution)/shard_map/pallas_call | solution.py:862
  213.8 1.5 fusion.102
  215.3 1.3 fusion.2
  218.9 2.9 %fusion.5 = (f32[1536]{0:T(1024)S(1)}, f32[1536]{0:T(1024)S(1)}, f32[1536]{0:T(1024)S(1)}, f32[1536]{0:T(1024)S(1)}, f32[1536]{0:T(1024)S(1)}, /*index=5*/f32[15...) fusion(f32[1,158,1536]{2,1,0:T(8,128)S(1)} %copy-done.11, ...), kind=kLoop, calls=%fused_computation.15 | loop fusion | flops 10785792 | bytes 18606080 | tf_op jit(solution)/shard_map/reduce_sum | solution.py:51
  221.8 1.5 fusion.59
  224.6 1.0 copy-done.8
  225.5 1.0 copy-done.9
  226.5 48.4 %shard_map.130 = (f32[16,4,1536]{2,1,0:T(4,128)S(1)}, bf16[128,1536]{1,0:T(8,128)(2,1)S(1)}, bf16[384,384]{1,0:T(8,128)(2,1)S(1)}, bf16[384,384]{1,0:T(8,128)(2,1)S(1)}) custom-call(f32[16,4,1536]{2,1,0:T(4,128)S(1)} %pad_maximum_fusion.x_ref, f32[128,1536]{1,0:T(8,128)S(1)} %get-tuple-element.183.grad_ref, f32[128,1536]{1,0:T(8,128)S(1)} %get-tuple-element.187.norm_ref, ...), custom_call_target="tpu_custom_call" | custom-call | tf_op jit(solution)/shard_map/pallas_call | solution.py:428
  275.9 1.1 reshape.214
  277.1 1.1 copy.34
  278.1 0.9 convert_element_type.66
  (185 shorter events, 14.0 us)
Async XLA Ops:
  0.6 62.3 %copy-start = (bf16[1536,8]{0,1:T(8,128)(2,1)S(1)}, bf16[1536,8]{0,1:T(8,128)(2,1)}, u32[]{:S(2)}) copy-start(bf16[1536,8]{0,1:T(8,128)(2,1)} %param.13) | copy-start | bytes 73732
  0.6 15.2 %copy-start.14 = (bf16[1,128,1536]{2,1,0:T(8,128)(2,1)S(1)}, bf16[1,128,1536]{2,1,0:T(8,128)(2,1)}, u32[]{:S(2)}) copy-start(bf16[1,128,1536]{2,1,0:T(8,128)(2,1)} %param.9) | copy-start | bytes 1179652
  1.5 14.3 %collective-permute-start = (bf16[1,15,1536]{2,1,0:T(8,128)(2,1)S(1)}, bf16[1,15,1536]{2,1,0:T(8,128)(2,1)S(1)}, u32[]{:S(2)}, u32[]{:S(2)}) collective-permute-start(bf16[1,15,1536]{2,1,0:T(8,128)(2,1)S(1)} %get-tuple-element.197), channel_id=1, source_target_pairs={{0,1},{1,2},{2,3},{3,4},{4,5},{5,6},{6,7},{7,8},{8,9},{9,10},{10,1... | collective-permute-start | bytes 138248 | tf_op jit(solution)/shard_map/ppermute | solution.py:27
  6.5 9.3 %collective-permute-start.1 = (bf16[1,15,1536]{2,1,0:T(8,128)(2,1)S(1)}, bf16[1,15,1536]{2,1,0:T(8,128)(2,1)S(1)}, u32[]{:S(2)}, u32[]{:S(2)}) collective-permute-start(bf16[1,15,1536]{2,1,0:T(8,128)(2,1)S(1)} %get-tuple-element.198), channel_id=1, source_target_pairs={{1,0},{2,1},{3,2},{4,3},{5,4},{6,5},{7,6},{8,7},{9,8},{10,9},{11,1... | collective-permute-start | bytes 138248 | tf_op jit(solution)/shard_map/ppermute | solution.py:30
  16.0 42.4 %copy-start.10 = (f32[1,158,1536]{2,1,0:T(8,128)}, f32[1,158,1536]{2,1,0:T(8,128)S(1)}, u32[]{:S(2)}) copy-start(f32[1,158,1536]{2,1,0:T(8,128)S(1)} %maximum_convert_fusion) | copy-start | bytes 2912260
  18.4 3.3 %copy-start.1 = (bf16[1536,384]{1,0:T(8,128)(2,1)S(1)}, bf16[1536,384]{1,0:T(8,128)(2,1)}, u32[]{:S(2)}) copy-start(bf16[1536,384]{1,0:T(8,128)(2,1)} %w_in_ref.1) | copy-start | bytes 3538948
  18.4 3.3 %copy-start.2 = (bf16[384,1536]{1,0:T(8,128)(2,1)S(1)}, bf16[384,1536]{1,0:T(8,128)(2,1)}, u32[]{:S(2)}) copy-start(bf16[384,1536]{1,0:T(8,128)(2,1)} %w_out_ref.1) | copy-start | bytes 3538948
  54.8 0.7 copy-start.4
  55.5 0.7 copy-start.5
  56.3 2.1 copy-start.15
  56.3 2.1 copy-start.17
  56.3 2.1 copy-start.18
  62.5 0.7 copy-start.19
  63.0 1.8 copy-start.12
  213.8 1.5 copy-start.13
  216.5 1.1 copy-start.16
  217.7 1.2 copy-start.11
  223.6 0.9 copy-start.3
  224.5 1.0 copy-start.8
  225.5 1.0 copy-start.9
  274.9 0.7 copy-start.6
  275.6 1.4 copy-start.7

commit v5 on v4

--- a/solution.py
+++ b/solution.py
@@ -19,41 +19,9 @@
 EXACT = lax.Precision.HIGHEST
 
 
-def extended(block, sides, width):
-    for axis, dim in sides:
-        count = lax.axis_size(axis)
-        forward = [(i, i + 1) for i in range(count - 1)]
-        backward = [(target, source) for source, target in forward]
-        low = lax.ppermute(
-            lax.slice_in_dim(block, block.shape[dim] - width, None, axis=dim), axis, forward
-        )
-        high = lax.ppermute(lax.slice_in_dim(block, 0, width, axis=dim), axis, backward)
-        block = jnp.concatenate([low, block, high], axis=dim)
-    return block
-
-
 def swish_slope(pre):
     sigma = jax.nn.sigmoid(pre)
     return sigma * (1.0 + pre * (1.0 - sigma))
-
-
-def conv_lags(rimmed, taps, length, reverse):
-    total = jnp.zeros((length, rimmed.shape[1]), jnp.float32)
-    last = taps.shape[0] - 1
-    for lag in range(taps.shape[0]):
-        start = last - lag if reverse else lag
-        total = total + taps[lag] * rimmed[start : start + length]
-    return total
-
-
-def lag_sums(value, rimmed):
-    length = value.shape[0]
-    return [jnp.sum(value * rimmed[lag : lag + length], axis=0) for lag in range(TAPS)]
-
-
-def by_rank(rows):
-    short = -len(rows) % NEAR
-    return jnp.pad(jnp.stack(rows), ((0, short), (0, 0))).reshape(NEAR, -1, D)
 
 
 class Groups:
@@ -71,7 +39,7 @@
     def far(self, rank):
         return (rank // self.lines, (rank % self.lines) * NEAR + self.near_rank)
 
-    def enter(self, others=()):
+    def greet(self, others=()):
         barrier = pltpu.get_barrier_semaphore()
         for other in others:
             pl.semaphore_signal(barrier, inc=1, device_id=other, device_id_type=MESH)
@@ -87,7 +55,10 @@
 
         greet(self.near_size, self.near_rank, self.near)
         greet(self.far_size, self.far_rank, self.far)
-        pl.semaphore_wait(barrier, self.near_size + self.far_size - 2 + len(others))
+        return self.near_size + self.far_size - 2 + len(others)
+
+    def wait(self, signals):
+        pl.semaphore_wait(pltpu.get_barrier_semaphore(), signals)
 
 
 CORES = 2
@@ -220,27 +191,139 @@
     return jnp.stack([mean, squares])
 
 
-def moments_kernel(
-    count,
-    x_ref,
+SIDE = 16
+LAG = 4
+
+
+def place_row(ref, row, columns, value):
+    depth = ref.shape[1]
+    ref[row // depth, pl.ds(row % depth, 1), columns] = value
+
+
+def row_of(ref, row):
+    depth = ref.shape[1]
+    return ref[row // depth, pl.ds(row % depth, 1), :]
+
+
+class Spread:
+    SEMS = ((1,), (ZEDS,), (ZEDS,), (LINES * ZEDS,), (LINES * ZEDS,), (3, ZEDS), (3, ZEDS))
+
+    def __init__(self, place, source, rows, sems):
+        self.place, self.source, self.rows = place, source, rows
+        self.own, self.z_send, self.z_recv = sems[:3]
+        self.share_send, self.share_recv, self.y_send, self.y_recv = sems[3:]
+        self.waits = []
+
+    def z_copy(self, k):
+        place = self.place
+        target = (place.z + k) % ZEDS
+        mine = self.rows.at[place.core, place.y, place.z]
+        return remote(
+            self.source.at[target], mine, self.z_send.at[k], self.z_recv.at[k], place.zed(target)
+        )
+
+    def own_copy(self):
+        place = self.place
+        mine = self.rows.at[place.core, place.y, place.z]
+        return pltpu.make_async_copy(self.source.at[place.z], mine, self.own.at[0])
+
+    def block(self, core, step, k):
+        place = self.place
+        return self.rows.at[core, (place.y + step + LINES) % LINES, (place.z - k + ZEDS) % ZEDS]
+
+    def pass_on(self, step, k, send_sem, recv_sem, device):
+        ref = self.block(self.place.core, step, k)
+        copy = remote(ref, ref, send_sem, recv_sem, device)
+        copy.start()
+        self.waits.append(copy)
+
+    def arrived(self, core, step, k, send_sem, recv_sem):
+        ref = self.block(core, step, k)
+        remote(ref, ref, send_sem, recv_sem, self.place.sibling()).wait_recv()
+
+    def share(self, step, k):
+        index = step % LINES * ZEDS + k
+        self.pass_on(
+            step, k, self.share_send.at[index], self.share_recv.at[index], self.place.sibling()
+        )
+
+    def start(self):
+        self.own_copy().start()
+        for k in SWEEP[1:]:
+            self.z_copy(k).start()
+
+    def step(self, m):
+        place, core = self.place, self.place.core
+        if m < ZEDS:
+            k = SWEEP[m]
+            if k == 0:
+                self.own_copy().wait()
+            else:
+                self.arrived(core, 0, k, self.z_send.at[k], self.z_recv.at[k])
+            for way, step in ((0, 1), (1, -1)):
+                self.pass_on(0, k, self.y_send.at[way, k], self.y_recv.at[way, k], place.line(step))
+            self.share(0, k)
+        if 0 <= m - LAG // 2 < ZEDS:
+            i = m - LAG // 2
+            k = SWEEP[i]
+            for way, step in ((0, 1), (1, -1)):
+                self.arrived(core, -step, k, self.y_send.at[way, k], self.y_recv.at[way, k])
+                if i % 2 == way:
+                    self.pass_on(-step, k, self.y_send.at[2, k], self.y_recv.at[2, k], place.line(step))
+                self.share(-step, k)
+        if 0 <= m - LAG < ZEDS:
+            k = SWEEP[m - LAG]
+            self.arrived(core, 2, k, self.y_send.at[2, k], self.y_recv.at[2, k])
+            self.share(2, k)
+
+    def arrive(self):
+        for step in range(LINES):
+            for k in range(ZEDS):
+                index = step * ZEDS + k
+                self.arrived(
+                    1 - self.place.core, step, k, self.share_send.at[index], self.share_recv.at[index]
+                )
+
+    def finish(self):
+        for k in SWEEP[1:]:
+            self.z_copy(k).wait_send()
+        for copy in self.waits:
+            copy.wait_send()
+
+
+def first_kernel(
+    frames_ref,
+    taps_ref,
     w_in_ref,
     w_out_ref,
+    u_ref,
     o_ref,
+    conv_ref,
+    wide_ref,
+    lags_ref,
     w_in_share,
     w_out_share,
+    rows_ref,
     near_held,
     far_held,
     w_in_mid,
     w_out_mid,
+    rims,
     near_send,
     near_recv,
     far_send,
     far_recv,
     y_sems,
     z_sems,
+    rim_send,
+    rim_recv,
+    *spread_sems,
 ):
     groups, place = Groups(), Place()
-    near_held[groups.near_rank] = x_ref[...]
+    length = frames_ref.shape[0]
+    tm, tm_size = groups.tm, lax.axis_size("tm")
+    after, before = (groups.dp, (tm + 1) % tm_size), (groups.dp, (tm + tm_size - 1) % tm_size)
+    spread = Spread(place, u_ref, rows_ref, spread_sems)
     line = work_line(place)
     zed = place.z // HALF * HALF + home_line(place)
     y_hops, z_hops = [], []
@@ -250,65 +333,139 @@
         mine = source.at[pl.ds(pl.multiple_of(place.dp * depth, depth), depth)]
         y_hops.append(Hop(mine, mid, line == place.y, place.at(line, place.z, place.core), y_sems.at[i]))
         z_hops.append(Hop(mid, share, zed == place.z, place.zed(zed), z_sems.at[i]))
-    groups.enter()
+    rim_copies = [
+        remote(
+            frames_ref.at[pl.ds(rows, SIDE)], rims.at[side], rim_send.at[side], rim_recv.at[side], device
+        )
+        for side, rows, device in ((0, length - SIDE, after), (1, 0, before))
+    ]
     mine = near_held.at[groups.near_rank]
     near = Trade(
         groups.near_size, groups.near_rank, groups.near, lambda p: mine, near_held, near_send, near_recv
     )
-    near.start()
-    for hop in y_hops:
-        hop.start()
-    near.finish()
-    far_held[groups.far_rank] = moments_merge(near_held[...], float(count))
     mine_far = far_held.at[groups.far_rank]
     far = Trade(
         groups.far_size, groups.far_rank, groups.far, lambda p: mine_far, far_held, far_send, far_recv
     )
+    groups.wait(groups.greet((after, before)))
+    for copy in rim_copies:
+        copy.start()
+    spread.start()
+    for hop in y_hops:
+        hop.start()
+    wide_ref[pl.ds(SIDE, length)] = frames_ref[...].astype(jnp.float32)
+    for copy in rim_copies:
+        copy.wait_recv()
+    for side, rows, edge in ((0, 0, tm == 0), (1, SIDE + length, tm == tm_size - 1)):
+        wide_ref[pl.ds(rows, SIDE)] = jnp.where(edge, 0.0, rims[side].astype(jnp.float32))
+
+    def columns_of(j, carry):
+        columns = pl.ds(pl.multiple_of(j * 128, 128), 128)
+        value = jnp.zeros((length, 128), jnp.float32)
+        for lag in range(TAPS):
+            start = SIDE - TAPS // 2 + lag
+            value = value + taps_ref[pl.ds(lag, 1), columns] * wide_ref[pl.ds(start, length), columns]
+        conv_ref[:, columns] = value
+        mean = jnp.sum(value, axis=0, keepdims=True) / length
+        spread_out = value - mean
+        near_held[groups.near_rank, pl.ds(0, 1), columns] = mean
+        near_held[groups.near_rank, pl.ds(1, 1), columns] = jnp.sum(
+            spread_out * spread_out, axis=0, keepdims=True
+        )
+        return carry
+
+    def lags_of(j, carry):
+        columns = pl.ds(pl.multiple_of(j * 128, 128), 128)
+        mean = near_held[groups.near_rank, pl.ds(0, 1), columns]
+        value = conv_ref[:, columns] - mean
+        for lag in range(TAPS):
+            shifted = wide_ref[pl.ds(SIDE - TAPS // 2 + lag, length), columns]
+            place_row(lags_ref, lag, columns, jnp.sum(shifted, axis=0, keepdims=True))
+            place_row(lags_ref, TAPS + lag, columns, jnp.sum(value * shifted, axis=0, keepdims=True))
+        return carry
+
+    tiles = frames_ref.shape[1] // 128
+    for m in range(3):
+        spread.step(m)
+        lax.fori_loop(m * tiles // 3, (m + 1) * tiles // 3, columns_of, 0)
+    near.start()
+    zeros = jnp.zeros((1, D), jnp.float32)
+    for row in range(2 * TAPS, lags_ref.shape[0] * lags_ref.shape[1]):
+        place_row(lags_ref, row, pl.ds(0, D), zeros)
+    for m in range(3, 6):
+        spread.step(m)
+        lax.fori_loop((m - 3) * tiles // 3, (m - 2) * tiles // 3, lags_of, 0)
+    near.finish()
+    far_held[groups.far_rank] = moments_merge(near_held[...], float(length))
     far.start()
+    for m in range(6, 8):
+        spread.step(m)
     for y_hop, z_hop in zip(y_hops, z_hops):
         y_hop.finish()
         z_hop.start()
     far.finish()
-    o_ref[...] = moments_merge(far_held[...], float(count * groups.near_size))
+    moments = moments_merge(far_held[...], float(length * groups.near_size))
+    o_ref[...] = moments
+    scale = lax.rsqrt(moments[1:] / (length * groups.near_size * groups.far_size) + EPS)
+    shift = near_held[groups.near_rank, pl.ds(0, 1), :] - moments[:1]
+    for lag in range(TAPS):
+        value = row_of(lags_ref, TAPS + lag) + shift * row_of(lags_ref, lag)
+        place_row(lags_ref, TAPS + lag, pl.ds(0, D), scale * value)
+    for m in range(8, ZEDS + LAG):
+        spread.step(m)
+    spread.arrive()
     for hop in z_hops:
         hop.finish()
-
-
-def moments_and_weights(x, count, w_in, w_out, collective_id):
+    for copy in rim_copies:
+        copy.wait_send()
+    spread.finish()
+
+
+def first_step(frames, taps, w_in, w_out, u, collective_id):
     dp_size = lax.axis_size("dp")
     far_size = dp_size * (lax.axis_size("tm") // NEAR)
     shares = [
         jax.ShapeDtypeStruct((w.shape[0] // dp_size, w.shape[1]), w.dtype) for w in (w_in, w_out)
     ]
-    dma = pltpu.SemaphoreType.DMA
+    f32, dma = jnp.float32, pltpu.SemaphoreType.DMA
+    length = frames.shape[0]
+    vmem, anywhere = pl.BlockSpec(memory_space=pltpu.VMEM), pl.BlockSpec(memory_space=pl.ANY)
     return pl.pallas_call(
-        functools.partial(moments_kernel, count),
-        out_shape=(jax.ShapeDtypeStruct(x.shape, x.dtype), *shares),
-        in_specs=[pl.BlockSpec(memory_space=pltpu.VMEM)] + [pl.BlockSpec(memory_space=pl.ANY)] * 2,
-        out_specs=[pl.BlockSpec(memory_space=pltpu.VMEM)] + [pl.BlockSpec(memory_space=pl.ANY)] * 2,
+        first_kernel,
+        out_shape=(
+            jax.ShapeDtypeStruct((2, D), f32),
+            jax.ShapeDtypeStruct((length, D), f32),
+            jax.ShapeDtypeStruct((length + 2 * SIDE, D), f32),
+            jax.ShapeDtypeStruct((NEAR, -(-2 * TAPS // NEAR), D), f32),
+            *shares,
+            jax.ShapeDtypeStruct((CORES, LINES) + u.shape, u.dtype),
+        ),
+        in_specs=[vmem] * 2 + [anywhere] * 3,
+        out_specs=[vmem] * 4 + [anywhere] * 3,
         scratch_shapes=[
-            pltpu.VMEM((NEAR,) + x.shape, x.dtype),
-            pltpu.VMEM((far_size,) + x.shape, x.dtype),
+            pltpu.VMEM((NEAR, 2, D), f32),
+            pltpu.VMEM((far_size, 2, D), f32),
             *[pltpu.VMEM(share.shape, share.dtype) for share in shares],
+            pltpu.VMEM((2, SIDE, D), frames.dtype),
             dma((NEAR,)),
             dma((NEAR,)),
             dma((far_size,)),
             dma((far_size,)),
             dma((2, 3)),
             dma((2, 3)),
+            dma((2,)),
+            dma((2,)),
+            *[dma(shape) for shape in Spread.SEMS],
         ],
         compiler_params=pltpu.CompilerParams(
-            collective_id=collective_id, has_side_effects=True, vmem_limit_bytes=16 << 20
+            collective_id=collective_id, has_side_effects=True, vmem_limit_bytes=24 << 20
         ),
-    )(x, w_in, w_out)
-
-
-SIDE = 16
+    )(frames, taps, w_in, w_out, u)
 
 
 def last_kernel(
     count,
-    x_ref,
+    signal_ref,
     grad_ref,
     norm_ref,
     resid_ref,
@@ -325,6 +482,7 @@
     mids,
     rims,
     wide,
+    x_ref,
     near_send,
     near_recv,
     far_send,
@@ -341,7 +499,6 @@
     length = grad_ref.shape[0]
     tm, tm_size = groups.tm, lax.axis_size("tm")
     after, before = (groups.dp, (tm + 1) % tm_size), (groups.dp, (tm + tm_size - 1) % tm_size)
-    near_held[rank] = x_ref[rank]
     half, line = place.z // HALF * HALF, place.z % HALF
     turn = look([entry for row in TURN for entry in row], place.y * HALF + line)
     home = home_line(place)
@@ -365,7 +522,29 @@
                     device,
                 )
             )
-    groups.enter((after, before))
+    signals = groups.greet((after, before))
+    rows = x_ref.shape[1] - 2
+
+    def lags_of(j, carry):
+        columns = pl.ds(pl.multiple_of(j * 128, 128), 128)
+        value = grad_ref[:, columns]
+        for lag in range(TAPS):
+            shifted = signal_ref[pl.ds(SIDE - TAPS // 2 + lag, length), columns]
+            x_ref[lag // rows, pl.ds(lag % rows, 1), columns] = jnp.sum(
+                value * shifted, axis=0, keepdims=True
+            )
+        first_row = jnp.sum(value, axis=0, keepdims=True)
+        second_row = jnp.sum(value * norm_ref[:, columns], axis=0, keepdims=True)
+        for p in range(x_ref.shape[0]):
+            x_ref[p, pl.ds(rows, 1), columns] = first_row
+            x_ref[p, pl.ds(rows + 1, 1), columns] = second_row
+        return carry
+
+    for lag in range(TAPS, rows * x_ref.shape[0]):
+        x_ref[lag // rows, pl.ds(lag % rows, 1), :] = jnp.zeros((1, D), jnp.float32)
+    lax.fori_loop(0, D // 128, lags_of, 0)
+    near_held[rank] = x_ref[rank]
+    groups.wait(signals)
     near = Trade(
         groups.near_size, rank, groups.near, lambda p: x_ref.at[p], near_held, near_send, near_recv
     )
@@ -420,15 +599,16 @@
         copy.wait_send()
 
 
-def last_step(x, grad, norm, resid, scale, taps, g0, g1, count, collective_id):
+def last_step(signal, grad, norm, resid, scale, taps, g0, g1, count, collective_id):
     far_size = lax.axis_size("dp") * (lax.axis_size("tm") // NEAR)
     length, f32, dma = grad.shape[0], jnp.float32, pltpu.SemaphoreType.DMA
+    sums = jax.ShapeDtypeStruct((NEAR, -(-TAPS // NEAR) + 2, D), f32)
     gradient = jax.ShapeDtypeStruct(g0.shape, g0.dtype)
     vmem, anywhere = pl.BlockSpec(memory_space=pltpu.VMEM), pl.BlockSpec(memory_space=pl.ANY)
     return pl.pallas_call(
         functools.partial(last_kernel, count),
         out_shape=(
-            jax.ShapeDtypeStruct(x.shape, x.dtype),
+            sums,
             jax.ShapeDtypeStruct(grad.shape, jnp.bfloat16),
             gradient,
             gradient,
@@ -436,11 +616,12 @@
         in_specs=[vmem] * 6 + [anywhere] * 2,
         out_specs=[vmem] * 2 + [anywhere] * 2,
         scratch_shapes=[
-            pltpu.VMEM(x.shape, x.dtype),
-            pltpu.VMEM((far_size,) + x.shape[1:], x.dtype),
+            pltpu.VMEM(sums.shape, f32),
+            pltpu.VMEM((far_size,) + sums.shape[1:], f32),
             pltpu.VMEM((2,) + g0.shape, g0.dtype),
             pltpu.VMEM((2, 2, SIDE, D), f32),
             pltpu.VMEM((length + 2 * SIDE, D), f32),
+            pltpu.VMEM(sums.shape, f32),
             dma((NEAR,)),
             dma((NEAR,)),
             dma((far_size,)),
@@ -455,16 +636,16 @@
         compiler_params=pltpu.CompilerParams(
             collective_id=collective_id, has_side_effects=True, vmem_limit_bytes=24 << 20
         ),
-    )(x, grad, norm, resid, scale, taps, g0, g1)
-
-
-CHUNKS = ((2, 0, 1, None), (2, 1, -1, None), (1, 1, 1, None), (3, 0, -1, None), (1, 0, 1, 0), (3, 1, -1, 1), (0, 0, 0, None), (0, 1, 0, None))
-LEAVING = 6
-LAG = 4
+    )(signal, grad, norm, resid, scale, taps, g0, g1)
+
+
+STEPS = (2, 1, 3, 0)
+PART = HALF // 2
 WIDE = 512
-
-
-def experts_kernel(shares, x_ref, u_ref, in_share, out_share, lags_ref, *refs):
+EXTRA = 128
+
+
+def experts_kernel(shares, x_ref, rows_ref, in_share, out_share, lags_ref, *refs):
     o_refs, g_refs, sums_ref, refs = refs[:2], refs[2:4], refs[4], refs[5:]
     (
         rows_x,
@@ -493,23 +674,17 @@
         weight_recv,
         part_send,
         part_recv,
-        own_sem,
-        zin_send,
-        zin_recv,
-        share_send,
-        share_recv,
-        yin_send,
-        yin_recv,
+        load_sem,
         pair_send,
         pair_recv,
         y_send,
         y_recv,
         z_send,
         z_recv,
-    ) = refs
+    ) = refs[:33]
     place, groups = Place(), Groups()
     y, z, core = place.y, place.z, place.core
-    arrays = ((x_ref, rows_x), (u_ref, rows_u))
+    spread = Spread(place, x_ref, rows_x, refs[33:])
     rank = groups.near_rank
     near_held[rank] = lags_ref[rank]
     near = Trade(
@@ -521,9 +696,10 @@
     )
     done = sums_ref.at[rank]
     out = Trade(groups.near_size, rank, groups.near, lambda p: done, sums_ref, out_send, out_recv)
-    waits = []
-
     weights = ((in_share, w_in), (out_share, w_out))
+
+    def load_copy():
+        return pltpu.make_async_copy(rows_ref, rows_u, load_sem.at[0])
 
     def weight_own_copy(i):
         share, held = weights[i]
@@ -549,114 +725,60 @@
                 ).wait_recv()
 
 
-    def zin_copy(a, k):
-        source, rows = arrays[a]
-        target = (z + k) % ZEDS
-        return remote(
-            source.at[target], rows.at[core, y, z], zin_send.at[a, k], zin_recv.at[a, k], place.zed(target)
-        )
-
-    def own_copy(a):
-        source, rows = arrays[a]
-        return pltpu.make_async_copy(source.at[z], rows.at[core, y, z], own_sem.at[a])
-
-    def block(a, from_core, step, k):
-        return arrays[a][1].at[from_core, (y + step + LINES) % LINES, (z - k + ZEDS) % ZEDS]
-
-    def pass_on(a, step, k, send_sem, recv_sem, device):
-        ref = block(a, core, step, k)
-        copy = remote(ref, ref, send_sem, recv_sem, device)
-        copy.start()
-        waits.append(copy)
-
-    def arrived(a, from_core, step, k, send_sem, recv_sem):
-        ref = block(a, from_core, step, k)
-        remote(ref, ref, send_sem, recv_sem, place.sibling()).wait_recv()
-
-    def share(a, step, k):
-        index = step % LINES * ZEDS + k
-        pass_on(a, step, k, share_send.at[a, index], share_recv.at[a, index], place.sibling())
-
-    def spread(a, m):
-        if m < ZEDS:
-            k = SWEEP[m]
-            if k == 0:
-                own_copy(a).wait()
-            else:
-                arrived(a, core, 0, k, zin_send.at[a, k], zin_recv.at[a, k])
-            for way, step in ((0, 1), (1, -1)):
-                pass_on(a, 0, k, yin_send.at[a, way, k], yin_recv.at[a, way, k], place.line(step))
-            share(a, 0, k)
-        if 0 <= m - LAG // 2 < ZEDS:
-            i = m - LAG // 2
-            k = SWEEP[i]
-            for way, step in ((0, 1), (1, -1)):
-                arrived(a, core, -step, k, yin_send.at[a, way, k], yin_recv.at[a, way, k])
-                if i % 2 == way:
-                    pass_on(a, -step, k, yin_send.at[a, 2, k], yin_recv.at[a, 2, k], place.line(step))
-                share(a, -step, k)
-        if 0 <= m - LAG < ZEDS:
-            k = SWEEP[m - LAG]
-            arrived(a, core, 2, k, yin_send.at[a, 2, k], yin_recv.at[a, 2, k])
-            share(a, 2, k)
-
-    def all_shared(a):
-        for step in range(LINES):
-            for k in range(ZEDS):
-                index = step * ZEDS + k
-                arrived(a, 1 - core, step, k, share_send.at[a, index], share_recv.at[a, index])
-
-
-    def chunk_of(ref, i):
-        step, half = CHUNKS[i][:2]
-        return ref.at[:, (y + step) % LINES, pl.ds(half * HALF, HALF)]
+    def chunk_of(ref, step, half, start=0, width=None):
+        width = ref.shape[-1] if width is None else width
+        return ref.at[:, (y + step) % LINES, pl.ds(half * HALF, HALF), :, pl.ds(start, width)]
 
     def flat(value):
         return value.reshape(-1, value.shape[-1])
 
-    def keep(ref, i, value):
-        target = chunk_of(ref, i)
+    def keep(ref, step, half, value):
+        target = chunk_of(ref, step, half)
         target[...] = value.astype(ref.dtype).reshape(target.shape)
 
-    def put(a, i, columns, value):
-        target = results.at[a, i, :, :, :, pl.ds(columns, WIDE)]
+    def put(a, step, half, columns, value):
+        target = results.at[a, step, half, :, :, :, pl.ds(columns, WIDE)]
         target[...] = value.astype(results.dtype).reshape(target.shape)
 
     w_in_rows, w_out_rows = w_in.shape[1] * shares, w_out.shape[1] * shares
 
-    def forward(i):
+    def forward(step, half):
         pre = jnp.dot(
-            flat(chunk_of(rows_x, i)[...]),
+            flat(chunk_of(rows_x, step, half, 0, D)[...]),
             w_in[...].reshape(w_in_rows, -1),
             preferred_element_type=jnp.float32,
         )
-        keep(pre_held, i, pre)
+        keep(pre_held, step, half, pre)
         hidden = (pre * jax.nn.sigmoid(pre)).astype(jnp.bfloat16)
-        keep(hid_held, i, hidden)
+        keep(hid_held, step, half, hidden)
         for columns in range(0, D, WIDE):
-            weights = w_out[:, :, pl.ds(columns, WIDE)].reshape(w_out_rows, WIDE)
-            put(0, i, columns, jnp.dot(hidden, weights, preferred_element_type=jnp.float32))
-        pair_copy(0, i).start()
-
-    def backward(i):
+            block = w_out[:, :, pl.ds(columns, WIDE)].reshape(w_out_rows, WIDE)
+            put(0, step, half, columns, jnp.dot(hidden, block, preferred_element_type=jnp.float32))
+
+    def backward(step, half):
+        gates = flat(chunk_of(rows_x, step, half, D, EXTRA)[...]).astype(jnp.float32)
+        gates = gates[:, :1] + gates[:, EXTRA // 2 : EXTRA // 2 + 1]
+        upstream = flat(chunk_of(rows_u, step, half)[...]).astype(jnp.float32)
+        sent = (upstream * gates).astype(jnp.bfloat16)
+        keep(rows_u, step, half, sent)
         dhidden = lax.dot_general(
-            flat(chunk_of(rows_u, i)[...]),
+            sent,
             w_out[...].reshape(w_out_rows, -1),
             CONTRACT_COLS,
             preferred_element_type=jnp.float32,
         )
-        dpre = (dhidden * swish_slope(flat(chunk_of(pre_held, i)[...]))).astype(jnp.bfloat16)
-        keep(dpre_held, i, dpre)
+        dpre = (dhidden * swish_slope(flat(chunk_of(pre_held, step, half)[...]))).astype(jnp.bfloat16)
+        keep(dpre_held, step, half, dpre)
         weights_all = w_in[...].reshape(w_in_rows, -1)
         for columns in range(0, D, WIDE):
-            weights = weights_all[columns : columns + WIDE]
+            block = weights_all[columns : columns + WIDE]
             put(
                 1,
-                i,
+                step,
+                half,
                 columns,
-                lax.dot_general(dpre, weights, CONTRACT_COLS, preferred_element_type=jnp.float32),
+                lax.dot_general(dpre, block, CONTRACT_COLS, preferred_element_type=jnp.float32),
             )
-        pair_copy(1, i).start()
 
     def part_copy(i, step):
         target = place.other_dp(step)
@@ -700,49 +822,75 @@
         g_refs[i][...] = total.astype(g_refs[i].dtype)
 
 
-    def pair_copy(a, i):
+    def pair_copy(a, step, half):
         return remote(
-            results.at[a, i, 1 - core],
-            pair_held.at[a, i],
-            pair_send.at[a, i],
-            pair_recv.at[a, i],
+            results.at[a, step, half, 1 - core],
+            pair_held.at[a, step, half],
+            pair_send.at[a, step, half],
+            pair_recv.at[a, step, half],
             place.sibling(),
         )
 
-    def y_copy(a, i):
+    def way(step, part):
+        return {2: (1, -1)[part], 1: 1, 3: -1}[step]
+
+    def y_copy(a, step, half, part):
+        blocks = pl.ds(part * PART, PART)
         return remote(
-            results.at[a, i, core],
-            line_held.at[a, i],
-            y_send.at[a, i],
-            y_recv.at[a, i],
-            place.line(CHUNKS[i][2]),
+            results.at[a, step, half, core, blocks],
+            line_held.at[a, step - 1, half, blocks],
+            y_send.at[a, step, half, part],
+            y_recv.at[a, step, half, part],
+            place.line(way(step, part)),
         )
 
     def z_copy(a, target):
-        source = results.at[a, LEAVING + target // HALF, core, target % HALF]
+        source = results.at[a, 0, target // HALF, core, target % HALF]
         return remote(source, o_refs[a].at[z], z_send.at[a, target], z_recv.at[a, z], place.zed(target))
 
-    def settle(a, i, extras):
-        pair_copy(a, i).wait_recv()
+    def settle(a, step, half, part, extras):
         for extra in extras:
-            y_copy(a, extra).wait_recv()
+            y_copy(a, extra, half, part).wait_recv()
 
         def one(j, carry):
-            value = results[a, i, core, j].astype(jnp.float32) + pair_held[a, i, j].astype(jnp.float32)
+            value = results[a, step, half, core, j].astype(jnp.float32)
+            value = value + pair_held[a, step, half, j].astype(jnp.float32)
             for extra in extras:
-                value = value + line_held[a, extra, j].astype(jnp.float32)
-            results[a, i, core, j] = value.astype(results.dtype)
+                value = value + line_held[a, extra - 1, half, j].astype(jnp.float32)
+            results[a, step, half, core, j] = value.astype(results.dtype)
             return carry
 
-        lax.fori_loop(0, HALF, one, 0)
-
-    def leave(a, i):
-        extra = CHUNKS[i][3]
-        settle(a, i, () if extra is None else (extra,))
-        y_copy(a, i).start()
+        lax.fori_loop(part * PART, (part + 1) * PART, one, 0)
+
+    def leave(a, step, half, part, extras=()):
+        settle(a, step, half, part, extras)
+        y_copy(a, step, half, part).start()
+
+    def work(a, half):
+        make = (forward, backward)[a]
+        before = None
+        for step in STEPS:
+            make(step, half)
+            pair_copy(a, step, half).start()
+            if before is not None:
+                pair_copy(a, before, half).wait_recv()
+            if before == 2:
+                leave(a, 2, half, 0)
+                leave(a, 2, half, 1)
+            elif before == 1:
+                leave(a, 1, half, 1)
+            elif before == 3:
+                leave(a, 3, half, 0)
+            before = step
+        pair_copy(a, 0, half).wait_recv()
+
+    def relay(a, half):
+        leave(a, 1, half, 0, (2,))
+        leave(a, 3, half, 1, (2,))
 
     def finish(a, half):
-        settle(a, LEAVING + half, (4, 3) if half == 0 else (2, 5))
+        for part in (1, 0):
+            settle(a, 0, half, part, (1, 3))
         for j in range(HALF):
             target = half * HALF + j
 
@@ -752,51 +900,43 @@
 
             @pl.when(target == z)
             def _():
-                o_refs[a][target] = results[a, LEAVING + half, core, j]
-
-    groups.enter()
-    for a in range(2):
-        own_copy(a).start()
-        for k in SWEEP[1:]:
-            zin_copy(a, k).start()
+                o_refs[a][target] = results[a, 0, half, core, j]
+
+    groups.wait(groups.greet())
+    spread.start()
     for i in range(2):
         weight_own_copy(i).start()
         for step in range(1, shares):
             weight_copy(i, step).start()
-    for m in range(ZEDS + LAG):
-        spread(0, m)
-    all_shared(0)
+    load_copy().start()
+    for m in range(ZEDS):
+        spread.step(m)
+    near.start()
+    for m in range(ZEDS, ZEDS + LAG):
+        spread.step(m)
+    spread.arrive()
     weights_arrive()
-    near.start()
-    for m in range(ZEDS + LAG):
-        spread(1, m)
-        if m < len(CHUNKS):
-            forward(m)
-        if 1 <= m <= 4:
-            leave(0, m - 1)
-    for i in (4, 5):
-        leave(0, i)
-    all_shared(1)
+    load_copy().wait()
+    work(0, 0)
     near.finish()
     far_held[groups.far_rank] = jnp.sum(near_held[...], axis=0)
     far.start()
-    for i in range(len(CHUNKS)):
-        backward(i)
-        if 1 <= i <= 4:
-            leave(1, i - 1)
-        if i == 6:
-            finish(0, 0)
-        if i == 7:
-            finish(0, 1)
+    work(0, 1)
+    relay(0, 0)
     far.finish()
     sums_ref[rank] = jnp.sum(far_held[...], axis=0)
     out.start()
+    work(1, 0)
+    relay(0, 1)
+    finish(0, 0)
+    work(1, 1)
+    relay(1, 0)
     weight_gradient(1, hid_held, rows_u)
-    for i in (4, 5):
-        leave(1, i)
+    finish(0, 1)
+    relay(1, 1)
     weight_gradient(0, dpre_held, rows_x)
-    for half in range(2):
-        finish(1, half)
+    finish(1, 0)
+    finish(1, 1)
     for i in (1, 0):
         gather_gradient(i)
     out.finish()
@@ -806,32 +946,31 @@
             ref = o_refs[a].at[other]
             remote(ref, ref, z_send.at[a, other], z_recv.at[a, other], place.zed(other)).wait_recv()
     for a in range(2):
-        for k in SWEEP[1:]:
-            zin_copy(a, k).wait_send()
-        for i in range(len(CHUNKS)):
-            pair_copy(a, i).wait_send()
-        for i in range(LEAVING):
-            y_copy(a, i).wait_send()
+        for half in range(2):
+            for step in STEPS:
+                pair_copy(a, step, half).wait_send()
+                for part in range(2):
+                    if step != 0:
+                        y_copy(a, step, half, part).wait_send()
         for k in range(1, ZEDS):
             z_copy(a, (z + k) % ZEDS).wait_send()
-    for copy in waits:
-        copy.wait_send()
+    spread.finish()
     for i in range(2):
         for step in range(1, shares):
             weight_copy(i, step).wait_send()
             part_copy(i, step).wait_send()
 
 
-def experts(x, u, in_share, out_share, lags, collective_id):
+def experts(x, rows_u, in_share, out_share, lags, collective_id):
     shares = lax.axis_size("dp")
     hidden = in_share.shape[1]
-    tile = x.shape[1:]
+    slots = x.shape[1]
     lines = (CORES, LINES, ZEDS)
-    chunk = (HALF,) + tile
+    chunk = (HALF, slots, D)
     bf16, f32, dma = jnp.bfloat16, jnp.float32, pltpu.SemaphoreType.DMA
-    out = jax.ShapeDtypeStruct(x.shape, bf16)
+    out = jax.ShapeDtypeStruct((ZEDS, slots, D), bf16)
     gradient = jax.ShapeDtypeStruct((hidden, D // shares), bf16)
-    held = lines + (tile[0], hidden)
+    held = lines + (slots, hidden)
     far_size = shares * (lax.axis_size("tm") // NEAR)
     sems = [
         (NEAR,),
@@ -845,36 +984,32 @@
         (2, shares),
         (2, shares),
         (2, shares),
-        (2,),
+        (1,),
+        (2, LINES, 2),
+        (2, LINES, 2),
+        (2, LINES, 2, 2),
+        (2, LINES, 2, 2),
         (2, ZEDS),
         (2, ZEDS),
-        (2, LINES * ZEDS),
-        (2, LINES * ZEDS),
-        (2, 3, ZEDS),
-        (2, 3, ZEDS),
-        (2, len(CHUNKS)),
-        (2, len(CHUNKS)),
-        (2, LEAVING),
-        (2, LEAVING),
-        (2, ZEDS),
-        (2, ZEDS),
+        *Spread.SEMS,
     ]
+    vmem, anywhere = pl.BlockSpec(memory_space=pltpu.VMEM), pl.BlockSpec(memory_space=pl.ANY)
     return pl.pallas_call(
         functools.partial(experts_kernel, shares),
         out_shape=(out, out, gradient, gradient, jax.ShapeDtypeStruct(lags.shape, lags.dtype)),
-        in_specs=[pl.BlockSpec(memory_space=pl.ANY)] * 4 + [pl.BlockSpec(memory_space=pltpu.VMEM)],
-        out_specs=[pl.BlockSpec(memory_space=pltpu.VMEM)] * 5,
+        in_specs=[anywhere] * 4 + [vmem],
+        out_specs=[vmem] * 5,
         scratch_shapes=[
-            pltpu.VMEM(lines + tile, bf16),
-            pltpu.VMEM(lines + tile, bf16),
+            pltpu.VMEM(lines + x.shape[1:], bf16),
+            pltpu.VMEM(lines + (slots, D), bf16),
             pltpu.VMEM((shares,) + in_share.shape, bf16),
             pltpu.VMEM((shares,) + out_share.shape, bf16),
             pltpu.VMEM(held, f32),
             pltpu.VMEM(held, bf16),
             pltpu.VMEM(held, bf16),
-            pltpu.VMEM((2, len(CHUNKS), CORES) + chunk, bf16),
-            pltpu.VMEM((2, len(CHUNKS)) + chunk, bf16),
-            pltpu.VMEM((2, LEAVING) + chunk, bf16),
+            pltpu.VMEM((2, LINES, 2, CORES) + chunk, bf16),
+            pltpu.VMEM((2, LINES, 2) + chunk, bf16),
+            pltpu.VMEM((2, LINES - 1, 2) + chunk, bf16),
             pltpu.VMEM((hidden, D), f32),
             pltpu.VMEM((2, shares) + gradient.shape, bf16),
             pltpu.VMEM((2, shares) + gradient.shape, bf16),
@@ -883,9 +1018,9 @@
         ]
         + [dma(shape) for shape in sems],
         compiler_params=pltpu.CompilerParams(
-            collective_id=collective_id, has_side_effects=True, vmem_limit_bytes=58 << 20
+            collective_id=collective_id, has_side_effects=True, vmem_limit_bytes=60 << 20
         ),
-    )(x, u, in_share, out_share, lags)
+    )(x, rows_u, in_share, out_share, lags)
 
 
 def body(
@@ -900,17 +1035,30 @@
     cotangent,
 ):
     length = frames.shape[1]
-    half = TAPS // 2
     element_count = lax.axis_size("dp") * lax.axis_size("tm") * length
     capacity = length * TOP // EXPERTS
+    ids = choices[0]
+    onehot = (ids[:, :, None] == jnp.arange(EXPERTS, dtype=jnp.int32)[None, None, :]).astype(
+        jnp.float32
+    )
+    flat_ids = ids.reshape(-1)
+    expert_hot = (flat_ids[:, None] == jnp.arange(EXPERTS, dtype=jnp.int32)[None, :]).astype(
+        jnp.int32
+    )
+    slots = jnp.sum((jnp.cumsum(expert_hot, axis=0) - 1) * expert_hot, axis=1)
+    places = (position(flat_ids) * capacity + slots).reshape(length, TOP)
+    place_hot = places[:, :, None] == jnp.arange(EXPERTS * capacity, dtype=jnp.int32)[None, None, :]
+    place_any = jnp.any(place_hot, axis=1).astype(jnp.bfloat16)
+    place_hot = place_hot.astype(jnp.float32)
+
+    def bucketed(rows):
+        return lax.dot_general(place_any, rows, CONTRACT_ROWS, preferred_element_type=jnp.float32)
+
+    up_buffer = bucketed(cotangent[0]).astype(jnp.bfloat16).reshape(EXPERTS, capacity, D)
+    moments, conv, wide, lags, w_in_share, w_out_share, rows_u = first_step(
+        frames[0], taps, w_in, w_out, up_buffer, 0
+    )
     signal = frames[0].astype(jnp.float32)
-    rimmed = extended(frames, (("tm", 1),), half)[0].astype(jnp.float32)
-    conv = conv_lags(rimmed, taps, length, False)
-    local_mean = jnp.sum(conv, axis=0) / length
-    local_spread = conv - local_mean
-    moments, w_in_share, w_out_share = moments_and_weights(
-        jnp.stack([local_mean, jnp.sum(local_spread * local_spread, axis=0)]), length, w_in, w_out, 0
-    )
     mean, variance = moments[0], moments[1] / element_count
     centered_values = conv - mean
     inverse_deviation = lax.rsqrt(variance + EPS)
@@ -922,34 +1070,18 @@
     vhat = lcent * lrstd
     normed = vhat.astype(jnp.bfloat16)
     logits = jnp.dot(normed, w_router, preferred_element_type=jnp.float32)
-    ids = choices[0]
-    onehot = (ids[:, :, None] == jnp.arange(EXPERTS, dtype=jnp.int32)[None, None, :]).astype(
-        jnp.float32
-    )
     picked = jnp.sum(onehot * logits[:, None, :], axis=-1)
     first = jax.nn.sigmoid(picked[:, 0] - picked[:, 1])
     gates = jnp.stack([first, 1.0 - first], axis=1)
-    flat_ids = ids.reshape(-1)
-    expert_hot = (flat_ids[:, None] == jnp.arange(EXPERTS, dtype=jnp.int32)[None, :]).astype(
-        jnp.int32
-    )
-    slots = jnp.sum((jnp.cumsum(expert_hot, axis=0) - 1) * expert_hot, axis=1)
-    places = (position(flat_ids) * capacity + slots).reshape(length, TOP)
-    place_hot = places[:, :, None] == jnp.arange(EXPERTS * capacity, dtype=jnp.int32)[None, None, :]
-    place_any = jnp.any(place_hot, axis=1).astype(jnp.bfloat16)
-    place_hot = place_hot.astype(jnp.float32)
     gate_rows = jnp.sum(place_hot * gates[:, :, None], axis=(0, 1))
 
-    def bucketed(rows):
-        return lax.dot_general(place_any, rows, CONTRACT_ROWS, preferred_element_type=jnp.float32)
-
-    buffer = bucketed(normed).astype(jnp.bfloat16).reshape(EXPERTS, capacity, D)
-    sent_buffer = (gate_rows[:, None] * bucketed(cotangent[0])).astype(jnp.bfloat16)
-    sent_buffer = sent_buffer.reshape(EXPERTS, capacity, D)
-    signal_lags = [jnp.sum(rimmed[lag : lag + length], axis=0) for lag in range(TAPS)]
-    lags = by_rank(signal_lags + lag_sums(normalized_input, rimmed))
+    gate_high = lax.reduce_precision(gate_rows, 8, 7)
+    gate_parts = jnp.stack([gate_high, gate_rows - gate_high], axis=1).astype(jnp.bfloat16)
+    buffer = jnp.concatenate(
+        [bucketed(normed).astype(jnp.bfloat16), jnp.repeat(gate_parts, EXTRA // 2, axis=1)], axis=1
+    ).reshape(EXPERTS, capacity, D + EXTRA)
     combined, back, grad_in_local, grad_out_local, lags = experts(
-        buffer, sent_buffer, w_in_share, w_out_share, lags, 1
+        buffer, rows_u, w_in_share, w_out_share, lags, 1
     )
     combined = combined.reshape(EXPERTS * capacity, D).astype(jnp.float32)
     back = back.reshape(EXPERTS * capacity, D).astype(jnp.float32)
@@ -967,21 +1099,8 @@
     dproj = jnp.mean(dnormed * vhat, axis=-1, keepdims=True)
     dresid = upstream + lrstd * (dnormed - dmean - vhat * dproj)
     normalized_gradient = dresid * swish_slope(before_activation) * batchnorm_gain_scale
-    moment_rows = jnp.stack(
-        [
-            jnp.sum(normalized_gradient, axis=0),
-            jnp.sum(normalized_gradient * normalized_input, axis=0),
-        ]
-    )
-    to_sum = jnp.concatenate(
-        [
-            by_rank(lag_sums(normalized_gradient, rimmed)),
-            jnp.broadcast_to(moment_rows[None], (NEAR,) + moment_rows.shape),
-        ],
-        axis=1,
-    )
     summed, grad_frames, grad_w_in, grad_w_out = last_step(
-        to_sum,
+        wide,
         normalized_gradient,
         normalized_input,
         dresid,

time: 286 us -> 252 us (0.88); the launches traced: 281 us -> 252 us
  other arithmetic: 18.7 us -> 7.22 us
  starting transfers between devices: 6.86 us -> 0 us
  local copies, waits for them, and re-layouts: 17.1 us -> 11.4 us
  Pallas kernels: 229 us -> 225 us
    pallas_call x1, Pallas kernels: 148 us -> 126 us  [experts(): pl.pallas_call(functools.partial(experts_kernel, shares), out_shape=(out,...]
    pallas_call x2, Pallas kernels: 81.4 us -> 99.2 us  [the longest x1 57.2 us: first_step(): pl.pallas_call(first_kernel, out_shape=(jax.ShapeDtypeStruct((2, D), f32)...]
    reduce_sum x8 -> x1, other arithmetic: 13.8 us -> 0.4 us  [body(): lcent = resid - jnp.mean(resid, axis=-1, keepdims=True)]
    ppermute x2 -> x0, starting transfers between devices: 6.86 us -> none  [the longest x1 4.94 us: extended(): lax.ppermute(lax.slice_in_dim(block, block.shape[dim] - width, None, axis...]
    slice x4 -> x1, local copies, waits for them, and re-layouts: 4.73 us -> 0.21 us  [the longest x2 3.63 us: conv_lags(): total = total + taps[lag] * rimmed[start:start + length]]
    unnamed x43 -> x39, local copies, waits for them, and re-layouts: 7.91 us -> 8.75 us
  transfers between devices with their start and end apart: 2 -> 0, of which waited for: 0 -> 0; matrix products, arithmetic and copies ran while one was open for 3% -> 0% of each run, Pallas kernels for 0% -> 0%
where the time goes in v5:
time: 252 us
  Pallas kernels  225 us (89%)
  local copies, waits for them, and re-layouts  11.4 us (5%)
  other arithmetic  7.22 us (3%)
  matrix products  6.86 us (3%)
    pallas_call x1, Pallas kernels, experts(): pl.pallas_call(functools.partial(experts_kernel, shares), out_shape=(out,...  126 us
    pallas_call x1, Pallas kernels, first_step(): pl.pallas_call(first_kernel, out_shape=(jax.ShapeDtypeStruct((2, D), f32)...  57.2 us
    pallas_call x1, Pallas kernels, last_step(): pl.pallas_call(functools.partial(last_kernel, count), out_shape=(sums, ja...  41.9 us
    unnamed x39, local copies, waits for them, and re-layouts  8.75 us

profile of v5, /device:TPU:1, one launch (start us, length us, event | category | flops | bytes accessed | tf_op | source)
XLA Modules:
  0.0 251.9 jit_solution(16423217869923494543)
XLA Ops:
  0.7 0.9 copy.33
  1.7 0.6 reduce-window.6
  3.0 0.7 multiply_add_fusion.2
  3.9 1.4 convolution_convert_fusion.1
  5.3 1.3 copy-done.4
  6.6 0.9 copy-done.5
  7.5 57.2 %shard_map.128 = (f32[2,1536]{1,0:T(2,128)S(1)}, f32[128,1536]{1,0:T(8,128)S(1)}, f32[160,1536]{1,0:T(8,128)S(1)}, f32[16,4,1536]{2,1,0:T(4,128)S(1)}, bf16[384,...) custom-call(bf16[128,1536]{1,0:T(8,128)(2,1)S(1)} %bitcast.63, ...), custom_call_target="tpu_custom_call" | custom-call | tf_op jit(solution)/shard_map/pallas_call | solution.py:433
  64.7 2.7 %copy-done.1 = bf16[2,4,8,32,1536]{4,3,2,1,0:T(8,128)(2,1)} copy-done((bf16[2,4,8,32,1536]{4,3,2,1,0:T(8,128)(2,1)}, bf16[2,4,8,32,1536]{4,3,2,1,0:T(8,128)(2,1)S(1)}, u32[]{:S(2)}) %copy-start.1) | copy-done | bytes 6291480
  67.4 0.7 copy-done.9
  68.2 0.4 fusion.27
  69.1 1.3 convolution_convert_fusion
  71.4 2.1 pad_maximum_fusion.x_ref
  73.5 126.3 %shard_map.129 = (bf16[8,32,1536]{2,1,0:T(8,128)(2,1)}, bf16[8,32,1536]{2,1,0:T(8,128)(2,1)}, bf16[384,384]{1,0:T(8,128)(2,1)}, bf16[384,384]{1,0:T(8,128)(2,1)}, f32[16,4,1536]{2,1,0:T(4,128)}) custom-call(bf16[8,32,1664]{2,1,0:T(8,128)(2,1)} %pad_maximum_fusion.x_ref, bf16[2,4,8,32,1536]{4,3,2,1,0:T(8,128)(2,1)} %copy-done.1, bf16[384,384]{1,0:T(8,128)(2,1)} %copy-done.8, ...), custom_call_target="tpu_custom_call" | custom-call | tf_op jit(solution)/shard_map/pallas_call | solution.py:997
  199.9 1.5 fusion.9
  201.4 1.3 fusion.1
  202.7 0.5 fusion.16
  203.2 0.7 fusion.26
  204.0 0.8 multiply_multiply_fusion
  205.1 41.9 %shard_map.130 = (f32[16,4,1536]{2,1,0:T(4,128)S(1)}, bf16[128,1536]{1,0:T(8,128)(2,1)S(1)}, bf16[384,384]{1,0:T(8,128)(2,1)S(1)}, bf16[384,384]{1,0:T(8,128)(2,1)S(1)}) custom-call(f32[160,1536]{1,0:T(8,128)S(1)} %get-tuple-element.28.signal_ref, f32[128,1536]{1,0:T(8,128)S(1)} %get-tuple-element.65.grad_ref, f32[128,1536]{1,0:T(8,128)S(1)} %get-tuple-element.71.norm_ref, ...), custom_call_target="tpu_custom_call" | custom-call | tf_op jit(solution)/shard_map/pallas_call | solution.py:608
  247.3 1.1 reshape.176
  248.5 0.7 fusion.7
  249.2 1.1 copy.37
  250.3 0.9 convert_element_type.54
  251.2 0.7 copy.40
  (65 shorter events, 3.2 us)
Async XLA Ops:
  0.6 69.7 %copy-start = (bf16[1536,8]{0,1:T(8,128)(2,1)S(1)}, bf16[1536,8]{0,1:T(8,128)(2,1)}, u32[]{:S(2)}) copy-start(bf16[1536,8]{0,1:T(8,128)(2,1)} %param.13) | copy-start | bytes 73732
  0.6 4.6 %copy-start.2 = (bf16[1,128,1536]{2,1,0:T(8,128)(2,1)S(1)}, bf16[1,128,1536]{2,1,0:T(8,128)(2,1)}, u32[]{:S(2)}) copy-start(bf16[1,128,1536]{2,1,0:T(8,128)(2,1)} %param.9) | copy-start | bytes 1179652
  0.7 4.6 %copy-start.3 = (bf16[1536,384]{1,0:T(8,128)(2,1)S(1)}, bf16[1536,384]{1,0:T(8,128)(2,1)}, u32[]{:S(2)}) copy-start(bf16[1536,384]{1,0:T(8,128)(2,1)} %w_in_ref.1) | copy-start | bytes 3538948
  5.3 1.3 copy-start.4
  6.6 0.9 copy-start.5
  7.5 60.7 %copy-start.15 = (f32[1536]{0:T(1024)S(1)}, f32[1536]{0:T(1024)}, u32[]{:S(2)}) copy-start(f32[1536]{0:T(1024)} %param.12) | copy-start | bytes 18436
  7.5 60.7 %copy-start.16 = (f32[1536]{0:T(1024)S(1)}, f32[1536]{0:T(1024)}, u32[]{:S(2)}) copy-start(f32[1536]{0:T(1024)} %param.11) | copy-start | bytes 18436
  64.7 2.7 %copy-start.1 = (bf16[2,4,8,32,1536]{4,3,2,1,0:T(8,128)(2,1)}, bf16[2,4,8,32,1536]{4,3,2,1,0:T(8,128)(2,1)S(1)}, u32[]{:S(2)}) copy-start(bf16[2,4,8,32,1536]{4,3,2,1,0:T(8,128)(2,1)S(1)} %get-tuple-element.23.rows_ref) | copy-start | bytes 18874372
  67.4 0.7 copy-start.9
  68.1 0.7 copy-start.7
  68.1 0.8 copy-start.8
  68.6 2.0 copy-start.17
  199.9 1.5 copy-start.12
  199.9 1.5 copy-start.13
  201.4 1.8 copy-start.14
  204.0 0.9 copy-start.6
  204.0 1.1 copy-start.10
  204.0 1.1 copy-start.11

commit v6 on v5

--- a/solution.py
+++ b/solution.py
@@ -289,178 +289,6 @@
             self.z_copy(k).wait_send()
         for copy in self.waits:
             copy.wait_send()
-
-
-def first_kernel(
-    frames_ref,
-    taps_ref,
-    w_in_ref,
-    w_out_ref,
-    u_ref,
-    o_ref,
-    conv_ref,
-    wide_ref,
-    lags_ref,
-    w_in_share,
-    w_out_share,
-    rows_ref,
-    near_held,
-    far_held,
-    w_in_mid,
-    w_out_mid,
-    rims,
-    near_send,
-    near_recv,
-    far_send,
-    far_recv,
-    y_sems,
-    z_sems,
-    rim_send,
-    rim_recv,
-    *spread_sems,
-):
-    groups, place = Groups(), Place()
-    length = frames_ref.shape[0]
-    tm, tm_size = groups.tm, lax.axis_size("tm")
-    after, before = (groups.dp, (tm + 1) % tm_size), (groups.dp, (tm + tm_size - 1) % tm_size)
-    spread = Spread(place, u_ref, rows_ref, spread_sems)
-    line = work_line(place)
-    zed = place.z // HALF * HALF + home_line(place)
-    y_hops, z_hops = [], []
-    cargo = ((w_in_ref, w_in_mid, w_in_share), (w_out_ref, w_out_mid, w_out_share))
-    for i, (source, mid, share) in enumerate(cargo):
-        depth = share.shape[0]
-        mine = source.at[pl.ds(pl.multiple_of(place.dp * depth, depth), depth)]
-        y_hops.append(Hop(mine, mid, line == place.y, place.at(line, place.z, place.core), y_sems.at[i]))
-        z_hops.append(Hop(mid, share, zed == place.z, place.zed(zed), z_sems.at[i]))
-    rim_copies = [
-        remote(
-            frames_ref.at[pl.ds(rows, SIDE)], rims.at[side], rim_send.at[side], rim_recv.at[side], device
-        )
-        for side, rows, device in ((0, length - SIDE, after), (1, 0, before))
-    ]
-    mine = near_held.at[groups.near_rank]
-    near = Trade(
-        groups.near_size, groups.near_rank, groups.near, lambda p: mine, near_held, near_send, near_recv
-    )
-    mine_far = far_held.at[groups.far_rank]
-    far = Trade(
-        groups.far_size, groups.far_rank, groups.far, lambda p: mine_far, far_held, far_send, far_recv
-    )
-    groups.wait(groups.greet((after, before)))
-    for copy in rim_copies:
-        copy.start()
-    spread.start()
-    for hop in y_hops:
-        hop.start()
-    wide_ref[pl.ds(SIDE, length)] = frames_ref[...].astype(jnp.float32)
-    for copy in rim_copies:
-        copy.wait_recv()
-    for side, rows, edge in ((0, 0, tm == 0), (1, SIDE + length, tm == tm_size - 1)):
-        wide_ref[pl.ds(rows, SIDE)] = jnp.where(edge, 0.0, rims[side].astype(jnp.float32))
-
-    def columns_of(j, carry):
-        columns = pl.ds(pl.multiple_of(j * 128, 128), 128)
-        value = jnp.zeros((length, 128), jnp.float32)
-        for lag in range(TAPS):
-            start = SIDE - TAPS // 2 + lag
-            value = value + taps_ref[pl.ds(lag, 1), columns] * wide_ref[pl.ds(start, length), columns]
-        conv_ref[:, columns] = value
-        mean = jnp.sum(value, axis=0, keepdims=True) / length
-        spread_out = value - mean
-        near_held[groups.near_rank, pl.ds(0, 1), columns] = mean
-        near_held[groups.near_rank, pl.ds(1, 1), columns] = jnp.sum(
-            spread_out * spread_out, axis=0, keepdims=True
-        )
-        return carry
-
-    def lags_of(j, carry):
-        columns = pl.ds(pl.multiple_of(j * 128, 128), 128)
-        mean = near_held[groups.near_rank, pl.ds(0, 1), columns]
-        value = conv_ref[:, columns] - mean
-        for lag in range(TAPS):
-            shifted = wide_ref[pl.ds(SIDE - TAPS // 2 + lag, length), columns]
-            place_row(lags_ref, lag, columns, jnp.sum(shifted, axis=0, keepdims=True))
-            place_row(lags_ref, TAPS + lag, columns, jnp.sum(value * shifted, axis=0, keepdims=True))
-        return carry
-
-    tiles = frames_ref.shape[1] // 128
-    for m in range(3):
-        spread.step(m)
-        lax.fori_loop(m * tiles // 3, (m + 1) * tiles // 3, columns_of, 0)
-    near.start()
-    zeros = jnp.zeros((1, D), jnp.float32)
-    for row in range(2 * TAPS, lags_ref.shape[0] * lags_ref.shape[1]):
-        place_row(lags_ref, row, pl.ds(0, D), zeros)
-    for m in range(3, 6):
-        spread.step(m)
-        lax.fori_loop((m - 3) * tiles // 3, (m - 2) * tiles // 3, lags_of, 0)
-    near.finish()
-    far_held[groups.far_rank] = moments_merge(near_held[...], float(length))
-    far.start()
-    for m in range(6, 8):
-        spread.step(m)
-    for y_hop, z_hop in zip(y_hops, z_hops):
-        y_hop.finish()
-        z_hop.start()
-    far.finish()
-    moments = moments_merge(far_held[...], float(length * groups.near_size))
-    o_ref[...] = moments
-    scale = lax.rsqrt(moments[1:] / (length * groups.near_size * groups.far_size) + EPS)
-    shift = near_held[groups.near_rank, pl.ds(0, 1), :] - moments[:1]
-    for lag in range(TAPS):
-        value = row_of(lags_ref, TAPS + lag) + shift * row_of(lags_ref, lag)
-        place_row(lags_ref, TAPS + lag, pl.ds(0, D), scale * value)
-    for m in range(8, ZEDS + LAG):
-        spread.step(m)
-    spread.arrive()
-    for hop in z_hops:
-        hop.finish()
-    for copy in rim_copies:
-        copy.wait_send()
-    spread.finish()
-
-
-def first_step(frames, taps, w_in, w_out, u, collective_id):
-    dp_size = lax.axis_size("dp")
-    far_size = dp_size * (lax.axis_size("tm") // NEAR)
-    shares = [
-        jax.ShapeDtypeStruct((w.shape[0] // dp_size, w.shape[1]), w.dtype) for w in (w_in, w_out)
-    ]
-    f32, dma = jnp.float32, pltpu.SemaphoreType.DMA
-    length = frames.shape[0]
-    vmem, anywhere = pl.BlockSpec(memory_space=pltpu.VMEM), pl.BlockSpec(memory_space=pl.ANY)
-    return pl.pallas_call(
-        first_kernel,
-        out_shape=(
-            jax.ShapeDtypeStruct((2, D), f32),
-            jax.ShapeDtypeStruct((length, D), f32),
-            jax.ShapeDtypeStruct((length + 2 * SIDE, D), f32),
-            jax.ShapeDtypeStruct((NEAR, -(-2 * TAPS // NEAR), D), f32),
-            *shares,
-            jax.ShapeDtypeStruct((CORES, LINES) + u.shape, u.dtype),
-        ),
-        in_specs=[vmem] * 2 + [anywhere] * 3,
-        out_specs=[vmem] * 4 + [anywhere] * 3,
-        scratch_shapes=[
-            pltpu.VMEM((NEAR, 2, D), f32),
-            pltpu.VMEM((far_size, 2, D), f32),
-            *[pltpu.VMEM(share.shape, share.dtype) for share in shares],
-            pltpu.VMEM((2, SIDE, D), frames.dtype),
-            dma((NEAR,)),
-            dma((NEAR,)),
-            dma((far_size,)),
-            dma((far_size,)),
-            dma((2, 3)),
-            dma((2, 3)),
-            dma((2,)),
-            dma((2,)),
-            *[dma(shape) for shape in Spread.SEMS],
-        ],
-        compiler_params=pltpu.CompilerParams(
-            collective_id=collective_id, has_side_effects=True, vmem_limit_bytes=24 << 20
-        ),
-    )(frames, taps, w_in, w_out, u)
 
 
 def last_kernel(
@@ -645,84 +473,172 @@
 EXTRA = 128
 
 
-def experts_kernel(shares, x_ref, rows_ref, in_share, out_share, lags_ref, *refs):
-    o_refs, g_refs, sums_ref, refs = refs[:2], refs[2:4], refs[4], refs[5:]
-    (
-        rows_x,
-        rows_u,
-        w_in,
-        w_out,
-        pre_held,
-        hid_held,
-        dpre_held,
-        results,
-        pair_held,
-        line_held,
-        gradient,
-        parting,
-        parts,
-        near_held,
-        far_held,
-        near_send,
-        near_recv,
-        far_send,
-        far_recv,
-        out_send,
-        out_recv,
-        weight_own,
-        weight_send,
-        weight_recv,
-        part_send,
-        part_recv,
-        load_sem,
-        pair_send,
-        pair_recv,
-        y_send,
-        y_recv,
-        z_send,
-        z_recv,
-    ) = refs[:33]
+def main_kernel(shares, *refs):
+    refs = list(refs)
+
+    def take(count):
+        taken = refs[:count]
+        del refs[:count]
+        return taken
+
+    frames_ref, taps_ref, gain_ref, bias_ref, router_ref, choose_ref, hot_ref = take(7)
+    w_in_ref, w_out_ref, u_ref = take(3)
+    o_refs, g_refs = take(2), take(2)
+    sums_ref, moments_ref, wide_ref, norm_ref, resid_ref, vhat_ref, lrstd_ref, gate_ref = take(8)
+    x_ref, normed, w_in_mid, w_out_mid, in_share, out_share, rims, lags_ref = take(8)
+    rows_x, rows_u, w_in, w_out, hid_held, dpre_held, results, pair_held, line_held = take(9)
+    gradient, parting, parts, near_held, far_held, near_moments, far_moments = take(7)
+    near_send, near_recv, far_send, far_recv, out_send, out_recv = take(6)
+    near_moments_send, near_moments_recv, far_moments_send, far_moments_recv = take(4)
+    yhop_sems, zhop_sems, rim_send, rim_recv = take(4)
+    weight_own, weight_send, weight_recv, part_send, part_recv = take(5)
+    pair_send, pair_recv, y_send, y_recv, z_send, z_recv = take(6)
     place, groups = Place(), Groups()
     y, z, core = place.y, place.z, place.core
-    spread = Spread(place, x_ref, rows_x, refs[33:])
+    spread_u = Spread(place, u_ref, rows_u, take(len(Spread.SEMS)))
+    spread_x = Spread(place, x_ref, rows_x, take(len(Spread.SEMS)))
+    length = frames_ref.shape[0]
+    count = length * groups.near_size * groups.far_size
+    tm, tm_size = groups.tm, lax.axis_size("tm")
+    after, before_me = (groups.dp, (tm + 1) % tm_size), (groups.dp, (tm + tm_size - 1) % tm_size)
+
+    line = work_line(place)
+    zed = z // HALF * HALF + home_line(place)
+    y_hops, z_hops = [], []
+    cargo = ((w_in_ref, w_in_mid, in_share), (w_out_ref, w_out_mid, out_share))
+    for i, (source, mid, share) in enumerate(cargo):
+        depth = share.shape[0]
+        part = source.at[pl.ds(pl.multiple_of(place.dp * depth, depth), depth)]
+        y_hops.append(Hop(part, mid, line == y, place.at(line, z, core), yhop_sems.at[i]))
+        z_hops.append(Hop(mid, share, zed == z, place.zed(zed), zhop_sems.at[i]))
+    rim_copies = [
+        remote(
+            frames_ref.at[pl.ds(rows, SIDE)], rims.at[side], rim_send.at[side], rim_recv.at[side], device
+        )
+        for side, rows, device in ((0, length - SIDE, after), (1, 0, before_me))
+    ]
+
+    def trades(near_ref, far_ref, source, sems):
+        mine = far_ref.at[groups.far_rank]
+        return (
+            Trade(groups.near_size, groups.near_rank, groups.near, source, near_ref, *sems[:2]),
+            Trade(groups.far_size, groups.far_rank, groups.far, lambda p: mine, far_ref, *sems[2:]),
+        )
+
     rank = groups.near_rank
-    near_held[rank] = lags_ref[rank]
-    near = Trade(
-        groups.near_size, rank, groups.near, lambda p: lags_ref.at[p], near_held, near_send, near_recv
-    )
-    mine = far_held.at[groups.far_rank]
-    far = Trade(
-        groups.far_size, groups.far_rank, groups.far, lambda p: mine, far_held, far_send, far_recv
-    )
+    mine_near = near_moments.at[rank]
+    moment_sems = (near_moments_send, near_moments_recv, far_moments_send, far_moments_recv)
+    moment_near, moment_far = trades(near_moments, far_moments, lambda p: mine_near, moment_sems)
+    lag_sems = (near_send, near_recv, far_send, far_recv)
+    near, far = trades(near_held, far_held, lambda p: lags_ref.at[p], lag_sems)
     done = sums_ref.at[rank]
     out = Trade(groups.near_size, rank, groups.near, lambda p: done, sums_ref, out_send, out_recv)
     weights = ((in_share, w_in), (out_share, w_out))
 
-    def load_copy():
-        return pltpu.make_async_copy(rows_ref, rows_u, load_sem.at[0])
+
+    def conv_of(j, carry):
+        columns = pl.ds(pl.multiple_of(j * 128, 128), 128)
+        value = jnp.zeros((length, 128), jnp.float32)
+        for lag in range(TAPS):
+            start = SIDE - TAPS // 2 + lag
+            value = value + taps_ref[pl.ds(lag, 1), columns] * wide_ref[pl.ds(start, length), columns]
+        norm_ref[:, columns] = value
+        mean = jnp.sum(value, axis=0, keepdims=True) / length
+        centred = value - mean
+        near_moments[rank, pl.ds(0, 1), columns] = mean
+        near_moments[rank, pl.ds(1, 1), columns] = jnp.sum(centred * centred, axis=0, keepdims=True)
+        return carry
+
+    def lags_of(j, carry):
+        columns = pl.ds(pl.multiple_of(j * 128, 128), 128)
+        value = norm_ref[:, columns] - near_moments[rank, pl.ds(0, 1), columns]
+        for lag in range(TAPS):
+            shifted = wide_ref[pl.ds(SIDE - TAPS // 2 + lag, length), columns]
+            place_row(lags_ref, lag, columns, jnp.sum(shifted, axis=0, keepdims=True))
+            place_row(lags_ref, TAPS + lag, columns, jnp.sum(value * shifted, axis=0, keepdims=True))
+        return carry
+
+    def normalize(j, carry):
+        rows = pl.ds(pl.multiple_of(j * SIDE, SIDE), SIDE)
+        norm = (norm_ref[rows] - moments_ref[:1]) * lax.rsqrt(moments_ref[1:] / count + EPS)
+        norm_ref[rows] = norm
+        pre = norm * gain_ref[...] + bias_ref[...]
+        resid = frames_ref[rows].astype(jnp.float32) + pre * jax.nn.sigmoid(pre)
+        resid_ref[rows] = resid
+        centred = resid - jnp.mean(resid, axis=-1, keepdims=True)
+        lrstd = lax.rsqrt(jnp.mean(centred * centred, axis=-1, keepdims=True) + EPS)
+        lrstd_ref[rows] = jnp.broadcast_to(lrstd, (SIDE, EXTRA))
+        vhat = centred * lrstd
+        vhat_ref[rows] = vhat
+        normed[rows] = vhat.astype(jnp.bfloat16)
+        return carry
+
+    def bucket():
+        logits = jnp.dot(normed[...], router_ref[...], preferred_element_type=jnp.float32)
+        first = jax.nn.sigmoid(jnp.sum(logits * choose_ref[...], axis=-1, keepdims=True))
+        gate_ref[...] = jnp.broadcast_to(first, gate_ref.shape)
+        gates = jnp.zeros((hot_ref.shape[2], EXTRA), jnp.float32)
+        for k, gate in enumerate((first, 1.0 - first)):
+            high = gate.astype(jnp.bfloat16)
+            low = (gate - high.astype(jnp.float32)).astype(jnp.bfloat16)
+            wide_gate = jnp.concatenate(
+                [jnp.broadcast_to(half, (length, EXTRA // 2)) for half in (high, low)], axis=1
+            )
+            gates = gates + lax.dot_general(
+                hot_ref[k], wide_gate, CONTRACT_ROWS, preferred_element_type=jnp.float32
+            )
+        x_ref[:, :, pl.ds(D, EXTRA)] = gates.astype(jnp.bfloat16).reshape(ZEDS, -1, EXTRA)
+        either = hot_ref[0] + hot_ref[1]
+        for columns in range(0, D, WIDE):
+            value = lax.dot_general(
+                either,
+                normed[:, pl.ds(columns, WIDE)],
+                CONTRACT_ROWS,
+                preferred_element_type=jnp.float32,
+            )
+            x_ref[:, :, pl.ds(columns, WIDE)] = value.astype(jnp.bfloat16).reshape(ZEDS, -1, WIDE)
 
     def weight_own_copy(i):
         share, held = weights[i]
         return pltpu.make_async_copy(share, held.at[place.dp], weight_own.at[i])
 
+    ways = (1, shares - 1)
+
     def weight_copy(i, step):
         share, held = weights[i]
+        if step == 2:
+            origin, step_to = place.other_dp(-ways[i]), ways[i]
+            source, slot = held.at[origin], origin
+        else:
+            source, slot, step_to = share, place.dp, step
         return remote(
-            share,
-            held.at[place.dp],
+            source,
+            held.at[slot],
             weight_send.at[i, step],
             weight_recv.at[i, step],
-            place.on_dp(place.other_dp(step)),
-        )
+            place.on_dp(place.other_dp(step_to)),
+        )
+
+    def weight_arrives(i, step):
+        ref = weights[i][1].at[place.other_dp(-step)]
+        remote(ref, ref, weight_send.at[i, step], weight_recv.at[i, step], place.sibling()).wait_recv()
+
+    def weights_start():
+        for i in range(2):
+            weight_own_copy(i).start()
+            for step in ways:
+                weight_copy(i, step).start()
+
+    def weights_relay():
+        for i in range(2):
+            weight_arrives(i, ways[i])
+            weight_copy(i, 2).start()
 
     def weights_arrive():
-        for i, (_, held) in enumerate(weights):
+        for i in range(2):
             weight_own_copy(i).wait()
-            for step in range(1, shares):
-                ref = held.at[place.other_dp(-step)]
-                remote(
-                    ref, ref, weight_send.at[i, step], weight_recv.at[i, step], place.sibling()
-                ).wait_recv()
+            weight_arrives(i, ways[1 - i])
+            weight_arrives(i, 2)
 
 
     def chunk_of(ref, step, half, start=0, width=None):
@@ -742,13 +658,15 @@
 
     w_in_rows, w_out_rows = w_in.shape[1] * shares, w_out.shape[1] * shares
 
-    def forward(step, half):
-        pre = jnp.dot(
+    def pre_of(step, half):
+        return jnp.dot(
             flat(chunk_of(rows_x, step, half, 0, D)[...]),
             w_in[...].reshape(w_in_rows, -1),
             preferred_element_type=jnp.float32,
         )
-        keep(pre_held, step, half, pre)
+
+    def forward(step, half):
+        pre = pre_of(step, half)
         hidden = (pre * jax.nn.sigmoid(pre)).astype(jnp.bfloat16)
         keep(hid_held, step, half, hidden)
         for columns in range(0, D, WIDE):
@@ -767,7 +685,7 @@
             CONTRACT_COLS,
             preferred_element_type=jnp.float32,
         )
-        dpre = (dhidden * swish_slope(flat(chunk_of(pre_held, step, half)[...]))).astype(jnp.bfloat16)
+        dpre = (dhidden * swish_slope(pre_of(step, half))).astype(jnp.bfloat16)
         keep(dpre_held, step, half, dpre)
         weights_all = w_in[...].reshape(w_in_rows, -1)
         for columns in range(0, D, WIDE):
@@ -902,21 +820,65 @@
             def _():
                 o_refs[a][target] = results[a, 0, half, core, j]
 
-    groups.wait(groups.greet())
-    spread.start()
-    for i in range(2):
-        weight_own_copy(i).start()
-        for step in range(1, shares):
-            weight_copy(i, step).start()
-    load_copy().start()
-    for m in range(ZEDS):
-        spread.step(m)
+    signals = groups.greet((after, before_me))
+    wide_ref[pl.ds(SIDE, length)] = frames_ref[...].astype(jnp.float32)
+    zeros = jnp.zeros((1, D), jnp.float32)
+    for row in range(2 * TAPS, lags_ref.shape[0] * lags_ref.shape[1]):
+        place_row(lags_ref, row, pl.ds(0, D), zeros)
+    groups.wait(signals)
+    for copy in rim_copies:
+        copy.start()
+    spread_u.start()
+    for hop in y_hops:
+        hop.start()
+    for copy in rim_copies:
+        copy.wait_recv()
+    for side, rows, edge in ((0, 0, tm == 0), (1, SIDE + length, tm == tm_size - 1)):
+        wide_ref[pl.ds(rows, SIDE)] = jnp.where(edge, 0.0, rims[side].astype(jnp.float32))
+    tiles = D // 128
+    for m in range(3):
+        spread_u.step(m)
+        lax.fori_loop(m * tiles // 3, (m + 1) * tiles // 3, conv_of, 0)
+    moment_near.start()
+    for m in range(3, 6):
+        spread_u.step(m)
+        lax.fori_loop((m - 3) * tiles // 3, (m - 2) * tiles // 3, lags_of, 0)
+    moment_near.finish()
+    far_moments[groups.far_rank] = moments_merge(near_moments[...], float(length))
+    moment_far.start()
+    for y_hop, z_hop in zip(y_hops, z_hops):
+        y_hop.finish()
+        z_hop.start()
+    for m in range(6, ZEDS):
+        spread_u.step(m)
+    moment_far.finish()
+    moments_ref[...] = moments_merge(far_moments[...], float(length * groups.near_size))
+    lax.fori_loop(0, length // SIDE, normalize, 0)
+    bucket()
+    spread_x.start()
+    for hop in z_hops:
+        hop.finish()
+    weights_start()
+    for m in range(ZEDS, ZEDS + LAG):
+        spread_u.step(m)
+    scale = lax.rsqrt(moments_ref[1:] / count + EPS)
+    shift = near_moments[rank, pl.ds(0, 1), :] - moments_ref[:1]
+    for lag in range(TAPS):
+        value = row_of(lags_ref, TAPS + lag) + shift * row_of(lags_ref, lag)
+        place_row(lags_ref, TAPS + lag, pl.ds(0, D), scale * value)
+    near_held[rank] = lags_ref[rank]
+    for m in range(4):
+        spread_x.step(m)
+    weights_relay()
+    for m in range(4, ZEDS):
+        spread_x.step(m)
     near.start()
     for m in range(ZEDS, ZEDS + LAG):
-        spread.step(m)
-    spread.arrive()
+        spread_x.step(m)
+    spread_u.arrive()
+    spread_u.finish()
+    spread_x.arrive()
     weights_arrive()
-    load_copy().wait()
     work(0, 0)
     near.finish()
     far_held[groups.far_rank] = jnp.sum(near_held[...], axis=0)
@@ -954,37 +916,42 @@
                         y_copy(a, step, half, part).wait_send()
         for k in range(1, ZEDS):
             z_copy(a, (z + k) % ZEDS).wait_send()
-    spread.finish()
+    spread_x.finish()
+    for copy in rim_copies:
+        copy.wait_send()
     for i in range(2):
         for step in range(1, shares):
             weight_copy(i, step).wait_send()
             part_copy(i, step).wait_send()
 
 
-def experts(x, rows_u, in_share, out_share, lags, collective_id):
+def main_step(frames, taps, gain, bias, router, choose, hot, w_in, w_out, u, collective_id):
     shares = lax.axis_size("dp")
-    hidden = in_share.shape[1]
-    slots = x.shape[1]
+    hidden, slots, length = w_in.shape[1], u.shape[1], frames.shape[0]
     lines = (CORES, LINES, ZEDS)
     chunk = (HALF, slots, D)
     bf16, f32, dma = jnp.bfloat16, jnp.float32, pltpu.SemaphoreType.DMA
-    out = jax.ShapeDtypeStruct((ZEDS, slots, D), bf16)
-    gradient = jax.ShapeDtypeStruct((hidden, D // shares), bf16)
+    shape = jax.ShapeDtypeStruct
+    gradient = (hidden, D // shares)
     held = lines + (slots, hidden)
     far_size = shares * (lax.axis_size("tm") // NEAR)
+    lags = (NEAR, -(-2 * TAPS // NEAR), D)
+    in_share, out_share = (w_in.shape[0] // shares, hidden), (w_out.shape[0] // shares, D)
+    trade_sems = [(NEAR,), (NEAR,), (far_size,), (far_size,)]
     sems = [
+        *trade_sems,
         (NEAR,),
         (NEAR,),
-        (far_size,),
-        (far_size,),
-        (NEAR,),
-        (NEAR,),
+        *trade_sems,
+        (2, 3),
+        (2, 3),
+        (2,),
+        (2,),
         (2,),
         (2, shares),
         (2, shares),
         (2, shares),
         (2, shares),
-        (1,),
         (2, LINES, 2),
         (2, LINES, 2),
         (2, LINES, 2, 2),
@@ -992,35 +959,52 @@
         (2, ZEDS),
         (2, ZEDS),
         *Spread.SEMS,
+        *Spread.SEMS,
+    ]
+    scratch = [
+        ((ZEDS, slots, D + EXTRA), bf16),
+        ((length, D), bf16),
+        (in_share, bf16),
+        (out_share, bf16),
+        (in_share, bf16),
+        (out_share, bf16),
+        ((2, SIDE, D), bf16),
+        (lags, f32),
+        (lines + (slots, D + EXTRA), bf16),
+        (lines + (slots, D), bf16),
+        ((shares,) + in_share, bf16),
+        ((shares,) + out_share, bf16),
+        (held, bf16),
+        (held, bf16),
+        ((2, LINES, 2, CORES) + chunk, bf16),
+        ((2, LINES, 2) + chunk, bf16),
+        ((2, LINES - 1, 2) + chunk, bf16),
+        ((hidden, D), f32),
+        ((2, shares) + gradient, bf16),
+        ((2, shares) + gradient, bf16),
+        (lags, f32),
+        ((far_size,) + lags[1:], f32),
+        ((NEAR, 2, D), f32),
+        ((far_size, 2, D), f32),
     ]
     vmem, anywhere = pl.BlockSpec(memory_space=pltpu.VMEM), pl.BlockSpec(memory_space=pl.ANY)
+    outs = (
+        [shape((ZEDS, slots, D), bf16)] * 2
+        + [shape(gradient, bf16)] * 2
+        + [shape(lags, f32), shape((2, D), f32), shape((length + 2 * SIDE, D), f32)]
+        + [shape((length, D), f32)] * 3
+        + [shape((length, EXTRA), f32)] * 2
+    )
     return pl.pallas_call(
-        functools.partial(experts_kernel, shares),
-        out_shape=(out, out, gradient, gradient, jax.ShapeDtypeStruct(lags.shape, lags.dtype)),
-        in_specs=[anywhere] * 4 + [vmem],
-        out_specs=[vmem] * 5,
-        scratch_shapes=[
-            pltpu.VMEM(lines + x.shape[1:], bf16),
-            pltpu.VMEM(lines + (slots, D), bf16),
-            pltpu.VMEM((shares,) + in_share.shape, bf16),
-            pltpu.VMEM((shares,) + out_share.shape, bf16),
-            pltpu.VMEM(held, f32),
-            pltpu.VMEM(held, bf16),
-            pltpu.VMEM(held, bf16),
-            pltpu.VMEM((2, LINES, 2, CORES) + chunk, bf16),
-            pltpu.VMEM((2, LINES, 2) + chunk, bf16),
-            pltpu.VMEM((2, LINES - 1, 2) + chunk, bf16),
-            pltpu.VMEM((hidden, D), f32),
-            pltpu.VMEM((2, shares) + gradient.shape, bf16),
-            pltpu.VMEM((2, shares) + gradient.shape, bf16),
-            pltpu.VMEM(lags.shape, lags.dtype),
-            pltpu.VMEM((far_size,) + lags.shape[1:], lags.dtype),
-        ]
-        + [dma(shape) for shape in sems],
+        functools.partial(main_kernel, shares),
+        out_shape=tuple(outs),
+        in_specs=[vmem] * 7 + [anywhere] * 3,
+        out_specs=[vmem] * len(outs),
+        scratch_shapes=[pltpu.VMEM(*entry) for entry in scratch] + [dma(entry) for entry in sems],
         compiler_params=pltpu.CompilerParams(
-            collective_id=collective_id, has_side_effects=True, vmem_limit_bytes=60 << 20
+            collective_id=collective_id, has_side_effects=True, vmem_limit_bytes=62 << 20
         ),
-    )(x, rows_u, in_share, out_share, lags)
+    )(frames, taps, gain, bias, router, choose, hot, w_in, w_out, u)
 
 
 def body(
@@ -1055,34 +1039,37 @@
         return lax.dot_general(place_any, rows, CONTRACT_ROWS, preferred_element_type=jnp.float32)
 
     up_buffer = bucketed(cotangent[0]).astype(jnp.bfloat16).reshape(EXPERTS, capacity, D)
-    moments, conv, wide, lags, w_in_share, w_out_share, rows_u = first_step(
-        frames[0], taps, w_in, w_out, up_buffer, 0
+    choose = onehot[:, 0] - onehot[:, 1]
+    (
+        combined,
+        back,
+        grad_in_local,
+        grad_out_local,
+        lags,
+        moments,
+        wide,
+        normalized_input,
+        resid,
+        vhat,
+        lrstd,
+        gate,
+    ) = main_step(
+        frames[0],
+        taps,
+        batchnorm_gain_scale[None],
+        batchnorm_shift_bias[None],
+        jnp.pad(w_router, ((0, 0), (0, EXTRA - EXPERTS))),
+        jnp.pad(choose, ((0, 0), (0, EXTRA - EXPERTS))),
+        jnp.stack([place_hot[:, k] for k in range(TOP)]).astype(jnp.bfloat16),
+        w_in,
+        w_out,
+        up_buffer,
+        0,
     )
-    signal = frames[0].astype(jnp.float32)
-    mean, variance = moments[0], moments[1] / element_count
-    centered_values = conv - mean
-    inverse_deviation = lax.rsqrt(variance + EPS)
-    normalized_input = centered_values * inverse_deviation
+    lrstd, first = lrstd[:, :1], gate[:, 0]
+    gates = jnp.stack([first, 1.0 - first], axis=1)
+    inverse_deviation = lax.rsqrt(moments[1] / element_count + EPS)
     before_activation = normalized_input * batchnorm_gain_scale + batchnorm_shift_bias
-    resid = signal + jax.nn.silu(before_activation)
-    lcent = resid - jnp.mean(resid, axis=-1, keepdims=True)
-    lrstd = lax.rsqrt(jnp.mean(lcent * lcent, axis=-1, keepdims=True) + EPS)
-    vhat = lcent * lrstd
-    normed = vhat.astype(jnp.bfloat16)
-    logits = jnp.dot(normed, w_router, preferred_element_type=jnp.float32)
-    picked = jnp.sum(onehot * logits[:, None, :], axis=-1)
-    first = jax.nn.sigmoid(picked[:, 0] - picked[:, 1])
-    gates = jnp.stack([first, 1.0 - first], axis=1)
-    gate_rows = jnp.sum(place_hot * gates[:, :, None], axis=(0, 1))
-
-    gate_high = lax.reduce_precision(gate_rows, 8, 7)
-    gate_parts = jnp.stack([gate_high, gate_rows - gate_high], axis=1).astype(jnp.bfloat16)
-    buffer = jnp.concatenate(
-        [bucketed(normed).astype(jnp.bfloat16), jnp.repeat(gate_parts, EXTRA // 2, axis=1)], axis=1
-    ).reshape(EXPERTS, capacity, D + EXTRA)
-    combined, back, grad_in_local, grad_out_local, lags = experts(
-        buffer, rows_u, w_in_share, w_out_share, lags, 1
-    )
     combined = combined.reshape(EXPERTS * capacity, D).astype(jnp.float32)
     back = back.reshape(EXPERTS * capacity, D).astype(jnp.float32)
     expert_out = [
@@ -1092,7 +1079,7 @@
     upstream = cotangent[0].astype(jnp.float32)
     dgate = [jnp.sum(upstream * expert_out[k], axis=-1) for k in range(TOP)]
     dpick = (dgate[0] - dgate[1]) * first * (1.0 - first)
-    dlogits = (onehot[:, 0] - onehot[:, 1]) * dpick[:, None]
+    dlogits = choose * dpick[:, None]
     dnormed = jnp.dot(dlogits, w_router.astype(jnp.float32).T, precision=EXACT)
     dnormed = dnormed + jnp.dot(jnp.sum(place_hot, axis=1), back, precision=EXACT)
     dmean = jnp.mean(dnormed, axis=-1, keepdims=True)

time: 252 us -> 250 us (level)
  Pallas kernels: 225 us -> 228 us
    pallas_call x1, Pallas kernels: 41.9 us -> 48.7 us  [last_step(): pl.pallas_call(functools.partial(last_kernel, count), out_shape=(sums, ja...]
    unnamed x39 -> x46, local copies, waits for them, and re-layouts: 8.75 us -> 4.73 us
    pallas_call x2 -> x1, Pallas kernels: 184 us -> 180 us  [main_step(): pl.pallas_call(functools.partial(main_kernel, shares), out_shape=tuple(ou...]
where the time goes in v6:
time: 250 us
  Pallas kernels  228 us (91%)
  local copies, waits for them, and re-layouts  9.95 us (4%)
  matrix products  5.17 us (2%)
  other arithmetic  5.09 us (2%)
    pallas_call x1, Pallas kernels, main_step(): pl.pallas_call(functools.partial(main_kernel, shares), out_shape=tuple(ou...  180 us
    pallas_call x1, Pallas kernels, last_step(): pl.pallas_call(functools.partial(last_kernel, count), out_shape=(sums, ja...  48.7 us

profile of v6, /device:TPU:1, one launch (start us, length us, event | category | flops | bytes accessed | tf_op | source)
XLA Modules:
  0.0 249.5 jit_solution(2740206770751632203)
XLA Ops:
  0.6 1.3 broadcast_in_dim.8.refs_2_
  1.9 1.3 broadcast_in_dim.9.refs_3_
  3.2 1.0 copy.25
  4.2 0.8 pad.8.refs_4_
  5.2 0.6 pad.9.refs_5_
  6.1 0.6 reduce-window.6
  6.7 0.2 slice_reduce_fusion.2
  7.6 0.7 pad_maximum_fusion.refs_6_
  8.2 1.3 convolution_convert_fusion
  9.5 179.6 %shard_map.128 = (bf16[8,32,1536]{2,1,0:T(8,128)(2,1)}, bf16[8,32,1536]{2,1,0:T(8,128)(2,1)}, bf16[384,384]{1,0:T(8,128)(2,1)}, bf16[384,384]{1,0:T(8,128)(2,1)}...) custom-call(bf16[128,1536]{1,0:T(8,128)(2,1)} %bitcast.51, ...), custom_call_target="tpu_custom_call" | custom-call | tf_op jit(solution)/shard_map/pallas_call | solution.py:998
  189.2 1.5 fusion.10
  190.7 1.2 fusion.1
  192.2 0.9 fusion.2
  193.2 0.5 fusion.12
  193.8 0.5 copy-done.6
  194.4 0.7 fusion.19
  195.1 0.4 copy-done
  195.6 0.5 multiply_multiply_fusion
  196.3 0.5 copy-done.1
  196.9 48.7 %shard_map.129 = (f32[16,4,1536]{2,1,0:T(4,128)S(1)}, bf16[128,1536]{1,0:T(8,128)(2,1)S(1)}, bf16[384,384]{1,0:T(8,128)(2,1)S(1)}, bf16[384,384]{1,0:T(8,128)(2,1)S(1)}) custom-call(f32[160,1536]{1,0:T(8,128)S(1)} %copy-done.1, f32[128,1536]{1,0:T(8,128)S(1)} %get-tuple-element.63.grad_ref, f32[128,1536]{1,0:T(8,128)S(1)} %copy-done, ...), custom_call_target="tpu_custom_call" | custom-call | tf_op jit(solution)/shard_map/pallas_call | solution.py:436
  246.1 0.7 fusion.6
  246.9 1.1 copy.30
  247.9 0.9 convert_element_type.46
  248.8 0.7 copy.33
  (65 shorter events, 2.2 us)
Async XLA Ops:
  0.6 4.4 %copy-start.17 = (s32[1,128,2]{1,2,0:T(2,128)S(1)}, s32[1,128,2]{1,2,0:T(2,128)}, u32[]{:S(2)}) copy-start(s32[1,128,2]{1,2,0:T(2,128)} %param.16) | copy-start | bytes 3076
  4.2 4.0 %copy-start.5 = (bf16[1,128,1536]{2,1,0:T(8,128)(2,1)S(1)}, bf16[1,128,1536]{2,1,0:T(8,128)(2,1)}, u32[]{:S(2)}) copy-start(bf16[1,128,1536]{2,1,0:T(8,128)(2,1)} %param.17) | copy-start | bytes 1179652
  7.4 2.2 copy-start.18
  7.5 181.6 %copy-start.11 = (pred[128,2,256]{2,0,1:T(32,128)(4,1)}, pred[128,2,256]{2,0,1:T(32,128)(4,1)S(1)}, u32[]{:S(2)}) copy-start(pred[128,2,256]{2,0,1:T(32,128)(4,1)S(1)} %get-tuple-element.67) | copy-start | bytes 196612
  189.1 1.5 copy-start.7
  190.7 1.4 copy-start.13
  190.7 1.4 copy-start.14
  190.7 1.5 copy-start.9
  192.2 1.0 copy-start.12
  192.2 1.5 copy-start.19
  192.2 1.6 copy-start.8
  193.2 1.2 copy-start.6
  194.4 1.1 copy-start
  194.4 1.1 copy-start.15
  194.4 1.1 copy-start.16
  195.5 0.7 copy-start.20
  195.5 1.2 copy-start.1
  195.5 1.2 copy-start.2
  195.5 1.3 copy-start.3
  195.5 1.4 copy-start.4
  196.9 48.7 %copy-start.10 = (f32[16,4,1536]{2,1,0:T(4,128)S(1)}, f32[16,4,1536]{2,1,0:T(4,128)}, u32[]{:S(2)}) copy-start(f32[16,4,1536]{2,1,0:T(4,128)} %get-tuple-element.34) | copy-start | bytes 1179652
